TPU v7x, 32 devices: a whole 2x2x4 slice. The times are simulated.
32 devices in a mesh: dp: 16 (over z, y, x), tensor: 2 (over core).
Axes of the slice: x: 2, y: 2, z: 4, core: 2. Of those that a mesh axis runs over, the one named last changes fastest.
Arguments:
- page_image: bfloat16 [3, 512, 128], P(None, ('dp', 'tensor')), may hold values from -12 to 12
- embeddings: bfloat16 [16384, 768], P('dp'), may hold values from -6 to 6
- cotangent: bfloat16 [16384, 768], P('dp'), may hold values from -6 to 6
- doc_ids: int32 [16, 1024], P('dp'), may hold values from 0 to 2, never falling along the last dimension, each value on 1 to 768 neighbouring positions
- pad_mask: int32 [16, 1024], P('dp'), may hold values 0 or 1
- token_boxes: int32 [4, 16, 1024], P(None, 'dp'), may hold values from 0 to 127, as said below
- conv_first: bfloat16 [3, 128], replicated, may hold values from -3.5 to 3.5
- conv_weights: bfloat16 [8, 128, 128], replicated, may hold values from -0.5 to 0.5
- group_gain: float32 [9, 128], replicated, may hold values from 0.25 to 1.75
- group_shift: float32 [9, 128], replicated, may hold values from -3 to 3
- roi_proj: bfloat16 [128, 768], replicated, may hold values from -0.5 to 0.5
- attn_norm: float32 [768], replicated, may hold values from 0.25 to 1.75
- query_proj: bfloat16 [768, 768], P(None, 'tensor'), may hold values from -0.21875 to 0.21875
- key_proj: bfloat16 [768, 768], P(None, 'tensor'), may hold values from -0.21875 to 0.21875
- value_proj: bfloat16 [768, 768], P(None, 'tensor'), may hold values from -0.21875 to 0.21875
- output_proj: bfloat16 [768, 768], P('tensor'), may hold values from -0.625 to 0.625
- bias_tables: float32 [3, 32, 12], P(None, None, 'tensor'), may hold values from -3 to 3
- ffn_norm: float32 [768], replicated, may hold values from 0.25 to 1.75
- up_proj: bfloat16 [768, 3072], P(None, 'tensor'), may hold values from -0.21875 to 0.21875
- down_proj: bfloat16 [3072, 768], P('tensor'), may hold values from -0.109375 to 0.109375
Outputs:
- layer_out: bfloat16 [16384, 768], P('dp')
- grad_embeddings: float32 [16384, 768], P('dp')
- grad_conv_first: float32 [3, 128], replicated
- grad_conv_weights: float32 [8, 128, 128], replicated
- grad_group_gain: float32 [9, 128], replicated
- grad_group_shift: float32 [9, 128], replicated
- grad_roi_proj: float32 [128, 768], P(None, 'dp')
- grad_attn_norm: float32 [768], P('dp')
- grad_query_proj: float32 [768, 768], P('dp', 'tensor')
- grad_key_proj: float32 [768, 768], P('dp', 'tensor')
- grad_value_proj: float32 [768, 768], P('dp', 'tensor')
- grad_output_proj: float32 [768, 768], P('tensor', 'dp')
- grad_bias_tables: float32 [3, 32, 12], P(None, None, 'tensor')
- grad_ffn_norm: float32 [768], P('dp')
- grad_up_proj: float32 [768, 3072], P('dp', 'tensor')
- grad_down_proj: float32 [3072, 768], P('tensor', 'dp')
Inputs may be any that keep to these rules, and one draw needn't show every extreme that they name: `doc_ids`: each row holds 3 documents in order; the longest has exactly 768 slots. `token_boxes`: x0 < x1 <= x0 + 8 and x1 <= 127; y0 < y1 <= y0 + 4 and y1 <= 31.
All inputs are finite; a program needn't handle non-finite values. No bound on the sum of `pad_mask` on one device may be relied on, other than what follows from the above.
Results may differ from a plain program's by a relative error of at most 0.013.
Values sent between devices are 32-bit elements; how exact they have to be, the bound alone decides.
A program may use at most 384 MiB of HBM per device.

v0:
```python
import jax
import jax.numpy as jnp
from jax import lax
from jax.sharding import PartitionSpec as P

HDIM = 64
NBUCKET = 32
GROUPS = 32
QBLK = 512


bucket_edges = (12, 16, 23, 32, 46, 64, 91)
norm_eps = 1e-06
group_eps = 1e-05
masked_score = -1e30
highest = lax.Precision.HIGHEST


def bucket_of(relative):
    magnitude = jnp.abs(relative)
    coarse = jnp.full(relative.shape, 8, jnp.int32)
    for edge in bucket_edges:
        coarse = coarse + (magnitude >= edge).astype(jnp.int32)
    return jnp.where(magnitude < 8, magnitude, coarse) + jnp.where(relative > 0, 16, 0).astype(
        jnp.int32
    )


def bucket_table(bucket_ids):
    return (bucket_ids[..., None] == jnp.arange(NBUCKET, dtype=jnp.int32)).astype(jnp.bfloat16)


def pool_down(values):
    return values.reshape(values.shape[0], values.shape[1] // 2, 2, values.shape[2] // 2, 2).mean(
        axis=(2, 4)
    )


def pool_down_back(grads):
    return jnp.repeat(jnp.repeat(grads, 2, axis=1), 2, axis=2) * 0.25


def pool_up(values):
    return jnp.repeat(jnp.repeat(values, 2, axis=1), 2, axis=2)


def pool_up_back(grads):
    return grads.reshape(grads.shape[0], grads.shape[1] // 2, 2, grads.shape[2] // 2, 2).sum(
        axis=(2, 4)
    )


def conv_apply(weights, layer_in):
    return jnp.einsum("co,crw->orw", weights.astype(jnp.float32), layer_in, precision=highest)


def conv_back(weights, layer_in, grad_conv):
    grad_weights = jnp.einsum("crw,orw->co", layer_in, grad_conv, precision=highest)
    grad_in = jnp.einsum("co,orw->crw", weights.astype(jnp.float32), grad_conv, precision=highest)
    return (grad_weights, grad_in)


def group_forward(pre_norm, gains, offsets, devices):
    grouped = pre_norm.reshape(GROUPS, -1)
    total_count = grouped.shape[1] * devices
    totals = lax.psum(jnp.sum(grouped, axis=1), ("dp", "tensor"))
    centre = totals / total_count
    centred = grouped - centre[:, None]
    spread = lax.psum(jnp.sum(centred * centred, axis=1), ("dp", "tensor"))
    variance = spread / total_count
    inv_std = lax.rsqrt(variance + group_eps)
    normed = ((grouped - centre[:, None]) * inv_std[:, None]).reshape(pre_norm.shape)
    lifted = normed * gains[:, None, None] + offsets[:, None, None]
    current = jax.nn.silu(lifted)
    return (current, lifted, normed, inv_std)


def group_backward(grads, lifted, normed, inv_std, gains, devices):
    sigma = jax.nn.sigmoid(lifted)
    active = grads * sigma * (1.0 + lifted * (1.0 - sigma))
    grad_gain = jnp.sum(active * normed, axis=(1, 2))
    grad_offset = jnp.sum(active, axis=(1, 2))
    scaled = (active * gains[:, None, None]).reshape(GROUPS, -1)
    flat_normed = normed.reshape(GROUPS, -1)
    total_count = flat_normed.shape[1] * devices
    first_sum, second_sum = lax.psum(
        (jnp.sum(scaled, axis=1), jnp.sum(scaled * flat_normed, axis=1)), ("dp", "tensor")
    )
    grad_pre = inv_std[:, None] * (
        scaled - first_sum[:, None] / total_count - flat_normed * second_sum[:, None] / total_count
    )
    return (grad_pre.reshape(lifted.shape), grad_gain, grad_offset)


def stem_forward(page_image, conv_first, conv_weights, group_gain, group_shift, devices):
    records = []
    layer_in = page_image.astype(jnp.float32)
    current, lifted, normed, inv_std = group_forward(
        conv_apply(conv_first, layer_in), group_gain[0], group_shift[0], devices
    )
    records.append((layer_in, lifted, normed, inv_std))
    downs = [current]
    for level in range(1, 5):
        layer_in = pool_down(current)
        current, lifted, normed, inv_std = group_forward(
            conv_apply(conv_weights[level - 1], layer_in),
            group_gain[level],
            group_shift[level],
            devices,
        )
        records.append((layer_in, lifted, normed, inv_std))
        downs.append(current)
    for level in range(3, -1, -1):
        layer_in = pool_up(current) + downs[level]
        current, lifted, normed, inv_std = group_forward(
            conv_apply(conv_weights[7 - level], layer_in),
            group_gain[8 - level],
            group_shift[8 - level],
            devices,
        )
        records.append((layer_in, lifted, normed, inv_std))
    return (current, records)


def stem_backward(grads, records, conv_weights, group_gain, devices):
    grad_convs = [None] * 8
    grad_gains = [None] * 9
    grad_offsets = [None] * 9
    skips = [None] * 4
    for level in range(4):
        layer = 8 - level
        layer_in, lifted, normed, inv_std = records[layer]
        grad_pre, grad_gains[layer], grad_offsets[layer] = group_backward(
            grads, lifted, normed, inv_std, group_gain[layer], devices
        )
        grad_convs[7 - level], grad_in = conv_back(conv_weights[7 - level], layer_in, grad_pre)
        skips[level] = grad_in
        grads = pool_up_back(grad_in)
    for level in range(4, 0, -1):
        layer_in, lifted, normed, inv_std = records[level]
        grad_pre, grad_gains[level], grad_offsets[level] = group_backward(
            grads, lifted, normed, inv_std, group_gain[level], devices
        )
        grad_convs[level - 1], grad_in = conv_back(conv_weights[level - 1], layer_in, grad_pre)
        grads = pool_down_back(grad_in) + skips[level - 1]
    layer_in, lifted, normed, inv_std = records[0]
    grad_pre, grad_gains[0], grad_offsets[0] = group_backward(
        grads, lifted, normed, inv_std, group_gain[0], devices
    )
    grad_first = jnp.einsum("crw,orw->co", layer_in, grad_pre, precision=highest)
    return (grad_first, jnp.stack(grad_convs), jnp.stack(grad_gains), jnp.stack(grad_offsets))


def rms_forward(values, gains):
    inverse = lax.rsqrt(jnp.mean(values * values, axis=-1, keepdims=True) + norm_eps)
    normal = values * inverse
    return ((normal * gains).astype(jnp.bfloat16), normal, inverse)


def rms_backward(grads, normal, inverse, gains):
    scaled = grads * gains
    grad_gain = jnp.sum(grads * normal, axis=0)
    back = inverse * (scaled - normal * jnp.mean(scaled * normal, axis=-1, keepdims=True))
    return (back, grad_gain)


def exact_gelu(values):
    return jax.nn.gelu(values, approximate=False)


def block_terms(start, segment, padding, left_edge, top_edge):
    positions = jnp.arange(segment.shape[0], dtype=jnp.int32)
    query_pos = positions[start : start + QBLK]
    relative = positions[None, :] - query_pos[:, None]
    rel_bucket = bucket_of(relative)
    left_bucket = bucket_of(left_edge[None, :] - left_edge[start : start + QBLK, None])
    top_bucket = bucket_of(top_edge[None, :] - top_edge[start : start + QBLK, None])
    allowed = (segment[None, :] == segment[start : start + QBLK, None]) & (
        (padding[None, :] > 0) | (relative == 0)
    )
    return ((rel_bucket, left_bucket, top_bucket), allowed)


def block_scores(query_block, key_heads, bias_tables, buckets, allowed):
    bias = jnp.einsum(
        "qkb,bh->hqk",
        bucket_table(buckets[0]),
        bias_tables[0],
        preferred_element_type=jnp.float32,
        precision=highest,
    )
    bias = bias + jnp.einsum(
        "qkb,bh->hqk",
        bucket_table(buckets[1]),
        bias_tables[1],
        preferred_element_type=jnp.float32,
        precision=highest,
    )
    bias = bias + jnp.einsum(
        "qkb,bh->hqk",
        bucket_table(buckets[2]),
        bias_tables[2],
        preferred_element_type=jnp.float32,
        precision=highest,
    )
    scores = (
        jnp.einsum("qhd,khd->hqk", query_block, key_heads, preferred_element_type=jnp.float32)
        * HDIM ** (-0.5)
        + bias
    )
    return jnp.where(allowed[None], scores, masked_score)


def bucket_sums(grad_upper, grad_lower, bucket_ids):
    table = bucket_table(bucket_ids)
    upper = jnp.einsum("hqk,qkb->bh", grad_upper, table, preferred_element_type=jnp.float32)
    return upper + jnp.einsum("hqk,qkb->bh", grad_lower, table, preferred_element_type=jnp.float32)


def on_device(
    page_image,
    embeddings,
    cotangent,
    doc_ids,
    pad_mask,
    token_boxes,
    conv_first,
    conv_weights,
    group_gain,
    group_shift,
    roi_proj,
    attn_norm,
    query_proj,
    key_proj,
    value_proj,
    output_proj,
    bias_tables,
    ffn_norm,
    up_proj,
    down_proj,
):
    devices = lax.axis_size("dp") * lax.axis_size("tensor")
    feature_map, records = stem_forward(
        page_image, conv_first, conv_weights, group_gain, group_shift, devices
    )
    tile_rows = page_image.shape[1]
    row_ids = lax.axis_index("tensor") * tile_rows + jnp.arange(tile_rows, dtype=jnp.int32)
    col_ids = jnp.arange(page_image.shape[2], dtype=jnp.int32)
    left_edge = token_boxes[0, 0]
    top_edge = token_boxes[1, 0]
    right_edge = token_boxes[2, 0]
    bottom_edge = token_boxes[3, 0]
    row_mask = (
        (row_ids[None, :] >= top_edge[:, None]) & (row_ids[None, :] < bottom_edge[:, None])
    ).astype(jnp.float32)
    col_mask = (
        (col_ids[None, :] >= left_edge[:, None]) & (col_ids[None, :] < right_edge[:, None])
    ).astype(jnp.float32)
    box_area = ((bottom_edge - top_edge) * (right_edge - left_edge)).astype(jnp.float32)
    column_sums = jnp.einsum("crw,tw->crt", feature_map, col_mask, precision=highest)
    partial_boxes = jnp.einsum("crt,tr->tc", column_sums, row_mask, precision=highest)
    box_sums = lax.psum(partial_boxes, "tensor")
    pooled = (box_sums / box_area[:, None]).astype(jnp.bfloat16)
    stream = embeddings.astype(jnp.float32) + jnp.dot(
        pooled, roi_proj, preferred_element_type=jnp.float32
    )
    attn_in, attn_hat, attn_inv = rms_forward(stream, attn_norm)
    tokens = stream.shape[0]
    local_heads = query_proj.shape[1] // HDIM
    query_heads = (
        jnp.dot(attn_in, query_proj, preferred_element_type=jnp.float32)
        .astype(jnp.bfloat16)
        .reshape(tokens, local_heads, HDIM)
    )
    key_heads = (
        jnp.dot(attn_in, key_proj, preferred_element_type=jnp.float32)
        .astype(jnp.bfloat16)
        .reshape(tokens, local_heads, HDIM)
    )
    value_heads = (
        jnp.dot(attn_in, value_proj, preferred_element_type=jnp.float32)
        .astype(jnp.bfloat16)
        .reshape(tokens, local_heads, HDIM)
    )
    segment = doc_ids[0]
    padding = pad_mask[0]
    scale = HDIM ** (-0.5)
    log_sums = []
    contexts = []
    for start in range(0, tokens, QBLK):
        buckets, allowed = block_terms(start, segment, padding, left_edge, top_edge)
        masked = block_scores(
            query_heads[start : start + QBLK], key_heads, bias_tables, buckets, allowed
        )
        top_score = jnp.max(masked, axis=-1, keepdims=True)
        weights = jnp.exp(masked - top_score)
        totals = jnp.sum(weights, axis=-1, keepdims=True)
        log_sums.append(top_score + jnp.log(totals))
        probs = (weights / totals).astype(jnp.bfloat16)
        contexts.append(
            jnp.einsum(
                "hqk,khd->qhd", probs, value_heads, preferred_element_type=jnp.float32
            ).astype(jnp.bfloat16)
        )
    context = jnp.concatenate(contexts, axis=0).reshape(tokens, -1)
    attn_out = lax.psum(jnp.dot(context, output_proj, preferred_element_type=jnp.float32), "tensor")
    middle = stream + attn_out
    ffn_in, ffn_hat, ffn_inv = rms_forward(middle, ffn_norm)
    pre_act = jnp.dot(ffn_in, up_proj, preferred_element_type=jnp.float32)
    activated, gelu_pullback = jax.vjp(exact_gelu, pre_act)
    hidden = activated.astype(jnp.bfloat16)
    ffn_out = lax.psum(jnp.dot(hidden, down_proj, preferred_element_type=jnp.float32), "tensor")
    layer_out = (middle + ffn_out).astype(jnp.bfloat16)
    grad_down = jnp.dot(hidden.T, cotangent, preferred_element_type=jnp.float32)
    grad_hidden = jnp.dot(cotangent, down_proj.T, preferred_element_type=jnp.float32)
    grad_pre = gelu_pullback(grad_hidden)[0].astype(jnp.bfloat16)
    grad_up = jnp.dot(ffn_in.T, grad_pre, preferred_element_type=jnp.float32)
    grad_ffn_in = lax.psum(
        jnp.dot(grad_pre, up_proj.T, preferred_element_type=jnp.float32), "tensor"
    )
    grad_mid_norm, grad_ffn_norm = rms_backward(grad_ffn_in, ffn_hat, ffn_inv, ffn_norm)
    grad_middle = cotangent.astype(jnp.float32) + grad_mid_norm
    grad_mid_low = grad_middle.astype(jnp.bfloat16)
    grad_output = jnp.dot(context.T, grad_mid_low, preferred_element_type=jnp.float32)
    grad_context = (
        jnp.dot(grad_mid_low, output_proj.T, preferred_element_type=jnp.float32)
        .astype(jnp.bfloat16)
        .reshape(tokens, local_heads, HDIM)
    )
    grad_value = jnp.zeros((tokens, local_heads, HDIM), jnp.float32)
    grad_key = jnp.zeros((tokens, local_heads, HDIM), jnp.float32)
    grad_tables = jnp.zeros((3, NBUCKET, local_heads), jnp.float32)
    grad_queries = []
    for index, start in enumerate(range(0, tokens, QBLK)):
        buckets, allowed = block_terms(start, segment, padding, left_edge, top_edge)
        masked = block_scores(
            query_heads[start : start + QBLK], key_heads, bias_tables, buckets, allowed
        )
        probs_full = jnp.exp(masked - log_sums[index])
        probs = probs_full.astype(jnp.bfloat16)
        grad_ctx_block = grad_context[start : start + QBLK]
        grad_value = grad_value + jnp.einsum(
            "hqk,qhd->khd", probs, grad_ctx_block, preferred_element_type=jnp.float32
        )
        grad_probs = jnp.einsum(
            "qhd,khd->hqk", grad_ctx_block, value_heads, preferred_element_type=jnp.float32
        )
        delta = jnp.sum(grad_probs * probs_full, axis=-1, keepdims=True)
        grad_full = probs_full * (grad_probs - delta)
        grad_scores = grad_full.astype(jnp.bfloat16)
        grad_lower = (grad_full - grad_scores.astype(jnp.float32)).astype(jnp.bfloat16)
        table_terms = jnp.stack(
            [bucket_sums(grad_scores, grad_lower, bucket_ids) for bucket_ids in buckets]
        )
        grad_tables = grad_tables + table_terms
        grad_queries.append(
            jnp.einsum("hqk,khd->qhd", grad_scores, key_heads, preferred_element_type=jnp.float32)
            * scale
        )
        grad_key = (
            grad_key
            + jnp.einsum(
                "hqk,qhd->khd",
                grad_scores,
                query_heads[start : start + QBLK],
                preferred_element_type=jnp.float32,
            )
            * scale
        )
    grad_query_low = jnp.concatenate(grad_queries, axis=0).reshape(tokens, -1).astype(jnp.bfloat16)
    grad_key_low = grad_key.reshape(tokens, -1).astype(jnp.bfloat16)
    grad_value_low = grad_value.reshape(tokens, -1).astype(jnp.bfloat16)
    grad_query_proj = jnp.dot(attn_in.T, grad_query_low, preferred_element_type=jnp.float32)
    grad_key_proj = jnp.dot(attn_in.T, grad_key_low, preferred_element_type=jnp.float32)
    grad_value_proj = jnp.dot(attn_in.T, grad_value_low, preferred_element_type=jnp.float32)
    attn_terms = jnp.dot(grad_query_low, query_proj.T, preferred_element_type=jnp.float32)
    attn_terms = attn_terms + jnp.dot(grad_key_low, key_proj.T, preferred_element_type=jnp.float32)
    attn_terms = attn_terms + jnp.dot(
        grad_value_low, value_proj.T, preferred_element_type=jnp.float32
    )
    grad_attn_in = lax.psum(attn_terms, "tensor")
    grad_stream_norm, grad_attn_norm = rms_backward(grad_attn_in, attn_hat, attn_inv, attn_norm)
    grad_stream = grad_middle + grad_stream_norm
    grad_low = grad_stream.astype(jnp.bfloat16)
    grad_roi = jnp.dot(pooled.T, grad_low, preferred_element_type=jnp.float32)
    grad_pooled = jnp.dot(grad_low, roi_proj.T, preferred_element_type=jnp.float32)
    grad_box = grad_pooled / box_area[:, None]
    spread_rows = grad_box.T[:, None, :] * row_mask.T[None, :, :]
    grad_map = jnp.einsum("crt,tw->crw", spread_rows, col_mask, precision=highest)
    grad_first, grad_convs, grad_gains, grad_offsets = stem_backward(
        grad_map, records, conv_weights, group_gain, devices
    )
    stem_totals = lax.psum((grad_first, grad_convs, grad_gains, grad_offsets), ("dp", "tensor"))
    table_totals = lax.psum(grad_tables, "dp")
    weight_parts = (
        lax.psum_scatter(grad_roi, "dp", scatter_dimension=1, tiled=True),
        lax.psum_scatter(grad_attn_norm, "dp", scatter_dimension=0, tiled=True),
        lax.psum_scatter(grad_query_proj, "dp", scatter_dimension=0, tiled=True),
        lax.psum_scatter(grad_key_proj, "dp", scatter_dimension=0, tiled=True),
        lax.psum_scatter(grad_value_proj, "dp", scatter_dimension=0, tiled=True),
        lax.psum_scatter(grad_output, "dp", scatter_dimension=1, tiled=True),
        lax.psum_scatter(grad_ffn_norm, "dp", scatter_dimension=0, tiled=True),
        lax.psum_scatter(grad_up, "dp", scatter_dimension=0, tiled=True),
        lax.psum_scatter(grad_down, "dp", scatter_dimension=1, tiled=True),
    )
    block_parts = weight_parts[:6]
    ffn_parts = weight_parts[6:]
    return (
        layer_out,
        grad_stream,
        stem_totals[0],
        stem_totals[1],
        stem_totals[2],
        stem_totals[3],
        block_parts[0],
        block_parts[1],
        block_parts[2],
        block_parts[3],
        block_parts[4],
        block_parts[5],
        table_totals,
        ffn_parts[0],
        ffn_parts[1],
        ffn_parts[2],
    )


def solution(mesh):
    placed = (
        P(None, ("dp", "tensor"), None),
        P("dp", None),
        P("dp", None),
        P("dp", None),
        P("dp", None),
        P(None, "dp", None),
        P(),
        P(),
        P(),
        P(),
        P(),
        P(),
        P(None, "tensor"),
        P(None, "tensor"),
        P(None, "tensor"),
        P("tensor", None),
        P(None, None, "tensor"),
        P(),
        P(None, "tensor"),
        P("tensor", None),
    )
    return jax.shard_map(
        on_device,
        mesh=mesh,
        in_specs=placed,
        out_specs=(
            P("dp", None),
            P("dp", None),
            P(),
            P(),
            P(),
            P(),
            P(None, "dp"),
            P("dp"),
            P("dp", "tensor"),
            P("dp", "tensor"),
            P("dp", "tensor"),
            P("tensor", "dp"),
            P(None, None, "tensor"),
            P("dp"),
            P("dp", "tensor"),
            P("tensor", "dp"),
        ),
        check_vma=False,
    )
```

profile of v0, /device:TPU:0, one launch (start us, length us, event | category | flops | bytes accessed | tf_op | source)
XLA Modules:
  0.0 2460.1 jit_solution(3722133997650275367)
XLA Ops:
  8.8 42.0 %psum.322 = f32[32]{0:T(128)S(1)} all-reduce(f32[32]{0:T(128)S(1)} %reduce_sum.738), channel_id=1, replica_groups=mesh['dp'=16,'tensor'=2] {'dp','tensor'}, use_global_device_ids=true, to_apply=%region_2.0 | all-reduce | flops 32 | bytes 256 | tf_op jit(solution)/shard_map/psum | solution.py:66
  51.6 40.2 %psum.323 = f32[32]{0:T(128)S(1)} all-reduce(f32[32]{0:T(128)S(1)} %reduce_sum.744), channel_id=1, replica_groups=mesh['dp'=16,'tensor'=2] {'dp','tensor'}, use_global_device_ids=true, to_apply=%region_5.6 | all-reduce | flops 32 | bytes 256 | tf_op jit(solution)/shard_map/psum | solution.py:69
  101.3 40.0 %psum.324 = f32[32]{0:T(128)S(1)} all-reduce(f32[32]{0:T(128)S(1)} %reduce_sum.751), channel_id=1, replica_groups=mesh['dp'=16,'tensor'=2] {'dp','tensor'}, use_global_device_ids=true, to_apply=%region_9.10 | all-reduce | flops 32 | bytes 256 | tf_op jit(solution)/shard_map/psum | solution.py:66
  142.7 40.1 %psum.325 = f32[32]{0:T(128)S(1)} all-reduce(f32[32]{0:T(128)S(1)} %reduce_sum.754), channel_id=1, replica_groups=mesh['dp'=16,'tensor'=2] {'dp','tensor'}, use_global_device_ids=true, to_apply=%region_12.13 | all-reduce | flops 32 | bytes 256 | tf_op jit(solution)/shard_map/psum | solution.py:69
  188.8 40.1 %psum.326 = f32[32]{0:T(128)S(1)} all-reduce(f32[32]{0:T(128)} %reduce_sum.761), channel_id=1, replica_groups=mesh['dp'=16,'tensor'=2] {'dp','tensor'}, use_global_device_ids=true, to_apply=%region_16.17 | all-reduce | flops 32 | bytes 256 | tf_op jit(solution)/shard_map/psum | solution.py:66
  232.3 40.3 %psum.327 = f32[32]{0:T(128)S(1)} all-reduce(f32[32]{0:T(128)} %reduce_sum.767), channel_id=1, replica_groups=mesh['dp'=16,'tensor'=2] {'dp','tensor'}, use_global_device_ids=true, to_apply=%region_19.20 | all-reduce | flops 32 | bytes 256 | tf_op jit(solution)/shard_map/psum | solution.py:69
  280.3 40.1 %psum.328 = f32[32]{0:T(128)} all-reduce(f32[32]{0:T(128)} %reduce_sum.774), channel_id=1, replica_groups=mesh['dp'=16,'tensor'=2] {'dp','tensor'}, use_global_device_ids=true, to_apply=%region_23.24 | all-reduce | flops 32 | bytes 256 | tf_op jit(solution)/shard_map/psum | solution.py:66
  327.0 40.5 %psum.329 = f32[32]{0:T(128)} all-reduce(f32[32]{0:T(128)} %reduce_sum.780), channel_id=1, replica_groups=mesh['dp'=16,'tensor'=2] {'dp','tensor'}, use_global_device_ids=true, to_apply=%region_26.27 | all-reduce | flops 32 | bytes 256 | tf_op jit(solution)/shard_map/psum | solution.py:69
  377.6 40.2 %psum.330 = f32[32]{0:T(128)} all-reduce(f32[32]{0:T(128)} %reduce_sum.789), channel_id=1, replica_groups=mesh['dp'=16,'tensor'=2] {'dp','tensor'}, use_global_device_ids=true, to_apply=%region_31.32 | all-reduce | flops 32 | bytes 256 | tf_op jit(solution)/shard_map/psum | solution.py:66
  424.4 41.1 %psum.331 = f32[32]{0:T(128)} all-reduce(f32[32]{0:T(128)} %reduce_sum.795), channel_id=1, replica_groups=mesh['dp'=16,'tensor'=2] {'dp','tensor'}, use_global_device_ids=true, to_apply=%region_34.35 | all-reduce | flops 32 | bytes 256 | tf_op jit(solution)/shard_map/psum | solution.py:69
  474.3 40.1 %psum.332 = f32[32]{0:T(128)} all-reduce(f32[32]{0:T(128)} %reduce_sum.801), channel_id=1, replica_groups=mesh['dp'=16,'tensor'=2] {'dp','tensor'}, use_global_device_ids=true, to_apply=%region_37.38 | all-reduce | flops 32 | bytes 256 | tf_op jit(solution)/shard_map/psum | solution.py:66
  521.0 40.7 %psum.333 = f32[32]{0:T(128)} all-reduce(f32[32]{0:T(128)} %reduce_sum.807), channel_id=1, replica_groups=mesh['dp'=16,'tensor'=2] {'dp','tensor'}, use_global_device_ids=true, to_apply=%region_40.41 | all-reduce | flops 32 | bytes 256 | tf_op jit(solution)/shard_map/psum | solution.py:69
  570.7 40.0 %psum.334 = f32[32]{0:T(128)} all-reduce(f32[32]{0:T(128)} %reduce_sum.958), channel_id=1, replica_groups=mesh['dp'=16,'tensor'=2] {'dp','tensor'}, use_global_device_ids=true, to_apply=%region_43.44 | all-reduce | flops 32 | bytes 256 | tf_op jit(solution)/shard_map/psum | solution.py:66
  617.3 40.8 %psum.335 = f32[32]{0:T(128)} all-reduce(f32[32]{0:T(128)} %reduce_sum.961), channel_id=1, replica_groups=mesh['dp'=16,'tensor'=2] {'dp','tensor'}, use_global_device_ids=true, to_apply=%region_46.47 | all-reduce | flops 32 | bytes 256 | tf_op jit(solution)/shard_map/psum | solution.py:69
  668.3 39.9 %psum.336 = f32[32]{0:T(128)} all-reduce(f32[32]{0:T(128)} %reduce_sum.964), channel_id=1, replica_groups=mesh['dp'=16,'tensor'=2] {'dp','tensor'}, use_global_device_ids=true, to_apply=%region_49.50 | all-reduce | flops 32 | bytes 256 | tf_op jit(solution)/shard_map/psum | solution.py:66
  715.2 40.9 %psum.337 = f32[32]{0:T(128)} all-reduce(f32[32]{0:T(128)} %reduce_sum.967), channel_id=1, replica_groups=mesh['dp'=16,'tensor'=2] {'dp','tensor'}, use_global_device_ids=true, to_apply=%region_52.53 | all-reduce | flops 32 | bytes 256 | tf_op jit(solution)/shard_map/psum | solution.py:69
  764.0 39.7 %psum.338 = f32[32]{0:T(128)S(1)} all-reduce(f32[32]{0:T(128)S(1)} %reduce_sum.970), channel_id=1, replica_groups=mesh['dp'=16,'tensor'=2] {'dp','tensor'}, use_global_device_ids=true, to_apply=%region_55.56 | all-reduce | flops 32 | bytes 256 | tf_op jit(solution)/shard_map/psum | solution.py:66
  804.4 40.6 %psum.339 = f32[32]{0:T(128)S(1)} all-reduce(f32[32]{0:T(128)S(1)} %reduce_sum.973), channel_id=1, replica_groups=mesh['dp'=16,'tensor'=2] {'dp','tensor'}, use_global_device_ids=true, to_apply=%region_58.59 | all-reduce | flops 32 | bytes 256 | tf_op jit(solution)/shard_map/psum | solution.py:69
  1527.5 40.8 %all-reduce.11 = (f32[32]{0:T(128)S(1)}, f32[32]{0:T(128)S(1)}) all-reduce(f32[32]{0:T(128)S(1)} %reduce_sum.987, f32[32]{0:T(128)S(1)} %reduce_sum.984), channel_id=1, replica_groups=mesh['dp'=16,'tensor'=2] {'dp','tensor'}, use_global_device_ids=true, to_apply=%region_79.80 | all-reduce | flops 64 | bytes 512 | tf_op jit(solution)/shard_map/psum | solution.py:86
  1584.5 40.1 %all-reduce.10 = (f32[32]{0:T(128)S(1)}, f32[32]{0:T(128)S(1)}) all-reduce(f32[32]{0:T(128)S(1)} %reduce_sum.994, f32[32]{0:T(128)S(1)} %reduce_sum.991), channel_id=1, replica_groups=mesh['dp'=16,'tensor'=2] {'dp','tensor'}, use_global_device_ids=true, to_apply=%region_86.87 | all-reduce | flops 64 | bytes 512 | tf_op jit(solution)/shard_map/psum | solution.py:86
  1639.6 40.2 %all-reduce.9 = (f32[32]{0:T(128)S(1)}, f32[32]{0:T(128)S(1)}) all-reduce(f32[32]{0:T(128)S(1)} %reduce_sum.1001, f32[32]{0:T(128)S(1)} %reduce_sum.998), channel_id=1, replica_groups=mesh['dp'=16,'tensor'=2] {'dp','tensor'}, use_global_device_ids=true, to_apply=%region_93.94 | all-reduce | flops 64 | bytes 512 | tf_op jit(solution)/shard_map/psum | solution.py:86
  1694.0 40.4 %all-reduce.8 = (f32[32]{0:T(128)S(1)}, f32[32]{0:T(128)S(1)}) all-reduce(f32[32]{0:T(128)S(1)} %reduce_sum.1008, f32[32]{0:T(128)S(1)} %reduce_sum.1005), channel_id=1, replica_groups=mesh['dp'=16,'tensor'=2] {'dp','tensor'}, use_global_device_ids=true, to_apply=%region_100.101 | all-reduce | flops 64 | bytes 512 | tf_op jit(solution)/shard_map/psum | solution.py:86
  1749.1 40.2 %all-reduce.7 = (f32[32]{0:T(128)S(1)}, f32[32]{0:T(128)S(1)}) all-reduce(f32[32]{0:T(128)S(1)} %reduce_sum.1017, f32[32]{0:T(128)S(1)} %reduce_sum.1014), channel_id=1, replica_groups=mesh['dp'=16,'tensor'=2] {'dp','tensor'}, use_global_device_ids=true, to_apply=%region_108.109 | all-reduce | flops 64 | bytes 512 | tf_op jit(solution)/shard_map/psum | solution.py:86
  1804.0 40.1 %all-reduce.6 = (f32[32]{0:T(128)S(1)}, f32[32]{0:T(128)S(1)}) all-reduce(f32[32]{0:T(128)S(1)} %reduce_sum.1023, f32[32]{0:T(128)S(1)} %reduce_sum.1020), channel_id=1, replica_groups=mesh['dp'=16,'tensor'=2] {'dp','tensor'}, use_global_device_ids=true, to_apply=%region_114.115 | all-reduce | flops 64 | bytes 512 | tf_op jit(solution)/shard_map/psum | solution.py:86
  1859.1 40.9 %all-reduce.5 = (f32[32]{0:T(128)S(1)}, f32[32]{0:T(128)S(1)}) all-reduce(f32[32]{0:T(128)S(1)} %reduce_sum.1029, f32[32]{0:T(128)S(1)} %reduce_sum.1026), channel_id=1, replica_groups=mesh['dp'=16,'tensor'=2] {'dp','tensor'}, use_global_device_ids=true, to_apply=%region_120.121 | all-reduce | flops 64 | bytes 512 | tf_op jit(solution)/shard_map/psum | solution.py:86
  1903.4 40.6 %all-reduce.4 = (f32[32]{0:T(128)}, f32[32]{0:T(128)}) all-reduce(f32[32]{0:T(128)S(1)} %reduce_sum.1035, f32[32]{0:T(128)S(1)} %reduce_sum.1032), channel_id=1, replica_groups=mesh['dp'=16,'tensor'=2] {'dp','tensor'}, use_global_device_ids=true, to_apply=%region_126.127 | all-reduce | flops 64 | bytes 512 | tf_op jit(solution)/shard_map/psum | solution.py:86
  1947.6 76.2 %all-reduce.12 = (f32[768]{0:T(1024)}, f32[3,32,6]{1,2,0:T(8,128)}, f32[768]{0:T(1024)}) all-reduce(f32[768]{0:T(1024)} %get-tuple-element.82, f32[3,32,6]{1,2,0:T(8,128)} %maximum_add_fusion, f32[768]{0:T(1024)} %get-tuple-element.80), channel_id=3, replica_groups=mesh['dp'=16,'tensor'=2] {'dp'}, use_global_device_ids=true, to_apply=%region_157.158.clone | all-reduce | flops 2112 | bytes 16896
  2061.3 37.7 %all-reduce.3 = (f32[32]{0:T(128)S(1)}, f32[32]{0:T(128)S(1)}) all-reduce(f32[32]{0:T(128)S(1)} %copy-done.186, f32[32]{0:T(128)S(1)} %copy-done.185), channel_id=1, replica_groups=mesh['dp'=16,'tensor'=2] {'dp','tensor'}, use_global_device_ids=true, to_apply=%region_132.133 | all-reduce | flops 64 | bytes 512 | tf_op jit(solution)/shard_map/psum | solution.py:86
  2109.2 41.1 %all-reduce.2 = (f32[3,128]{1,0:T(4,128)}, f32[9,128]{1,0:T(8,128)}, f32[9,128]{1,0:T(8,128)}) all-reduce(f32[3,128]{1,0:T(4,128)S(1)} %convolution_bitcast_fusion.9, f32[9,128]{1,0:T(8,128)S(1)} %stack.129, f32[9,128]{1,0:T(8,128)S(1)} %stack.139), channel_id=1, replica_groups=mesh['dp'=16,'tensor'=2] {'dp','tensor'}, use_global_device_ids=true, to_apply=%region_133.134 | all-reduce | flops 2688 | bytes 21504 | tf_op jit(solution)/shard_map/psum | solution.py:393
  2150.3 42.1 %reduce-scatter.20.cloned.1.call-done = f32[1536,48]{0,1:T(8,128)} async-done(((f32[1536,768]{0,1:T(8,128)}), f32[1536,48]{0,1:T(8,128)}) %reduce-scatter.20.cloned.1.call-update) | async-done | bytes 294928 | tf_op jit(solution)/shard_map/reduce_scatter | solution.py:404
  2192.4 132.7 %all-reduce.26.cloned.1.call-done = f32[8,128,128]{2,1,0:T(8,128)} async-done(((f32[8,128,128]{2,1,0:T(8,128)}), f32[8,128,128]{2,1,0:T(8,128)}) %all-reduce.26.cloned.1.call-update) | async-done | bytes 524304 | tf_op jit(solution)/shard_map/psum | solution.py:393
  2325.1 126.2 %reduce-scatter.8.cloned.1.call-done = f32[128,48]{0,1:T(8,128)} async-done(((f32[128,768]{0,1:T(8,128)}), f32[128,48]{0,1:T(8,128)}) %reduce-scatter.8.cloned.1.call-update) | async-done | bytes 24592 | tf_op jit(solution)/shard_map/reduce_scatter | solution.py:396
  (799 shorter events, 935.5 us)
Async XLA Ops:
  7.2 1235.8 %copy-start = (bf16[1536,768]{1,0:T(8,128)(2,1)S(1)}, bf16[1536,768]{1,0:T(8,128)(2,1)}, u32[]{:S(2)}) copy-start(bf16[1536,768]{1,0:T(8,128)(2,1)} %param.39) | copy-start | bytes 7077892
  7.2 1128.3 %all-reduce.20.cloned.1.call-start = ((), (), s32[]{:S(2)}) async-start(), calls=%async_computation.7 | async-start | bytes 1048576 | tf_op jit(solution)/shard_map/psum | solution.py:262
  8.6 751.7 %copy-start.14 = (f32[128,2048]{0,1}, f32[128,2048]{0,1:S(1)}, u32[]{:S(2)}) copy-start(f32[128,2048]{0,1:S(1)} %get-tuple-element.201) | copy-start | bytes 3145732
  51.0 131.8 %copy-start.121 = (f32[128]{0:T(128)}, f32[128]{0:T(128)S(1)}, u32[]{:S(2)}) copy-start(f32[128]{0:T(128)S(1)} %sub.644) | copy-start | bytes 1540
  93.5 91.2 %copy-start.107 = (f32[128]{0:T(128)}, f32[128]{0:T(128)S(1)}, u32[]{:S(2)}) copy-start(f32[128]{0:T(128)S(1)} %get-tuple-element.180) | copy-start | bytes 1540
  95.1 89.6 %copy-start.130 = (f32[128]{0:T(128)}, f32[128]{0:T(128)S(1)}, u32[]{:S(2)}) copy-start(f32[128]{0:T(128)S(1)} %get-tuple-element.189) | copy-start | bytes 1540
  185.9 379.3 %copy-start.59 = (f32[128,4,32]{0,2,1:T(8,128)}, f32[128,4,32]{0,2,1:T(8,128)S(1)}, u32[]{:S(2)}) copy-start(f32[128,4,32]{0,2,1:T(8,128)S(1)} %reduce_sum.758) | copy-start | bytes 196612
  187.4 572.9 %copy-start.35 = (f32[4,32,128]{2,1,0:T(8,128)}, f32[4,32,128]{2,1,0:T(8,128)S(1)}, u32[]{:S(2)}) copy-start(f32[4,32,128]{2,1,0:T(8,128)S(1)} %get-tuple-element.205) | copy-start | bytes 196612
  277.6 482.7 %copy-start.62 = (f32[2,16,128]{2,1,0:T(8,128)}, f32[2,16,128]{2,1,0:T(8,128)S(1)}, u32[]{:S(2)}) copy-start(f32[2,16,128]{2,1,0:T(8,128)S(1)} %get-tuple-element.207) | copy-start | bytes 49156
  568.0 193.4 %copy-start.45 = (f32[4,32,128]{2,1,0:T(8,128)}, f32[4,32,128]{2,1,0:T(8,128)S(1)}, u32[]{:S(2)}) copy-start(f32[4,32,128]{2,1,0:T(8,128)S(1)} %get-tuple-element.213) | copy-start | bytes 196612
  760.3 84.9 %copy-start.125 = (f32[128]{0:T(128)S(1)}, f32[128]{0:T(128)}, u32[]{:S(2)}) copy-start(f32[128]{0:T(128)} %get-tuple-element.174) | copy-start | bytes 1540
  760.3 84.9 %copy-start.163 = (f32[128]{0:T(128)S(1)}, f32[128]{0:T(128)}, u32[]{:S(2)}) copy-start(f32[128]{0:T(128)} %get-tuple-element.183) | copy-start | bytes 1540
  763.8 92.7 %copy-start.12 = (f32[16,128,128]{2,1,0:T(8,128)}, f32[16,128,128]{2,1,0:T(8,128)S(1)}, u32[]{:S(2)}) copy-start(f32[16,128,128]{2,1,0:T(8,128)S(1)} %get-tuple-element.217) | copy-start | bytes 3145732
  763.8 85.4 %copy-start.87 = (s32[4,1,1024]{2,1,0:T(1,128)S(1)}, s32[4,1,1024]{2,1,0:T(1,128)}, u32[]{:S(2)}) copy-start(s32[4,1,1024]{2,1,0:T(1,128)} %param.25) | copy-start | bytes 49156
  858.6 377.3 %all-reduce.22.cloned.1.call-start = ((), (), s32[]{:S(2)}) async-start(), calls=%async_computation.8 | async-start | bytes 6291456 | tf_op jit(solution)/shard_map/psum | solution.py:306
  858.8 276.7 %copy-start.80 = (f32[1024]{0:T(1024)}, f32[1024]{0:T(1024)S(1)}, u32[]{:S(2)}) copy-start(f32[1024]{0:T(1024)S(1)} %multiply_convert_fusion.4) | copy-start | bytes 12292
  1212.0 79.6 %all-reduce.24.cloned.1.call-start = ((), (), s32[]{:S(2)}) async-start(), calls=%async_computation.9 | async-start | bytes 6291456 | tf_op jit(solution)/shard_map/psum | solution.py:318
  1267.1 230.8 %all-reduce.28.cloned.1.call-start = ((), (), s32[]{:S(2)}) async-start(), calls=%async_computation.18 | async-start | bytes 12582912 | tf_op jit(solution)/shard_map/psum | solution.py:312
  1359.6 790.7 %reduce-scatter.16.cloned.1.call-start = ((), (), s32[]{:S(2)}) async-start(), calls=%async_computation.15 | async-start | bytes 1253376 | tf_op jit(solution)/shard_map/reduce_scatter | solution.py:401
  1364.6 785.7 %reduce-scatter.14.cloned.1.call-start = ((), (), s32[]{:S(2)}) async-start(), calls=%async_computation.14 | async-start | bytes 1253376 | tf_op jit(solution)/shard_map/reduce_scatter | solution.py:400
  1368.1 782.1 %reduce-scatter.12.cloned.1.call-start = ((), (), s32[]{:S(2)}) async-start(), calls=%async_computation.13 | async-start | bytes 1253376 | tf_op jit(solution)/shard_map/reduce_scatter | solution.py:399
  1371.9 778.4 %reduce-scatter.10.cloned.1.call-start = ((), (), s32[]{:S(2)}) async-start(), calls=%async_computation.12 | async-start | bytes 1253376 | tf_op jit(solution)/shard_map/reduce_scatter | solution.py:398
  1374.4 775.9 %reduce-scatter.18.cloned.1.call-start = ((), (), s32[]{:S(2)}) async-start(), calls=%async_computation.16 | async-start | bytes 5013504 | tf_op jit(solution)/shard_map/reduce_scatter | solution.py:403
  1382.2 810.2 %reduce-scatter.20.cloned.1.call-start = ((), (), s32[]{:S(2)}) async-start(), calls=%async_computation.17 | async-start | bytes 5013504 | tf_op jit(solution)/shard_map/reduce_scatter | solution.py:404
  1390.9 934.1 %all-reduce.26.cloned.1.call-start = ((), (), s32[]{:S(2)}) async-start(), calls=%async_computation.10 | async-start | bytes 1048576 | tf_op jit(solution)/shard_map/psum | solution.py:393
  1845.7 54.7 %copy-start.61 = (f32[128,4,32]{0,2,1:T(8,128)}, f32[128,4,32]{0,2,1:T(8,128)S(1)}, u32[]{:S(2)}) copy-start(f32[128,4,32]{0,2,1:T(8,128)S(1)} %get-tuple-element.152) | copy-start | bytes 196612
  1846.2 56.5 %copy-start.157 = (f32[1,32,6]{1,2,0:T(8,128)S(1)}, f32[1,32,6]{1,2,0:T(8,128)}, u32[]{:S(2)}) copy-start(f32[1,32,6]{1,2,0:T(8,128)} %fusion.166) | copy-start | bytes 2308
  1846.2 56.5 %copy-start.158 = (f32[1,32,6]{1,2,0:T(8,128)S(1)}, f32[1,32,6]{1,2,0:T(8,128)}, u32[]{:S(2)}) copy-start(f32[1,32,6]{1,2,0:T(8,128)} %fusion.164) | copy-start | bytes 2308
  1846.3 56.5 %copy-start.159 = (f32[1,32,6]{1,2,0:T(8,128)S(1)}, f32[1,32,6]{1,2,0:T(8,128)}, u32[]{:S(2)}) copy-start(f32[1,32,6]{1,2,0:T(8,128)} %fusion.162) | copy-start | bytes 2308
  1947.6 85.8 %copy-start.15 = (f32[128,2048]{0,1:S(1)}, f32[128,2048]{0,1}, u32[]{:S(2)}) copy-start(f32[128,2048]{0,1} %copy-done.14) | copy-start | bytes 3145732
  2057.8 393.4 %reduce-scatter.8.cloned.1.call-start = ((), (), s32[]{:S(2)}) async-start(), calls=%async_computation.11 | async-start | bytes 417792 | tf_op jit(solution)/shard_map/reduce_scatter | solution.py:396
  2099.4 353.7 %copy-start.1 = (bf16[1536,768]{1,0:T(8,128)(2,1)S(1)}, bf16[1536,768]{1,0:T(8,128)(2,1)}, u32[]{:S(2)}) copy-start(bf16[1536,768]{1,0:T(8,128)(2,1)} %param.39) | copy-start | bytes 7077892
  (176 other events, 3251.4 us)
Sparse Core Ops, SparseCore 0:
  858.7 19.4 all-reduce.19
  1212.1 23.7 all-reduce.21
  1267.2 24.3 all-reduce.23
  1359.7 33.3 all-reduce.27
  1398.2 124.9 reduce-scatter.15
  1528.4 122.6 reduce-scatter.13
  1656.5 122.6 reduce-scatter.11
  1784.5 122.7 reduce-scatter.9
  1913.0 136.4 reduce-scatter.17
  2056.0 136.3 reduce-scatter.19
  2198.2 126.7 all-reduce.25
  2330.8 120.3 reduce-scatter.7
where the time goes:
time: 2480 us; the launch traced here: 2460 us
  blocking collectives  1210 us (49%)
  matrix products  489 us (20%)
  waiting for transfers between devices  334 us (13%)
  local copies, waits for them, and re-layouts  258 us (10%)
  other arithmetic  154 us (6%)
    psum x9, blocking collectives, group_forward(): spread = lax.psum(jnp.sum(centred * centred, axis=1), ('dp', 'tensor'))  365 us
    psum x9, blocking collectives, group_forward(): totals = lax.psum(jnp.sum(grouped, axis=1), ('dp', 'tensor'))  362 us
    psum x9, blocking collectives, group_backward(): lax.psum((jnp.sum(scaled, axis=1), jnp.sum(scaled * flat_normed, axis=1))...  361 us
    psum x1, waiting for transfers between devices, on_device(): lax.psum((grad_first, grad_convs, grad_gains, grad_offsets), ('dp', 'tens...  133 us
    reduce_scatter x1, waiting for transfers between devices, on_device(): lax.psum_scatter(grad_roi, 'dp', scatter_dimension=1, tiled=True)  126 us
    unnamed x1, blocking collectives  76.2 us
    dot_general x6, matrix products, bucket_sums(): jnp.einsum('hqk,qkb->bh', grad_lower, table, preferred_element_type=jnp.f...  75.5 us
    dot_general x6, matrix products, bucket_sums(): jnp.einsum('hqk,qkb->bh', grad_upper, table, preferred_element_type=jnp.f...  71.4 us
  transfers between devices with their start and end apart: 12, of which 5 were waited for; matrix products, arithmetic and copies ran while one was open for 24% of the time, Pallas kernels for 0%

commit v1 on v0

--- a/solution.py
+++ b/solution.py
@@ -1,6 +1,10 @@
+import functools
+
 import jax
 import jax.numpy as jnp
 from jax import lax
+from jax.experimental import pallas as pl
+from jax.experimental.pallas import tpu as pltpu
 from jax.sharding import PartitionSpec as P
 
 HDIM = 64
@@ -30,125 +34,546 @@
     return (bucket_ids[..., None] == jnp.arange(NBUCKET, dtype=jnp.int32)).astype(jnp.bfloat16)
 
 
-def pool_down(values):
-    return values.reshape(values.shape[0], values.shape[1] // 2, 2, values.shape[2] // 2, 2).mean(
-        axis=(2, 4)
-    )
-
-
-def pool_down_back(grads):
-    return jnp.repeat(jnp.repeat(grads, 2, axis=1), 2, axis=2) * 0.25
-
-
-def pool_up(values):
-    return jnp.repeat(jnp.repeat(values, 2, axis=1), 2, axis=2)
-
-
-def pool_up_back(grads):
-    return grads.reshape(grads.shape[0], grads.shape[1] // 2, 2, grads.shape[2] // 2, 2).sum(
-        axis=(2, 4)
-    )
-
-
-def conv_apply(weights, layer_in):
-    return jnp.einsum("co,crw->orw", weights.astype(jnp.float32), layer_in, precision=highest)
-
-
-def conv_back(weights, layer_in, grad_conv):
-    grad_weights = jnp.einsum("crw,orw->co", layer_in, grad_conv, precision=highest)
-    grad_in = jnp.einsum("co,orw->crw", weights.astype(jnp.float32), grad_conv, precision=highest)
-    return (grad_weights, grad_in)
-
-
-def group_forward(pre_norm, gains, offsets, devices):
-    grouped = pre_norm.reshape(GROUPS, -1)
-    total_count = grouped.shape[1] * devices
-    totals = lax.psum(jnp.sum(grouped, axis=1), ("dp", "tensor"))
-    centre = totals / total_count
-    centred = grouped - centre[:, None]
-    spread = lax.psum(jnp.sum(centred * centred, axis=1), ("dp", "tensor"))
-    variance = spread / total_count
-    inv_std = lax.rsqrt(variance + group_eps)
-    normed = ((grouped - centre[:, None]) * inv_std[:, None]).reshape(pre_norm.shape)
-    lifted = normed * gains[:, None, None] + offsets[:, None, None]
-    current = jax.nn.silu(lifted)
-    return (current, lifted, normed, inv_std)
-
-
-def group_backward(grads, lifted, normed, inv_std, gains, devices):
-    sigma = jax.nn.sigmoid(lifted)
-    active = grads * sigma * (1.0 + lifted * (1.0 - sigma))
-    grad_gain = jnp.sum(active * normed, axis=(1, 2))
-    grad_offset = jnp.sum(active, axis=(1, 2))
-    scaled = (active * gains[:, None, None]).reshape(GROUPS, -1)
-    flat_normed = normed.reshape(GROUPS, -1)
-    total_count = flat_normed.shape[1] * devices
-    first_sum, second_sum = lax.psum(
-        (jnp.sum(scaled, axis=1), jnp.sum(scaled * flat_normed, axis=1)), ("dp", "tensor")
-    )
-    grad_pre = inv_std[:, None] * (
-        scaled - first_sum[:, None] / total_count - flat_normed * second_sum[:, None] / total_count
-    )
-    return (grad_pre.reshape(lifted.shape), grad_gain, grad_offset)
+MESH = pl.DeviceIdType.MESH
+LAYERS = 9
+PIX_CHUNK = 256
+
+
+def level_of(layer):
+    return layer if layer <= 4 else 8 - layer
+
+
+def stem_rows(pixels):
+    return [pixels >> (2 * level_of(layer)) for layer in range(LAYERS)]
+
+
+def row_starts(rows):
+    starts = [0]
+    for count in rows:
+        starts.append(starts[-1] + count)
+    return starts
+
+
+def split_two(values):
+    high = values.astype(jnp.bfloat16)
+    low = (values - high.astype(jnp.float32)).astype(jnp.bfloat16)
+    return jnp.concatenate([high, low], axis=1)
+
+
+def group_sum(values):
+    lane = lax.broadcasted_iota(jnp.int32, values.shape, 1)
+    pairs = values + jnp.where(
+        lane % 2 == 0, pltpu.roll(values, 127, 1), pltpu.roll(values, 1, 1)
+    )
+    return pairs + jnp.where(
+        (lane // 2) % 2 == 0, pltpu.roll(pairs, 126, 1), pltpu.roll(pairs, 2, 1)
+    )
+
+
+def wide(row):
+    return jnp.broadcast_to(row, (8, row.shape[1]))
+
+
+def my_index():
+    return lax.axis_index("dp") * 2 + lax.axis_index("tensor")
+
+
+def greet_all(count):
+    barrier = pltpu.get_barrier_semaphore()
+    me = my_index()
+
+    def greet(step, carry):
+        other = lax.rem(me + step, count)
+        pl.semaphore_signal(
+            barrier, inc=1, device_id=(other // 2, lax.rem(other, 2)), device_id_type=MESH
+        )
+        return carry
+
+    lax.fori_loop(1, count, greet, 0)
+
+
+def greeted(count):
+    pl.semaphore_wait(pltpu.get_barrier_semaphore(), count - 1)
+
+
+def send_all(count, source, target, send_sem, recv_sem):
+    me = my_index()
+
+    def send(step, carry):
+        other = lax.rem(me + step, count)
+        pltpu.make_async_remote_copy(
+            src_ref=source,
+            dst_ref=target,
+            send_sem=send_sem,
+            recv_sem=recv_sem,
+            device_id=(other // 2, lax.rem(other, 2)),
+            device_id_type=MESH,
+        ).start()
+        return carry
+
+    lax.fori_loop(1, count, send, 0, unroll=count <= 32)
+
+
+def wait_all(count, slots, sem):
+    part = slots.at[pl.ds(0, count - 1)]
+    pltpu.make_async_copy(part, part, sem).wait()
+
+
+def natural_places(tile_rows, columns):
+    spacing = columns // 8
+    places = []
+    for row in range(tile_rows):
+        for col in range(spacing):
+            place = 0
+            for bit in range(4):
+                place = place * 4 + ((row >> bit) & 1) * 2 + ((col >> bit) & 1)
+            places.append((row * columns + col, place * 8))
+    return places
+
+
+def stem_forward_kernel(
+    count,
+    places,
+    image_ref,
+    first_ref,
+    weights_ref,
+    gain_ref,
+    shift_ref,
+    feature_ref,
+    norm_ref,
+    input_ref,
+    scale_ref,
+    natural,
+    skip,
+    current,
+    source,
+    slots,
+    send_sem,
+    recv_sem,
+):
+    me = my_index()
+    greet_all(count)
+    pixels = feature_ref.shape[0]
+    rows = stem_rows(pixels)
+    norm_at = row_starts(rows)
+    input_at = row_starts(rows[1:])
+    skip_at = row_starts(rows[:4])
+    spacing = 16
+    natural[...] = lax.dot_general(
+        image_ref[...],
+        first_ref[...],
+        (((0,), (0,)), ((), ())),
+        preferred_element_type=jnp.float32,
+    )
+    for start, place in places:
+        norm_ref[place : place + 8, :] = natural[pl.ds(start, 8, stride=spacing), :]
+    for layer in range(LAYERS):
+        height = rows[layer]
+        chunk = min(height, PIX_CHUNK)
+        base = norm_at[layer]
+        total = jnp.zeros((8, 128), jnp.float32)
+        if layer > 0:
+            weights = weights_ref[layer - 1]
+            stacked = jnp.concatenate([weights, weights], axis=0)
+
+            def convolve(index, total):
+                at = pl.multiple_of(index * chunk, chunk)
+                values = jnp.dot(
+                    split_two(input_ref[pl.ds(input_at[layer - 1] + at, chunk), :]),
+                    stacked,
+                    preferred_element_type=jnp.float32,
+                )
+                norm_ref[pl.ds(base + at, chunk), :] = values
+                return total + jnp.sum(values.reshape(chunk // 8, 8, 128), axis=0)
+
+        else:
+
+            def convolve(index, total):
+                at = pl.multiple_of(index * chunk, chunk)
+                values = norm_ref[pl.ds(base + at, chunk), :]
+                return total + jnp.sum(values.reshape(chunk // 8, 8, 128), axis=0)
+
+        total = lax.fori_loop(0, height // chunk, convolve, total)
+        mean = jnp.sum(total, axis=0, keepdims=True) * (1.0 / height)
+
+        def deviate(index, total):
+            at = pl.multiple_of(index * chunk, chunk)
+            values = norm_ref[pl.ds(base + at, chunk), :] - mean
+            return total + jnp.sum((values * values).reshape(chunk // 8, 8, 128), axis=0)
+
+        square = lax.fori_loop(0, height // chunk, deviate, jnp.zeros((8, 128), jnp.float32))
+        square = jnp.sum(square, axis=0, keepdims=True)
+        stats = jnp.concatenate([mean, square], axis=0)
+        source[layer] = stats
+        slots[layer, me] = stats
+        if layer == 0:
+            greeted(count)
+        send_all(
+            count,
+            source.at[layer],
+            slots.at[layer, me],
+            send_sem.at[layer],
+            recv_sem.at[layer],
+        )
+        wait_all(count, slots.at[layer], recv_sem.at[layer])
+        means = slots[layer, :, 0, :]
+        centre = group_sum(wide(jnp.sum(means, axis=0, keepdims=True))) * (0.25 / count)
+        apart = means - centre[0:1]
+        spread = jnp.sum(slots[layer, :, 1, :], axis=0, keepdims=True) + height * jnp.sum(
+            apart * apart, axis=0, keepdims=True
+        )
+        variance = group_sum(wide(spread)) * (1.0 / (4 * height * count))
+        inverse = lax.rsqrt(variance + group_eps)[0:1]
+        centre = centre[0:1]
+        scale_ref[layer : layer + 1, :] = inverse
+        gain = gain_ref[layer : layer + 1, :]
+        shift = shift_ref[layer : layer + 1, :]
+
+        def activate(start, size):
+            normed = (norm_ref[pl.ds(base + start, size), :] - centre) * inverse
+            norm_ref[pl.ds(base + start, size), :] = normed
+            lifted = normed * gain + shift
+            return lifted / (1.0 + jnp.exp(-lifted))
+
+        if layer < 4:
+            quarter = height // 4
+            part = min(quarter, 64)
+
+            def pool(index, carry):
+                at = pl.multiple_of(index * part, part)
+                mean_of = jnp.zeros((part, 128), jnp.float32)
+                for corner in range(4):
+                    value = activate(corner * quarter + at, part)
+                    skip[pl.ds(skip_at[layer] + corner * quarter + at, part), :] = value
+                    mean_of = mean_of + value
+                input_ref[pl.ds(input_at[layer] + at, part), :] = mean_of * 0.25
+                return carry
+
+            lax.fori_loop(0, quarter // part, pool, 0)
+        elif layer < 8:
+            part = min(height, 64)
+            skipped = skip_at[7 - layer]
+
+            def grow(index, carry):
+                at = pl.multiple_of(index * part, part)
+                value = activate(at, part)
+                for corner in range(4):
+                    place = corner * height + at
+                    input_ref[pl.ds(input_at[layer] + place, part), :] = (
+                        value + skip[pl.ds(skipped + place, part), :]
+                    )
+                return carry
+
+            lax.fori_loop(0, height // part, grow, 0)
+        else:
+
+            def finish(index, carry):
+                at = pl.multiple_of(index * chunk, chunk)
+                current[pl.ds(at, chunk), :] = activate(at, chunk)
+                return carry
+
+            lax.fori_loop(0, height // chunk, finish, 0)
+    for start, place in places:
+        feature_ref[pl.ds(start, 8, stride=spacing), :] = current[place : place + 8, :]
+    for layer in range(LAYERS):
+        wait_all(count, slots.at[layer], send_sem.at[layer])
+
+
+def stem_backward_kernel(
+    count,
+    places,
+    grad_ref,
+    image_ref,
+    norm_ref,
+    input_ref,
+    scale_ref,
+    weights_ref,
+    gain_ref,
+    shift_ref,
+    first_out,
+    weights_out,
+    gain_out,
+    shift_out,
+    natural,
+    ordered,
+    active,
+    grad_conv,
+    skip,
+    grads,
+    product,
+    source,
+    slots,
+    first_source,
+    first_slots,
+    parts,
+    shared,
+    send_sem,
+    recv_sem,
+    part_send,
+    part_recv,
+    share_send,
+    share_recv,
+):
+    me = my_index()
+    greet_all(count)
+    pixels = grad_ref.shape[0]
+    rows = stem_rows(pixels)
+    norm_at = row_starts(rows)
+    input_at = row_starts(rows[1:])
+    skip_at = row_starts(rows[:4])
+    spacing = 16
+    owners = count // 8
+    owned = parts.shape[1]
+    for start, place in places:
+        ordered[place : place + 8, :] = grad_ref[pl.ds(start, 8, stride=spacing), :]
+
+    def weight_grad(layer):
+        height = rows[layer]
+        chunk = min(height, 512)
+
+        def add(index, total):
+            at = pl.multiple_of(index * chunk, chunk)
+            return total + lax.dot_general(
+                input_ref[pl.ds(input_at[layer - 1] + at, chunk), :].astype(jnp.bfloat16),
+                grad_conv[pl.ds(norm_at[layer] + at, chunk), :].astype(jnp.bfloat16),
+                (((0,), (0,)), ((), ())),
+                preferred_element_type=jnp.float32,
+            )
+
+        product[layer - 1] = lax.fori_loop(
+            0, height // chunk, add, jnp.zeros((128, 128), jnp.float32)
+        ).reshape(owners, owned, 128)
+
+        def send(index, carry):
+            owner = layer - 1 + 8 * index
+
+            @pl.when(owner != me)
+            def _():
+                pltpu.make_async_remote_copy(
+                    src_ref=product.at[layer - 1, index],
+                    dst_ref=parts.at[me],
+                    send_sem=part_send,
+                    recv_sem=part_recv,
+                    device_id=(owner // 2, lax.rem(owner, 2)),
+                    device_id_type=MESH,
+                ).start()
+
+            @pl.when(owner == me)
+            def _():
+                parts[me] = product[layer - 1, index]
+
+            return carry
+
+        lax.fori_loop(0, owners, send, 0)
+
+    for layer in range(LAYERS - 1, -1, -1):
+        height = rows[layer]
+        chunk = min(height, PIX_CHUNK)
+        base = norm_at[layer]
+        gain = gain_ref[layer : layer + 1, :]
+        shift = shift_ref[layer : layer + 1, :]
+        inverse = scale_ref[layer : layer + 1, :]
+        incoming = ordered if layer == 8 else grads
+
+        def activate(index, carry):
+            first, second = carry
+            at = pl.multiple_of(index * chunk, chunk)
+            normed = norm_ref[pl.ds(base + at, chunk), :]
+            lifted = normed * gain + shift
+            sigma = 1.0 / (1.0 + jnp.exp(-lifted))
+            value = incoming[pl.ds(at, chunk), :] * sigma * (1.0 + lifted * (1.0 - sigma))
+            active[pl.ds(at, chunk), :] = value
+            first = first + jnp.sum(value.reshape(chunk // 8, 8, 128), axis=0)
+            second = second + jnp.sum((value * normed).reshape(chunk // 8, 8, 128), axis=0)
+            return first, second
+
+        zero = jnp.zeros((8, 128), jnp.float32)
+        first, second = lax.fori_loop(0, height // chunk, activate, (zero, zero))
+        sums = jnp.concatenate(
+            [jnp.sum(first, axis=0, keepdims=True), jnp.sum(second, axis=0, keepdims=True)], axis=0
+        )
+        source[layer] = sums
+        slots[layer, me] = sums
+        if layer == 8:
+            greeted(count)
+        send_all(
+            count, source.at[layer], slots.at[layer, me], send_sem.at[layer], recv_sem.at[layer]
+        )
+        if layer < 8:
+            weight_grad(layer + 1)
+        wait_all(count, slots.at[layer], recv_sem.at[layer])
+        totals = jnp.sum(slots[layer], axis=0)
+        shift_out[layer : layer + 1, :] = totals[0:1]
+        gain_out[layer : layer + 1, :] = totals[1:2]
+        share = 1.0 / (4 * height * count)
+        first_mean = group_sum(wide(totals[0:1] * gain))[0:1] * share
+        second_mean = group_sum(wide(totals[1:2] * gain))[0:1] * share
+
+        def conv_grad(start, size):
+            value = inverse * (
+                active[pl.ds(start, size), :] * gain
+                - first_mean
+                - norm_ref[pl.ds(base + start, size), :] * second_mean
+            )
+            grad_conv[pl.ds(base + start, size), :] = value
+            return value
+
+        if layer > 0:
+            weights = weights_ref[layer - 1]
+            stacked = jnp.concatenate([weights, weights], axis=1)
+
+            def input_grad(start, size):
+                return lax.dot_general(
+                    split_two(conv_grad(start, size)),
+                    stacked,
+                    (((1,), (1,)), ((), ())),
+                    preferred_element_type=jnp.float32,
+                )
+
+        if layer > 4:
+            quarter = height // 4
+            part = min(quarter, 64)
+            skipped = skip_at[8 - layer]
+
+            def shrink(index, carry):
+                at = pl.multiple_of(index * part, part)
+                total = jnp.zeros((part, 128), jnp.float32)
+                for corner in range(4):
+                    place = corner * quarter + at
+                    value = input_grad(place, part)
+                    skip[pl.ds(skipped + place, part), :] = value
+                    total = total + value
+                grads[pl.ds(at, part), :] = total
+                return carry
+
+            lax.fori_loop(0, quarter // part, shrink, 0)
+        elif layer > 0:
+            part = min(height, 128)
+            skipped = skip_at[layer - 1]
+
+            def spread_out(index, carry):
+                at = pl.multiple_of(index * part, part)
+                value = input_grad(at, part) * 0.25
+                for corner in range(4):
+                    place = corner * height + at
+                    grads[pl.ds(place, part), :] = value + skip[pl.ds(skipped + place, part), :]
+                return carry
+
+            lax.fori_loop(0, height // part, spread_out, 0)
+        else:
+
+            def finish(index, carry):
+                at = pl.multiple_of(index * chunk, chunk)
+                conv_grad(at, chunk)
+                return carry
+
+            lax.fori_loop(0, height // chunk, finish, 0)
+    for start, place in places:
+        natural[pl.ds(start, 8, stride=spacing), :] = grad_conv[place : place + 8, :]
+    first_part = jnp.dot(
+        image_ref[...], natural[...].astype(jnp.bfloat16), preferred_element_type=jnp.float32
+    )
+    first_source[...] = first_part
+    first_slots[me] = first_part
+    send_all(count, first_source, first_slots.at[me], send_sem.at[LAYERS], recv_sem.at[LAYERS])
+    wait_all(count, parts, part_recv)
+    mine = jnp.sum(parts[...], axis=0)
+    shared[me] = mine
+    send_all(count, shared.at[me], shared.at[me], share_send, share_recv)
+    wait_all(count, first_slots, recv_sem.at[LAYERS])
+    first_out[...] = jnp.sum(first_slots[...], axis=0)
+    wait_all(count, shared, share_recv)
+    for device in range(count):
+        weights_out[device % 8, (device // 8) * owned : (device // 8 + 1) * owned, :] = shared[
+            device
+        ]
+    for layer in range(LAYERS):
+        wait_all(count, slots.at[layer], send_sem.at[layer])
+    wait_all(count, first_slots, send_sem.at[LAYERS])
+    wait_all(count, parts, part_send)
+    wait_all(count, shared, share_send)
 
 
 def stem_forward(page_image, conv_first, conv_weights, group_gain, group_shift, devices):
-    records = []
-    layer_in = page_image.astype(jnp.float32)
-    current, lifted, normed, inv_std = group_forward(
-        conv_apply(conv_first, layer_in), group_gain[0], group_shift[0], devices
-    )
-    records.append((layer_in, lifted, normed, inv_std))
-    downs = [current]
-    for level in range(1, 5):
-        layer_in = pool_down(current)
-        current, lifted, normed, inv_std = group_forward(
-            conv_apply(conv_weights[level - 1], layer_in),
-            group_gain[level],
-            group_shift[level],
-            devices,
-        )
-        records.append((layer_in, lifted, normed, inv_std))
-        downs.append(current)
-    for level in range(3, -1, -1):
-        layer_in = pool_up(current) + downs[level]
-        current, lifted, normed, inv_std = group_forward(
-            conv_apply(conv_weights[7 - level], layer_in),
-            group_gain[8 - level],
-            group_shift[8 - level],
-            devices,
-        )
-        records.append((layer_in, lifted, normed, inv_std))
-    return (current, records)
-
-
-def stem_backward(grads, records, conv_weights, group_gain, devices):
-    grad_convs = [None] * 8
-    grad_gains = [None] * 9
-    grad_offsets = [None] * 9
-    skips = [None] * 4
-    for level in range(4):
-        layer = 8 - level
-        layer_in, lifted, normed, inv_std = records[layer]
-        grad_pre, grad_gains[layer], grad_offsets[layer] = group_backward(
-            grads, lifted, normed, inv_std, group_gain[layer], devices
-        )
-        grad_convs[7 - level], grad_in = conv_back(conv_weights[7 - level], layer_in, grad_pre)
-        skips[level] = grad_in
-        grads = pool_up_back(grad_in)
-    for level in range(4, 0, -1):
-        layer_in, lifted, normed, inv_std = records[level]
-        grad_pre, grad_gains[level], grad_offsets[level] = group_backward(
-            grads, lifted, normed, inv_std, group_gain[level], devices
-        )
-        grad_convs[level - 1], grad_in = conv_back(conv_weights[level - 1], layer_in, grad_pre)
-        grads = pool_down_back(grad_in) + skips[level - 1]
-    layer_in, lifted, normed, inv_std = records[0]
-    grad_pre, grad_gains[0], grad_offsets[0] = group_backward(
-        grads, lifted, normed, inv_std, group_gain[0], devices
-    )
-    grad_first = jnp.einsum("crw,orw->co", layer_in, grad_pre, precision=highest)
-    return (grad_first, jnp.stack(grad_convs), jnp.stack(grad_gains), jnp.stack(grad_offsets))
+    planes, tile_rows, columns = page_image.shape
+    pixels = tile_rows * columns
+    rows = stem_rows(pixels)
+    image = page_image.reshape(planes, pixels)
+    places = natural_places(tile_rows, columns)
+    whole = pl.BlockSpec(memory_space=pltpu.VMEM)
+    return pl.pallas_call(
+        functools.partial(stem_forward_kernel, devices, places),
+        out_shape=(
+            jax.ShapeDtypeStruct((pixels, 128), jnp.float32),
+            jax.ShapeDtypeStruct((sum(rows), 128), jnp.float32),
+            jax.ShapeDtypeStruct((sum(rows[1:]), 128), jnp.float32),
+            jax.ShapeDtypeStruct((LAYERS, 128), jnp.float32),
+        ),
+        in_specs=[whole] * 5,
+        out_specs=(whole,) * 4,
+        scratch_shapes=[
+            pltpu.VMEM((pixels, 128), jnp.float32),
+            pltpu.VMEM((sum(rows[:4]), 128), jnp.float32),
+            pltpu.VMEM((pixels, 128), jnp.float32),
+            pltpu.VMEM((LAYERS, 2, 128), jnp.float32),
+            pltpu.VMEM((LAYERS, devices, 2, 128), jnp.float32),
+            pltpu.SemaphoreType.DMA((LAYERS,)),
+            pltpu.SemaphoreType.DMA((LAYERS,)),
+        ],
+        compiler_params=pltpu.CompilerParams(
+            collective_id=0, has_side_effects=True, vmem_limit_bytes=40 * 2**20
+        ),
+        name="stem_forward",
+    )(image, conv_first, conv_weights, group_gain, group_shift)
+
+
+def stem_backward(
+    grad_map, page_image, records, conv_weights, group_gain, group_shift, devices
+):
+    planes, tile_rows, columns = page_image.shape
+    pixels = tile_rows * columns
+    rows = stem_rows(pixels)
+    norms, inputs, scales = records
+    image = page_image.reshape(planes, pixels)
+    places = natural_places(tile_rows, columns)
+    whole = pl.BlockSpec(memory_space=pltpu.VMEM)
+    owned = 1024 // devices
+    return pl.pallas_call(
+        functools.partial(stem_backward_kernel, devices, places),
+        out_shape=(
+            jax.ShapeDtypeStruct((planes, 128), jnp.float32),
+            jax.ShapeDtypeStruct((8, 128, 128), jnp.float32),
+            jax.ShapeDtypeStruct((LAYERS, 128), jnp.float32),
+            jax.ShapeDtypeStruct((LAYERS, 128), jnp.float32),
+        ),
+        in_specs=[whole] * 8,
+        out_specs=(whole,) * 4,
+        scratch_shapes=[
+            pltpu.VMEM((pixels, 128), jnp.float32),
+            pltpu.VMEM((pixels, 128), jnp.float32),
+            pltpu.VMEM((pixels, 128), jnp.float32),
+            pltpu.VMEM((sum(rows), 128), jnp.float32),
+            pltpu.VMEM((sum(rows[:4]), 128), jnp.float32),
+            pltpu.VMEM((pixels, 128), jnp.float32),
+            pltpu.VMEM((8, devices // 8, owned, 128), jnp.float32),
+            pltpu.VMEM((LAYERS, 2, 128), jnp.float32),
+            pltpu.VMEM((LAYERS, devices, 2, 128), jnp.float32),
+            pltpu.VMEM((planes, 128), jnp.float32),
+            pltpu.VMEM((devices, planes, 128), jnp.float32),
+            pltpu.VMEM((devices, owned, 128), jnp.float32),
+            pltpu.VMEM((devices, owned, 128), jnp.float32),
+            pltpu.SemaphoreType.DMA((LAYERS + 1,)),
+            pltpu.SemaphoreType.DMA((LAYERS + 1,)),
+            pltpu.SemaphoreType.DMA,
+            pltpu.SemaphoreType.DMA,
+            pltpu.SemaphoreType.DMA,
+            pltpu.SemaphoreType.DMA,
+        ],
+        compiler_params=pltpu.CompilerParams(
+            collective_id=1, has_side_effects=True, vmem_limit_bytes=40 * 2**20
+        ),
+        name="stem_backward",
+    )(grad_map, image, norms, inputs, scales, conv_weights, group_gain, group_shift)
 
 
 def rms_forward(values, gains):
@@ -240,7 +665,7 @@
     down_proj,
 ):
     devices = lax.axis_size("dp") * lax.axis_size("tensor")
-    feature_map, records = stem_forward(
+    feature_map, *records = stem_forward(
         page_image, conv_first, conv_weights, group_gain, group_shift, devices
     )
     tile_rows = page_image.shape[1]
@@ -257,8 +682,11 @@
         (col_ids[None, :] >= left_edge[:, None]) & (col_ids[None, :] < right_edge[:, None])
     ).astype(jnp.float32)
     box_area = ((bottom_edge - top_edge) * (right_edge - left_edge)).astype(jnp.float32)
-    column_sums = jnp.einsum("crw,tw->crt", feature_map, col_mask, precision=highest)
-    partial_boxes = jnp.einsum("crt,tr->tc", column_sums, row_mask, precision=highest)
+    box_mask = (row_mask[:, :, None] * col_mask[:, None, :]).astype(jnp.bfloat16)
+    box_mask = box_mask.reshape(box_mask.shape[0], -1)
+    feature_pair = split_two(feature_map)
+    box_pair = jnp.dot(box_mask, feature_pair, preferred_element_type=jnp.float32)
+    partial_boxes = box_pair[:, :128] + box_pair[:, 128:]
     box_sums = lax.psum(partial_boxes, "tensor")
     pooled = (box_sums / box_area[:, None]).astype(jnp.bfloat16)
     stream = embeddings.astype(jnp.float32) + jnp.dot(
@@ -385,12 +813,11 @@
     grad_roi = jnp.dot(pooled.T, grad_low, preferred_element_type=jnp.float32)
     grad_pooled = jnp.dot(grad_low, roi_proj.T, preferred_element_type=jnp.float32)
     grad_box = grad_pooled / box_area[:, None]
-    spread_rows = grad_box.T[:, None, :] * row_mask.T[None, :, :]
-    grad_map = jnp.einsum("crt,tw->crw", spread_rows, col_mask, precision=highest)
-    grad_first, grad_convs, grad_gains, grad_offsets = stem_backward(
-        grad_map, records, conv_weights, group_gain, devices
-    )
-    stem_totals = lax.psum((grad_first, grad_convs, grad_gains, grad_offsets), ("dp", "tensor"))
+    map_pair = jnp.dot(box_mask.T, split_two(grad_box), preferred_element_type=jnp.float32)
+    grad_map = map_pair[:, :128] + map_pair[:, 128:]
+    stem_totals = stem_backward(
+        grad_map, page_image, records, conv_weights, group_gain, group_shift, devices
+    )
     table_totals = lax.psum(grad_tables, "dp")
     weight_parts = (
         lax.psum_scatter(grad_roi, "dp", scatter_dimension=1, tiled=True),

time: 2480 us -> 1560 us (0.63)
  blocking collectives: 1210 us -> 77.1 us
  waiting for transfers between devices: 334 us -> 605 us
  Pallas kernels: 0 us -> 116 us
  local copies, waits for them, and re-layouts: 258 us -> 198 us
  other arithmetic: 154 us -> 96.3 us
  matrix products: 489 us -> 438 us
    psum x28 -> x0, blocking collectives: 1130 us -> none  [the longest x9 365 us: group_forward(): spread = lax.psum(jnp.sum(centred * centred, axis=1), ('dp', 'tensor'))]
    reduce_scatter x1, waiting for transfers between devices: 0.01 us -> 142 us  [on_device(): lax.psum_scatter(grad_up, 'dp', scatter_dimension=0, tiled=True)]
    psum x1 -> x0, waiting for transfers between devices: 133 us -> none  [on_device(): lax.psum((grad_first, grad_convs, grad_gains, grad_offsets), ('dp', 'tens...]
    reduce_scatter x1, waiting for transfers between devices: 0.01 us -> 128 us  [on_device(): lax.psum_scatter(grad_query_proj, 'dp', scatter_dimension=0, tiled=True)]
    pallas_call x0 -> x2, Pallas kernels: none -> 116 us  [the longest x1 62.2 us: stem_backward(): pl.pallas_call(functools.partial(stem_backward_kernel, devices, places),...]
    reduce_scatter x1, waiting for transfers between devices: 42.1 us -> 142 us  [on_device(): lax.psum_scatter(grad_down, 'dp', scatter_dimension=1, tiled=True)]
    reduce_sum x62 -> x0, other arithmetic: 45.6 us -> none  [the longest x18 16.9 us: group_forward(): spread = lax.psum(jnp.sum(centred * centred, axis=1), ('dp', 'tensor'))]
    dot_general x27 -> x2, matrix products: 49.4 us -> 5.69 us  [the longest x1 4.44 us: on_device(): jnp.dot(box_mask.T, split_two(grad_box), preferred_element_type=jnp.float32)]
  transfers between devices with their start and end apart: 12 -> 11, of which waited for: 5 -> 7; matrix products, arithmetic and copies ran while one was open for 24% -> 35% of each run, Pallas kernels for 0% -> 4%
where the time goes in v1:
time: 1560 us; the launch traced here: 1550 us
  waiting for transfers between devices  605 us (39%)
  matrix products  438 us (28%)
  local copies, waits for them, and re-layouts  198 us (13%)
  Pallas kernels  116 us (7%)
  other arithmetic  96.3 us (6%)
  blocking collectives  77.1 us (5%)
  between operations  16 us (1%)
    reduce_scatter x1, waiting for transfers between devices, on_device(): lax.psum_scatter(grad_down, 'dp', scatter_dimension=1, tiled=True)  142 us
    reduce_scatter x1, waiting for transfers between devices, on_device(): lax.psum_scatter(grad_up, 'dp', scatter_dimension=0, tiled=True)  142 us
    reduce_scatter x1, waiting for transfers between devices, on_device(): lax.psum_scatter(grad_query_proj, 'dp', scatter_dimension=0, tiled=True)  128 us
    reduce_scatter x1, waiting for transfers between devices, on_device(): lax.psum_scatter(grad_roi, 'dp', scatter_dimension=1, tiled=True)  126 us
    unnamed x1, blocking collectives  77.1 us
    dot_general x6, matrix products, bucket_sums(): jnp.einsum('hqk,qkb->bh', grad_lower, table, preferred_element_type=jnp.f...  70.2 us
    dot_general x6, matrix products, bucket_sums(): jnp.einsum('hqk,qkb->bh', grad_upper, table, preferred_element_type=jnp.f...  70.1 us
    pallas_call x1, Pallas kernels, stem_backward(): pl.pallas_call(functools.partial(stem_backward_kernel, devices, places),...  62.2 us
  transfers between devices with their start and end apart: 11, of which 7 were waited for; matrix products, arithmetic and copies ran while one was open for 35% of the time, Pallas kernels for 4%

profile of v1, /device:TPU:0, one launch (start us, length us, event | category | flops | bytes accessed | tf_op | source)
XLA Modules:
  0.0 1548.0 jit_solution(5018438773811901593)
XLA Ops:
  12.2 54.2 %stem_forward.1 = (f32[2048,128]{1,0:T(8,128)S(1)}, f32[5448,128]{1,0:T(8,128)S(1)}, f32[3400,128]{1,0:T(8,128)S(1)}, f32[9,128]{1,0:T(8,128)S(1)}) custom-call(bf16[3,2048]{1,0:T(4,128)(2,1)S(1)} %bitcast.196, bf16[3,128]{1,0:T(4,128)(2,1)S(1)} %copy-done.14, bf16[8,128,128]{2,1,0:T(8,128)(2,1)S(1)} %copy-done.6, f32[9,128]{1,0:T(8,128)S(1)} %copy-done.10, ...), custom_call_target="tpu_custom_call" | custom-call | tf_op jit(solution)/shard_map/stem_forward/pallas_call | solution.py:504
  92.9 23.8 %fusion.14 = f32[512,1024,6]{0,2,1:T(8,128)} fusion(s32[512,1024]{0,1:T(8,128)} %copy.122, f32[3,32,6]{1,2,0:T(8,128)S(1)} %copy-done.74), kind=kOutput, calls=%fused_computation.19 | convolution fusion | flops 1224736768 | bytes 14684160 | tf_op jit(solution)/shard_map/qkb,bh->hqk/dot_general | solution.py:617
  116.8 23.0 %fusion.11 = f32[512,1024,6]{0,2,1:T(8,128)} fusion(s32[512,1024]{0,1:T(8,128)S(1)} %copy-done.25, f32[3,32,6]{1,2,0:T(8,128)S(1)} %copy-done.74), kind=kOutput, calls=%fused_computation.15 | convolution fusion | flops 1224736768 | bytes 14684160 | tf_op jit(solution)/shard_map/qkb,bh->hqk/dot_general | solution.py:624
  146.2 23.8 %fusion.17 = f32[512,1024,6]{0,2,1:T(8,128)} fusion(s32[512,1024]{0,1:T(8,128)} %copy.120, f32[3,32,6]{1,2,0:T(8,128)S(1)} %copy-done.74), kind=kOutput, calls=%fused_computation.23 | convolution fusion | flops 1224736768 | bytes 14684160 | tf_op jit(solution)/shard_map/qkb,bh->hqk/dot_general | solution.py:610
  172.9 23.6 %fusion.5 = f32[512,1024,6]{0,2,1:T(8,128)} fusion(s32[512,1024]{0,1:T(8,128)} %copy.131, f32[3,32,6]{1,2,0:T(8,128)S(1)} %copy-done.74), kind=kOutput, calls=%fused_computation.7 | convolution fusion | flops 1224736768 | bytes 14684160 | tf_op jit(solution)/shard_map/qkb,bh->hqk/dot_general | solution.py:617
  199.4 23.8 %fusion.2 = f32[512,1024,6]{0,2,1:T(8,128)} fusion(s32[512,1024]{0,1:T(8,128)} %copy.135, f32[3,32,6]{1,2,0:T(8,128)S(1)} %copy-done.74), kind=kOutput, calls=%fused_computation.3 | convolution fusion | flops 1224736768 | bytes 14684160 | tf_op jit(solution)/shard_map/qkb,bh->hqk/dot_general | solution.py:624
  229.6 24.0 %fusion.8 = f32[512,1024,6]{0,2,1:T(8,128)} fusion(s32[512,1024]{0,1:T(8,128)} %copy.129, f32[3,32,6]{1,2,0:T(8,128)S(1)} %copy-done.74), kind=kOutput, calls=%fused_computation.11 | convolution fusion | flops 1224736768 | bytes 14684160 | tf_op jit(solution)/shard_map/qkb,bh->hqk/dot_general | solution.py:610
  256.2 15.7 %copy.125 = f32[512,1024,6]{1,0,2:T(8,128)} copy(f32[512,1024,6]{0,2,1:T(8,128)} %fusion.14) | data formatting | bytes 25165824 | tf_op jit(solution)/shard_map/qkb,bh->hqk/dot_general | solution.py:617
  271.9 15.6 %copy.128 = f32[512,1024,6]{1,0,2:T(8,128)} copy(f32[512,1024,6]{0,2,1:T(8,128)} %fusion.11) | data formatting | bytes 25165824 | tf_op jit(solution)/shard_map/qkb,bh->hqk/dot_general | solution.py:624
  287.5 15.7 %copy.124 = f32[512,1024,6]{1,0,2:T(8,128)} copy(f32[512,1024,6]{0,2,1:T(8,128)} %fusion.17) | data formatting | bytes 25165824 | tf_op jit(solution)/shard_map/qkb,bh->hqk/dot_general | solution.py:610
  303.2 15.7 %copy.134 = f32[512,1024,6]{1,0,2:T(8,128)} copy(f32[512,1024,6]{0,2,1:T(8,128)} %fusion.5) | data formatting | bytes 25165824 | tf_op jit(solution)/shard_map/qkb,bh->hqk/dot_general | solution.py:617
  318.8 15.7 %copy.137 = f32[512,1024,6]{1,0,2:T(8,128)} copy(f32[512,1024,6]{0,2,1:T(8,128)} %fusion.2) | data formatting | bytes 25165824 | tf_op jit(solution)/shard_map/qkb,bh->hqk/dot_general | solution.py:624
  334.5 15.8 %copy.133 = f32[512,1024,6]{1,0,2:T(8,128)} copy(f32[512,1024,6]{0,2,1:T(8,128)} %fusion.8) | data formatting | bytes 25165824 | tf_op jit(solution)/shard_map/qkb,bh->hqk/dot_general | solution.py:610
  361.5 19.5 %fusion.195 = (f32[6,512]{1,0:T(8,128)}, f32[6,512,1024]{2,1,0:T(8,128)}) fusion(f32[512,1024,6]{1,0,2:T(8,128)} %copy.128, f32[512,1024,6]{1,0,2:T(8,128)} %copy.124, f32[512,1024,6]{1,0,2:T(8,128)} %copy.125, bf16[512,6,64]{0,2,1:T(8,128)(2,1)} %bitcast.212, bf16[1024,6,64]{0,2,1:T(8,128)(2,1)S(1)} %bitcast.202, pred[512,1024]{1,0:T(8,128)(4,1)} %get-tuple-element.113), kind=kOutput, calls=%fused_computation.279 | convolution fusion | flops 421524480 | bytes 52047872 | tf_op jit(solution)/shard_map/qhd,khd->hqk/dot_general | solution.py:632
  393.6 19.7 %fusion.194 = (f32[6,512]{1,0:T(8,128)}, f32[6,512,1024]{2,1,0:T(8,128)}) fusion(f32[512,1024,6]{1,0,2:T(8,128)} %copy.137, f32[512,1024,6]{1,0,2:T(8,128)} %copy.133, f32[512,1024,6]{1,0,2:T(8,128)} %copy.134, bf16[512,6,64]{0,2,1:T(8,128)(2,1)S(1)} %bitcast.210, bf16[1024,6,64]{0,2,1:T(8,128)(2,1)S(1)} %bitcast.203, pred[512,1024]{1,0:T(8,128)(4,1)} %get-tuple-element.114), kind=kOutput, calls=%fused_computation.278 | convolution fusion | flops 421524480 | bytes 52047872 | tf_op jit(solution)/shard_map/qhd,khd->hqk/dot_general | solution.py:632
  429.4 23.4 %all-reduce.11.cloned.1.call-done = f32[1024,768]{0,1:T(8,128)} async-done(((f32[1024,768]{0,1:T(8,128)}), f32[1024,768]{0,1:T(8,128)}) %all-reduce.11.cloned.1.call-update) | async-done | bytes 3145744 | tf_op jit(solution)/shard_map/psum | solution.py:734
  459.9 18.0 %add_convert_fusion = (bf16[1024,1536]{1,0:T(8,128)(2,1)S(1)}, f32[1024,1536]{1,0:T(8,128)}) fusion(f32[1024,1536]{1,0:T(8,128)S(1)} %fusion.185, bf16[1024,768]{1,0:T(8,128)(2,1)S(1)} %copy-done.52, bf16[1536,768]{1,0:T(8,128)(2,1)S(1)} %copy-done), kind=kOutput, calls=%fused_computation.69 | convolution fusion | flops 2529165312 | bytes 19660800 | tf_op jit(solution)/shard_map/dot_general | solution.py:743
  555.3 12.5 subtract_convert_fusion
  607.9 12.1 copy.152
  620.0 12.6 fusion.138
  654.1 12.1 copy.146
  666.2 12.7 fusion.132
  713.7 12.7 fusion.136
  737.4 12.9 fusion.147
  750.4 13.4 fusion.145
  800.5 77.1 %all-reduce.2 = (f32[768]{0:T(1024)S(1)}, f32[3,32,6]{1,2,0:T(8,128)}, f32[768]{0:T(1024)S(1)}) all-reduce(f32[768]{0:T(1024)S(1)} %get-tuple-element.82, f32[3,32,6]{1,2,0:T(8,128)S(1)} %maximum_add_fusion, f32[768]{0:T(1024)S(1)} %copy-done.79), channel_id=3, replica_groups=mesh['dp'=16,'tensor'=2] {'dp'}, use_global_device_ids=true, to_apply=%region_17.18.clone | all-reduce | flops 2112 | bytes 16896
  899.3 62.2 %stem_backward.1 = (f32[3,128]{1,0:T(4,128)S(1)}, f32[8,128,128]{2,1,0:T(8,128)S(1)}, f32[9,128]{1,0:T(8,128)S(1)}, f32[9,128]{1,0:T(8,128)S(1)}) custom-call(f32[2048,128]{1,0:T(8,128)S(1)} %slice_add_fusion.grad_ref, bf16[3,2048]{1,0:T(4,128)(2,1)S(1)} %bitcast.197, f32[5448,128]{1,0:T(8,128)S(1)} %copy-done.3, f32[3400,128]{1,0:T(8,128)S(1)} %copy-done.5, ...), custom_call_target="tpu_custom_call" | custom-call | tf_op jit(solution)/shard_map/stem_backward/pallas_call | solution.py:541
  965.8 35.0 %reduce-scatter.12.cloned.1.call-done = f32[48,384]{1,0:T(8,128)} async-done(((f32[768,384]{1,0:T(8,128)}), f32[48,384]{1,0:T(8,128)}) %reduce-scatter.12.cloned.1.call-update) | async-done | bytes 73744 | tf_op jit(solution)/shard_map/reduce_scatter | solution.py:826
  1000.8 127.9 %reduce-scatter.10.cloned.1.call-done = f32[48,384]{1,0:T(8,128)} async-done(((f32[768,384]{1,0:T(8,128)}), f32[48,384]{1,0:T(8,128)}) %reduce-scatter.10.cloned.1.call-update) | async-done | bytes 73744 | tf_op jit(solution)/shard_map/reduce_scatter | solution.py:825
  1128.7 141.9 %reduce-scatter.18.cloned.1.call-done = f32[48,1536]{1,0:T(8,128)} async-done(((f32[768,1536]{1,0:T(8,128)}), f32[48,1536]{1,0:T(8,128)}) %reduce-scatter.18.cloned.1.call-update) | async-done | bytes 294928 | tf_op jit(solution)/shard_map/reduce_scatter | solution.py:830
  1270.6 142.4 %reduce-scatter.20.cloned.1.call-done = f32[1536,48]{0,1:T(8,128)} async-done(((f32[1536,768]{0,1:T(8,128)}), f32[1536,48]{0,1:T(8,128)}) %reduce-scatter.20.cloned.1.call-update) | async-done | bytes 294928 | tf_op jit(solution)/shard_map/reduce_scatter | solution.py:831
  1413.0 125.6 %reduce-scatter.8.cloned.1.call-done = f32[128,48]{0,1:T(8,128)} async-done(((f32[128,768]{0,1:T(8,128)}), f32[128,48]{0,1:T(8,128)}) %reduce-scatter.8.cloned.1.call-update) | async-done | bytes 24592 | tf_op jit(solution)/shard_map/reduce_scatter | solution.py:823
  (319 shorter events, 347.9 us)
Async XLA Ops:
  7.2 452.7 %copy-start = (bf16[1536,768]{1,0:T(8,128)(2,1)S(1)}, bf16[1536,768]{1,0:T(8,128)(2,1)}, u32[]{:S(2)}) copy-start(bf16[1536,768]{1,0:T(8,128)(2,1)} %param.39) | copy-start | bytes 7077892
  7.2 345.5 %all-reduce.9.cloned.1.call-start = ((), (), s32[]{:S(2)}) async-start(), calls=%async_computation.7 | async-start | bytes 1048576 | tf_op jit(solution)/shard_map/psum | solution.py:690
  9.1 63.6 %copy-start.8 = (bf16[1,3,16,128]{3,1,2,0:T(4,128)(2,1)}, bf16[1,3,16,128]{3,1,2,0:T(4,128)(2,1)S(1)}, u32[]{:S(2)}) copy-start(bf16[1,3,16,128]{3,1,2,0:T(4,128)(2,1)S(1)} %copy.196) | copy-start | bytes 36868
  75.6 377.2 %all-reduce.11.cloned.1.call-start = ((), (), s32[]{:S(2)}) async-start(), calls=%async_computation.8 | async-start | bytes 6291456 | tf_op jit(solution)/shard_map/psum | solution.py:734
  75.9 276.8 %copy-start.72 = (f32[1024]{0:T(1024)}, f32[1024]{0:T(1024)S(1)}, u32[]{:S(2)}) copy-start(f32[1024]{0:T(1024)S(1)} %multiply_convert_fusion.5) | copy-start | bytes 12292
  92.9 23.8 %copy-start.25 = (s32[512,1024]{0,1:T(8,128)S(1)}, s32[512,1024]{0,1:T(8,128)}, u32[]{:S(2)}) copy-start(s32[512,1024]{0,1:T(8,128)} %copy.126) | copy-start | bytes 6291460
  229.6 24.1 %copy-start.80 = (s32[1,1024]{1,0:T(1,128)S(1)}, s32[1,1024]{1,0:T(1,128)}, u32[]{:S(2)}) copy-start(s32[1,1024]{1,0:T(1,128)} %param.23) | copy-start | bytes 12292
  334.5 15.8 %copy-start.81 = (s32[1,1024]{1,0:T(1,128)S(1)}, s32[1,1024]{1,0:T(1,128)}, u32[]{:S(2)}) copy-start(s32[1,1024]{1,0:T(1,128)} %param.24) | copy-start | bytes 12292
  334.5 18.2 %copy-start.56 = (bf16[128,768]{1,0:T(8,128)(2,1)S(1)}, bf16[128,768]{1,0:T(8,128)(2,1)}, u32[]{:S(2)}) copy-start(bf16[128,768]{1,0:T(8,128)(2,1)} %param.30) | copy-start | bytes 589828
  359.7 33.9 %copy-start.40 = (bf16[512,384]{0,1:T(8,128)(2,1)}, bf16[512,384]{0,1:T(8,128)(2,1)S(1)}, u32[]{:S(2)}) copy-start(bf16[512,384]{0,1:T(8,128)(2,1)S(1)} %get-tuple-element.104) | copy-start | bytes 1179652
  429.4 27.7 %copy-start.78 = (f32[768]{0:T(1024)S(1)}, f32[768]{0:T(1024)}, u32[]{:S(2)}) copy-start(f32[768]{0:T(1024)} %param.37) | copy-start | bytes 9220
  429.4 79.1 %all-reduce.13.cloned.1.call-start = ((), (), s32[]{:S(2)}) async-start(), calls=%async_computation.9 | async-start | bytes 6291456 | tf_op jit(solution)/shard_map/psum | solution.py:746
  459.9 18.1 %copy-start.38 = (f32[1024,1536]{1,0:T(8,128)}, f32[1024,1536]{1,0:T(8,128)S(1)}, u32[]{:S(2)}) copy-start(f32[1024,1536]{1,0:T(8,128)S(1)} %fusion.185) | copy-start | bytes 18874372
  483.9 312.9 %all-reduce.15.cloned.1.call-start = ((), (), s32[]{:S(2)}) async-start(), calls=%async_computation.17 | async-start | bytes 12582912 | tf_op jit(solution)/shard_map/psum | solution.py:740
  499.7 13.2 copy-start.39
  555.3 18.5 %copy-start.45 = (bf16[6,64,1024]{2,1,0:T(8,128)(2,1)}, bf16[6,64,1024]{2,1,0:T(8,128)(2,1)S(1)}, u32[]{:S(2)}) copy-start(bf16[6,64,1024]{2,1,0:T(8,128)(2,1)S(1)} %add_convert_fusion.2) | copy-start | bytes 2359300
  576.6 389.2 %reduce-scatter.16.cloned.1.call-start = ((), (), s32[]{:S(2)}) async-start(), calls=%async_computation.14 | async-start | bytes 1253376 | tf_op jit(solution)/shard_map/reduce_scatter | solution.py:828
  581.7 384.1 %reduce-scatter.14.cloned.1.call-start = ((), (), s32[]{:S(2)}) async-start(), calls=%async_computation.13 | async-start | bytes 1253376 | tf_op jit(solution)/shard_map/reduce_scatter | solution.py:827
  585.2 415.6 %reduce-scatter.12.cloned.1.call-start = ((), (), s32[]{:S(2)}) async-start(), calls=%async_computation.12 | async-start | bytes 1253376 | tf_op jit(solution)/shard_map/reduce_scatter | solution.py:826
  589.0 539.8 %reduce-scatter.10.cloned.1.call-start = ((), (), s32[]{:S(2)}) async-start(), calls=%async_computation.11 | async-start | bytes 1253376 | tf_op jit(solution)/shard_map/reduce_scatter | solution.py:825
  591.3 679.3 %reduce-scatter.18.cloned.1.call-start = ((), (), s32[]{:S(2)}) async-start(), calls=%async_computation.15 | async-start | bytes 5013504 | tf_op jit(solution)/shard_map/reduce_scatter | solution.py:830
  599.1 813.9 %reduce-scatter.20.cloned.1.call-start = ((), (), s32[]{:S(2)}) async-start(), calls=%async_computation.16 | async-start | bytes 5013504 | tf_op jit(solution)/shard_map/reduce_scatter | solution.py:831
  607.9 930.8 %reduce-scatter.8.cloned.1.call-start = ((), (), s32[]{:S(2)}) async-start(), calls=%async_computation.10 | async-start | bytes 417792 | tf_op jit(solution)/shard_map/reduce_scatter | solution.py:823
  666.2 12.7 copy-start.24
  666.2 12.7 copy-start.36
  737.4 13.0 copy-start.31
  737.4 26.4 %slice-start.6 = ((s8[8388608]{0:T(1024)(128)(4,1)}), s8[4194304]{0:T(1024)(128)(4,1)S(1)}, s32[]{:S(2)}) async-start(s8[8388608]{0:T(1024)(128)(4,1)} %bitcast.208), calls=%async_computation.24 | async-start | bytes 8388608
  750.4 13.5 copy-start.27
  750.4 13.5 slice-start.7
  893.0 68.5 %copy-start.47 = (f32[1024,768]{0,1:T(8,128)S(1)}, f32[1024,768]{0,1:T(8,128)}, u32[]{:S(2)}) copy-start(f32[1024,768]{0,1:T(8,128)} %get-tuple-element.87) | copy-start | bytes 9437188
  897.7 63.9 %copy-start.23 = (f32[1024,768]{0,1:T(8,128)S(1)}, f32[1024,768]{0,1:T(8,128)}, u32[]{:S(2)}) copy-start(f32[1024,768]{0,1:T(8,128)} %copy-done.22) | copy-start | bytes 9437188
  961.5 579.7 %copy-start.1 = (bf16[1536,768]{1,0:T(8,128)(2,1)S(1)}, bf16[1536,768]{1,0:T(8,128)(2,1)}, u32[]{:S(2)}) copy-start(bf16[1536,768]{1,0:T(8,128)(2,1)} %param.39) | copy-start | bytes 7077892
  (72 other events, 340.1 us)
Sparse Core Ops, SparseCore 0:
  75.8 18.8 all-reduce.8
  429.5 23.3 all-reduce.10
  484.0 24.3 all-reduce.12
  576.7 33.3 all-reduce.14
  615.2 124.9 reduce-scatter.15
  745.4 122.6 reduce-scatter.13
  873.4 127.2 reduce-scatter.11
  1006.1 122.5 reduce-scatter.9
  1134.5 136.0 reduce-scatter.17
  1277.0 135.9 reduce-scatter.19
  1418.2 120.3 reduce-scatter.7

commit v2 on v1

--- a/solution.py
+++ b/solution.py
@@ -10,7 +10,6 @@
 HDIM = 64
 NBUCKET = 32
 GROUPS = 32
-QBLK = 512
 
 
 bucket_edges = (12, 16, 23, 32, 46, 64, 91)
@@ -28,10 +27,6 @@
     return jnp.where(magnitude < 8, magnitude, coarse) + jnp.where(relative > 0, 16, 0).astype(
         jnp.int32
     )
-
-
-def bucket_table(bucket_ids):
-    return (bucket_ids[..., None] == jnp.arange(NBUCKET, dtype=jnp.int32)).astype(jnp.bfloat16)
 
 
 MESH = pl.DeviceIdType.MESH
@@ -290,10 +285,14 @@
     weights_ref,
     gain_ref,
     shift_ref,
+    split_ref,
+    small_ref,
     first_out,
     weights_out,
     gain_out,
     shift_out,
+    split_out,
+    small_out,
     natural,
     ordered,
     active,
@@ -313,8 +312,16 @@
     part_recv,
     share_send,
     share_recv,
+    split_slots,
+    split_half,
+    small_slots,
+    row_send,
+    row_recv,
 ):
     me = my_index()
+    row = lax.axis_index("dp")
+    core = lax.axis_index("tensor")
+    rows_count = count // 2
     greet_all(count)
     pixels = grad_ref.shape[0]
     rows = stem_rows(pixels)
@@ -326,6 +333,21 @@
     owned = parts.shape[1]
     for start, place in places:
         ordered[place : place + 8, :] = grad_ref[pl.ds(start, 8, stride=spacing), :]
+
+    def send_rows(first, last, source_of, target, place):
+        def send(step, carry):
+            other = lax.rem(row + step, rows_count)
+            pltpu.make_async_remote_copy(
+                src_ref=source_of(other),
+                dst_ref=target.at[row],
+                send_sem=row_send.at[place],
+                recv_sem=row_recv.at[place],
+                device_id=(other, core),
+                device_id_type=MESH,
+            ).start()
+            return carry
+
+        lax.fori_loop(first, last, send, 0)
 
     def weight_grad(layer):
         height = rows[layer]
@@ -399,6 +421,32 @@
         send_all(
             count, source.at[layer], slots.at[layer, me], send_sem.at[layer], recv_sem.at[layer]
         )
+        middle = (rows_count + 1) // 2
+        if layer == 7:
+            small_slots[row] = small_ref[...]
+            split_slots[row] = split_ref[row, core]
+            send_rows(1, rows_count, lambda other: small_ref, small_slots, 0)
+        if layer == 6:
+            send_rows(1, middle, lambda other: split_ref.at[other, core], split_slots, 1)
+        if layer == 5:
+            send_rows(middle, rows_count, lambda other: split_ref.at[other, core], split_slots, 1)
+        if layer == 3:
+            wait_all(rows_count, small_slots, row_recv.at[0])
+            small_out[...] = jnp.sum(small_slots[...], axis=0)
+            wait_all(rows_count, split_slots, row_recv.at[1])
+            split_half[core] = jnp.sum(split_slots[...], axis=0)
+            swap = pltpu.make_async_remote_copy(
+                src_ref=split_half.at[core],
+                dst_ref=split_half.at[core],
+                send_sem=row_send.at[2],
+                recv_sem=row_recv.at[2],
+                device_id=(row, 1 - core),
+                device_id_type=MESH,
+            )
+            swap.start()
+        if layer == 1:
+            swap.wait()
+            split_out[...] = split_half[...]
         if layer < 8:
             weight_grad(layer + 1)
         wait_all(count, slots.at[layer], recv_sem.at[layer])
@@ -490,6 +538,8 @@
     for layer in range(LAYERS):
         wait_all(count, slots.at[layer], send_sem.at[layer])
     wait_all(count, first_slots, send_sem.at[LAYERS])
+    wait_all(rows_count, small_slots, row_send.at[0])
+    wait_all(rows_count, split_slots, row_send.at[1])
     wait_all(count, parts, part_send)
     wait_all(count, shared, share_send)
 
@@ -528,7 +578,7 @@
 
 
 def stem_backward(
-    grad_map, page_image, records, conv_weights, group_gain, group_shift, devices
+    grad_map, page_image, records, conv_weights, group_gain, group_shift, split, small, devices
 ):
     planes, tile_rows, columns = page_image.shape
     pixels = tile_rows * columns
@@ -545,9 +595,11 @@
             jax.ShapeDtypeStruct((8, 128, 128), jnp.float32),
             jax.ShapeDtypeStruct((LAYERS, 128), jnp.float32),
             jax.ShapeDtypeStruct((LAYERS, 128), jnp.float32),
+            jax.ShapeDtypeStruct(split.shape[1:], jnp.float32),
+            jax.ShapeDtypeStruct(small.shape, jnp.float32),
         ),
-        in_specs=[whole] * 8,
-        out_specs=(whole,) * 4,
+        in_specs=[whole] * 10,
+        out_specs=(whole,) * 6,
         scratch_shapes=[
             pltpu.VMEM((pixels, 128), jnp.float32),
             pltpu.VMEM((pixels, 128), jnp.float32),
@@ -568,12 +620,19 @@
             pltpu.SemaphoreType.DMA,
             pltpu.SemaphoreType.DMA,
             pltpu.SemaphoreType.DMA,
+            pltpu.VMEM((devices // 2, *split.shape[2:]), jnp.float32),
+            pltpu.VMEM(split.shape[1:], jnp.float32),
+            pltpu.VMEM((devices // 2, *small.shape), jnp.float32),
+            pltpu.SemaphoreType.DMA((3,)),
+            pltpu.SemaphoreType.DMA((3,)),
         ],
         compiler_params=pltpu.CompilerParams(
             collective_id=1, has_side_effects=True, vmem_limit_bytes=40 * 2**20
         ),
         name="stem_backward",
-    )(grad_map, image, norms, inputs, scales, conv_weights, group_gain, group_shift)
+    )(
+        grad_map, image, norms, inputs, scales, conv_weights, group_gain, group_shift, split, small
+    )
 
 
 def rms_forward(values, gains):
@@ -593,53 +652,431 @@
     return jax.nn.gelu(values, approximate=False)
 
 
-def block_terms(start, segment, padding, left_edge, top_edge):
-    positions = jnp.arange(segment.shape[0], dtype=jnp.int32)
-    query_pos = positions[start : start + QBLK]
-    relative = positions[None, :] - query_pos[:, None]
-    rel_bucket = bucket_of(relative)
-    left_bucket = bucket_of(left_edge[None, :] - left_edge[start : start + QBLK, None])
-    top_bucket = bucket_of(top_edge[None, :] - top_edge[start : start + QBLK, None])
-    allowed = (segment[None, :] == segment[start : start + QBLK, None]) & (
-        (padding[None, :] > 0) | (relative == 0)
-    )
-    return ((rel_bucket, left_bucket, top_bucket), allowed)
-
-
-def block_scores(query_block, key_heads, bias_tables, buckets, allowed):
-    bias = jnp.einsum(
-        "qkb,bh->hqk",
-        bucket_table(buckets[0]),
-        bias_tables[0],
-        preferred_element_type=jnp.float32,
-        precision=highest,
-    )
-    bias = bias + jnp.einsum(
-        "qkb,bh->hqk",
-        bucket_table(buckets[1]),
-        bias_tables[1],
-        preferred_element_type=jnp.float32,
-        precision=highest,
-    )
-    bias = bias + jnp.einsum(
-        "qkb,bh->hqk",
-        bucket_table(buckets[2]),
-        bias_tables[2],
-        preferred_element_type=jnp.float32,
-        precision=highest,
-    )
-    scores = (
-        jnp.einsum("qhd,khd->hqk", query_block, key_heads, preferred_element_type=jnp.float32)
-        * HDIM ** (-0.5)
-        + bias
-    )
-    return jnp.where(allowed[None], scores, masked_score)
-
-
-def bucket_sums(grad_upper, grad_lower, bucket_ids):
-    table = bucket_table(bucket_ids)
-    upper = jnp.einsum("hqk,qkb->bh", grad_upper, table, preferred_element_type=jnp.float32)
-    return upper + jnp.einsum("hqk,qkb->bh", grad_lower, table, preferred_element_type=jnp.float32)
+TILE = 128
+QROWS = 256
+KIND_ROWS = 8
+FAR_LANE = 32
+LOW_LANE = 40
+PAD_LANE = 48
+DOC_LANE = 56
+
+
+def dot_last(left, right):
+    return lax.dot_general(
+        left, right, (((1,), (1,)), ((), ())), preferred_element_type=jnp.float32
+    )
+
+
+def dot_plain(left, right):
+    return jnp.dot(left, right, preferred_element_type=jnp.float32)
+
+
+def bucket_vector(tables_ref, table, head, relative):
+    buckets = bucket_of(relative)
+    values = jnp.zeros(relative.shape, jnp.float32)
+    for bucket in range(NBUCKET):
+        values = jnp.where(buckets == bucket, tables_ref[table, bucket, head], values)
+    return values
+
+
+def signed_lanes(width):
+    lane = lax.broadcasted_iota(jnp.int32, (8, width), 1)
+    return jnp.where(lane < width // 2, lane, lane - width)
+
+
+def rolled(row, height):
+    return pltpu.roll(
+        jnp.broadcast_to(row[0:1], (height, row.shape[1])), 0, 1, stride=1, stride_axis=0
+    )
+
+
+def token_lanes(info_ref, one_hot_x, query_base, key_base, pad_tiles):
+    tokens = info_ref.shape[0]
+    lane = lax.broadcasted_iota(jnp.int32, (TILE, 128), 1)
+    row = lax.broadcasted_iota(jnp.int32, (TILE, 128), 0)
+    for tile in range(tokens // TILE):
+        at = slice(tile * TILE, (tile + 1) * TILE)
+        left = info_ref[at, 0:1]
+        top = info_ref[at, 1:2]
+        doc = info_ref[at, 2:3]
+        hidden = jnp.where(info_ref[at, 3:4] > 0, 0.0, masked_score)
+        one_hot_x[at, :] = (lane == left).astype(jnp.float32).astype(jnp.bfloat16)
+        shared = jnp.where((lane == top) | (lane == DOC_LANE + doc), 1.0, 0.0)
+        query_base[at, :] = jnp.where(lane == FAR_LANE + tile, 1.0, shared).astype(jnp.bfloat16)
+        key = jnp.where((lane == FAR_LANE + tile) | (lane == LOW_LANE + tile), 1.0, shared)
+        key = jnp.where(lane == PAD_LANE + tile, hidden, key)
+        key_base[1, at, :] = key.astype(jnp.bfloat16)
+        key_base[0, at, :] = pltpu.roll(key, 64, 1).astype(jnp.bfloat16)
+        pad_tiles[at, :] = jnp.where(lane == row, 0.0, jnp.broadcast_to(hidden, (TILE, 128)))
+
+
+def head_matrices(tables_ref, head, side):
+    first = bucket_vector(tables_ref, 1, head, signed_lanes(256))
+    across = rolled(first, 128)[:, :128].astype(jnp.bfloat16)
+    second = rolled(bucket_vector(tables_ref, 2, head, signed_lanes(128)), 128)
+    row = lax.broadcasted_iota(jnp.int32, (128, 128), 0)
+    lane = lax.broadcasted_iota(jnp.int32, (128, 128), 1)
+    mixed = jnp.where((row < FAR_LANE) & (lane < FAR_LANE), second, 0.0)
+    gap = lane % 8 - (row - FAR_LANE)
+    before = jnp.full((128, 128), tables_ref[0, NBUCKET // 2 - 1, head], jnp.float32)
+    after = jnp.full((128, 128), tables_ref[0, NBUCKET - 1, head], jnp.float32)
+    far = jnp.where(gap <= -2, before, jnp.where(gap >= 2, after, 0.0))
+    high = far.astype(jnp.bfloat16).astype(jnp.float32)
+    of_tile = (row >= FAR_LANE) & (row < LOW_LANE)
+    mixed = jnp.where(of_tile & (lane >= FAR_LANE) & (lane < LOW_LANE), high, mixed)
+    mixed = jnp.where(of_tile & (lane >= LOW_LANE) & (lane < PAD_LANE), far - high, mixed)
+    mixed = jnp.where(
+        of_tile & (lane >= PAD_LANE) & (lane < DOC_LANE) & (gap != 0), 1.0, mixed
+    )
+    docs = (row >= DOC_LANE) & (row < 64) & (lane >= DOC_LANE) & (lane < 64)
+    mixed = jnp.where(docs & (row != lane), masked_score, mixed)
+    if side == 0:
+        mixed = pltpu.roll(mixed, 64, 1)
+    near = rolled(bucket_vector(tables_ref, 0, head, -signed_lanes(512)), 128)
+    tiles = {0: near[:, :128], 1: near[:, 384:], -1: near[:, 128:256]}
+    return across, mixed.astype(jnp.bfloat16), tiles
+
+
+def own_half(side, own, other):
+    lane = lax.broadcasted_iota(jnp.int32, own.shape, 1)
+    return jnp.where((lane < 64) if side == 0 else (lane >= 64), own, other)
+
+
+def widen_operands(
+    side, head, tables_ref, query_ref, key_ref, one_hot_x, query_base, key_base, query_wide, key_wide, near
+):
+    across, mixed, tiles = head_matrices(tables_ref, head, side)
+    for gap in (-1, 0, 1):
+        near[side, gap + 1] = tiles[gap]
+    scaled = (query_ref[...].astype(jnp.float32) * HDIM ** (-0.5)).astype(jnp.bfloat16)
+    query_wide[side, :, :128] = own_half(
+        side, scaled, dot_plain(query_base[...], mixed).astype(jnp.bfloat16)
+    )
+    query_wide[side, :, 128:] = dot_plain(one_hot_x[...], across).astype(jnp.bfloat16)
+    key_wide[side, :, :128] = own_half(side, key_ref[...], key_base[side])
+    key_wide[side, :, 128:] = one_hot_x[...]
+
+
+def near_scores(scores, side, block, tile, near, pad_tiles):
+    halves = []
+    for half in range(QROWS // TILE):
+        part = scores[:, half * TILE : (half + 1) * TILE]
+        gap = tile - (block * (QROWS // TILE) + half)
+        if abs(gap) <= 1:
+            part = part + near[side, gap + 1]
+        if gap == 0:
+            part = part + pad_tiles[tile * TILE : (tile + 1) * TILE, :]
+        halves.append(part)
+    return jnp.concatenate(halves, axis=1)
+
+
+def attention_forward_kernel(
+    tables_ref,
+    info_ref,
+    query_ref,
+    key_ref,
+    value_ref,
+    context_ref,
+    exact_ref,
+    lse_ref,
+    one_hot_x,
+    query_base,
+    key_base,
+    pad_tiles,
+    query_wide,
+    key_wide,
+    near,
+    scores,
+    weights,
+):
+    pair = pl.program_id(0)
+    tokens = query_ref.shape[0]
+
+    @pl.when(pair == 0)
+    def _():
+        token_lanes(info_ref, one_hot_x, query_base, key_base, pad_tiles)
+
+    for side in range(2):
+        widen_operands(
+            side, pair * 2 + side, tables_ref, query_ref, key_ref, one_hot_x, query_base, key_base,
+            query_wide, key_wide, near,
+        )
+    values = value_ref[...].T
+    for block in range(tokens // QROWS):
+        columns = slice(block * QROWS, (block + 1) * QROWS)
+        contexts = []
+        for side in range(2):
+            scores[side] = dot_last(key_wide[side], query_wide[side, columns, :])
+            top = jnp.full((8, QROWS), masked_score, jnp.float32)
+            for tile in range(tokens // TILE):
+                at = slice(tile * TILE, (tile + 1) * TILE)
+                part = scores[side, at, :]
+                if any(abs(tile - 2 * block - half) <= 1 for half in range(2)):
+                    part = near_scores(part, side, block, tile, near, pad_tiles)
+                    scores[side, at, :] = part
+                top = jnp.maximum(top, jnp.max(part.reshape(TILE // 8, 8, QROWS), axis=0))
+            top = jnp.max(top, axis=0, keepdims=True)
+            total = jnp.zeros((8, QROWS), jnp.float32)
+            for tile in range(tokens // TILE):
+                at = slice(tile * TILE, (tile + 1) * TILE)
+                part = jnp.exp(scores[side, at, :] - top)
+                total = total + jnp.sum(part.reshape(TILE // 8, 8, QROWS), axis=0)
+                weights[side, at, :] = part.astype(jnp.bfloat16)
+            total = jnp.sum(total, axis=0, keepdims=True)
+            context = dot_plain(values[side * 64 : (side + 1) * 64, :], weights[side])
+            contexts.append(context * (1.0 / total))
+            lse_ref[0, side : side + 1, columns] = top + jnp.log(total)
+        context = jnp.concatenate(contexts, axis=0)
+        exact_ref[:, columns] = context
+        context_ref[columns, :] = context.T.astype(jnp.bfloat16)
+
+
+def attention_backward_kernel(
+    tables_ref,
+    info_ref,
+    query_ref,
+    key_ref,
+    value_ref,
+    grad_ref,
+    exact_ref,
+    lse_ref,
+    grad_query_ref,
+    grad_key_ref,
+    grad_value_ref,
+    diagonal_ref,
+    one_hot_x,
+    query_base,
+    key_base,
+    pad_tiles,
+    reverse,
+    query_wide,
+    key_wide,
+    near,
+    scores,
+    grad_probs,
+    probs_low,
+    grad_low,
+    key_turned,
+    grad_near,
+    grad_blocks,
+    grad_key,
+    grad_value,
+):
+    pair = pl.program_id(0)
+    tokens = query_ref.shape[0]
+
+    @pl.when(pair == 0)
+    def _():
+        token_lanes(info_ref, one_hot_x, query_base, key_base, pad_tiles)
+        lane = lax.broadcasted_iota(jnp.int32, (TILE, 128), 1)
+        for tile in range(tokens // TILE):
+            at = slice(tile * TILE, (tile + 1) * TILE)
+            left = info_ref[at, 0:1]
+            top = info_ref[at, 1:2]
+            reverse[at, :128] = jnp.where(lane == 127 - left, 1.0, 0.0).astype(jnp.bfloat16)
+            reverse[at, 128:] = jnp.where(
+                (lane == 31 - top) | (lane == FAR_LANE + tile), 1.0, 0.0
+            ).astype(jnp.bfloat16)
+
+    for side in range(2):
+        widen_operands(
+            side, pair * 2 + side, tables_ref, query_ref, key_ref, one_hot_x, query_base, key_base,
+            query_wide, key_wide, near,
+        )
+        key_turned[side] = key_wide[side].T
+    grad_near[...] = jnp.zeros_like(grad_near)
+    grad_blocks[...] = jnp.zeros_like(grad_blocks)
+    values = [
+        own_half(side, value_ref[...], jnp.zeros(value_ref.shape, jnp.bfloat16)) for side in range(2)
+    ]
+    for block in range(tokens // QROWS):
+        columns = slice(block * QROWS, (block + 1) * QROWS)
+        grad_block = grad_ref[columns, :]
+        product = grad_block.astype(jnp.float32).T * exact_ref[:, columns]
+        scaled = (query_ref[columns, :].astype(jnp.float32) * HDIM ** (-0.5)).astype(jnp.bfloat16)
+        turned = []
+        key_terms = []
+        value_terms = []
+        for side in range(2):
+            delta = jnp.sum(product[side * 64 : (side + 1) * 64, :], axis=0, keepdims=True)
+            lse = lse_ref[0, side : side + 1, columns]
+            scores[side] = dot_last(key_wide[side], query_wide[side, columns, :])
+            grad_probs[side] = dot_last(values[side], grad_block)
+            for tile in range(tokens // TILE):
+                at = slice(tile * TILE, (tile + 1) * TILE)
+                part = near_scores(scores[side, at, :], side, block, tile, near, pad_tiles)
+                probs = jnp.exp(part - lse)
+                grad_part = probs * (grad_probs[side, at, :] - delta)
+                probs_low[side, at, :] = probs.astype(jnp.bfloat16)
+                grad_low[side, at, :] = grad_part.astype(jnp.bfloat16)
+                for half in range(QROWS // TILE):
+                    gap = tile - (block * (QROWS // TILE) + half)
+                    if abs(gap) <= 1:
+                        grad_near[side, gap + 1] += grad_part[:, half * TILE : (half + 1) * TILE]
+            value_terms.append(dot_plain(probs_low[side], grad_block))
+            key_terms.append(dot_plain(grad_low[side], scaled))
+            sums = dot_plain(key_turned[side], grad_low[side])
+            turned.append(sums[side * 64 : (side + 1) * 64, :])
+            grad_blocks[side] += dot_plain(sums.astype(jnp.bfloat16), reverse[columns, :])
+        grad_query_ref[columns, :] = (
+            (jnp.concatenate(turned, axis=0) * HDIM ** (-0.5)).T.astype(jnp.bfloat16)
+        )
+        key_term = own_half(0, key_terms[0], key_terms[1])
+        value_term = own_half(0, value_terms[0], value_terms[1])
+        if block == 0:
+            grad_key[...] = key_term
+            grad_value[...] = value_term
+        else:
+            grad_key[...] += key_term
+            grad_value[...] += value_term
+    grad_key_ref[...] = grad_key[...].astype(jnp.bfloat16)
+    grad_value_ref[...] = grad_value[...].astype(jnp.bfloat16)
+    row = lax.broadcasted_iota(jnp.int32, (128, 128), 0)
+    lane = lax.broadcasted_iota(jnp.int32, (128, 128), 1)
+    flip = jnp.where(row + lane == 127, 1.0, 0.0).astype(jnp.bfloat16)
+    blank = jnp.zeros((128, 128), jnp.float32)
+
+    def diagonal_sums(values):
+        spread = jnp.concatenate([values, blank], axis=1)
+        return jnp.sum(
+            pltpu.roll(spread, 0, 1, stride=1, stride_axis=0), axis=0, keepdims=True
+        )
+
+    for side in range(2):
+        misc = 64 * (1 - side)
+        sums = [diagonal_sums(grad_blocks[side, 128:, :128])]
+        below = grad_blocks[side, misc : misc + 64, 128:]
+        small_row = lax.broadcasted_iota(jnp.int32, (64, 128), 0)
+        small_lane = lax.broadcasted_iota(jnp.int32, (64, 128), 1)
+        upright = jnp.where((small_row < FAR_LANE) & (small_lane < FAR_LANE), below, 0.0)
+        sums.append(diagonal_sums(jnp.concatenate([upright, jnp.zeros((64, 128), jnp.float32)], axis=0)))
+        for gap in range(3):
+            tile = grad_near[side, gap]
+            high = tile.astype(jnp.bfloat16)
+            rest = (tile - high.astype(jnp.float32)).astype(jnp.bfloat16)
+            sums.append(diagonal_sums(dot_plain(high, flip) + dot_plain(rest, flip)))
+        gap = (small_row - FAR_LANE) - (small_lane - FAR_LANE)
+        inside = (
+            (small_row >= FAR_LANE)
+            & (small_row < LOW_LANE)
+            & (small_lane >= FAR_LANE)
+            & (small_lane < LOW_LANE)
+        )
+        for chosen in (gap <= -2, gap >= 2):
+            far = jnp.sum(jnp.where(inside & chosen, below, 0.0), axis=0, keepdims=True)
+            sums.append(jnp.concatenate([far, blank[0:1]], axis=1))
+        sums.append(jnp.zeros((1, 256), jnp.float32))
+        diagonal_ref[side] = jnp.concatenate(sums, axis=0)
+
+
+def attention_scratch(tokens):
+    return [
+        pltpu.VMEM((tokens, 128), jnp.bfloat16),
+        pltpu.VMEM((tokens, 128), jnp.bfloat16),
+        pltpu.VMEM((2, tokens, 128), jnp.bfloat16),
+        pltpu.VMEM((tokens, 128), jnp.float32),
+    ], [
+        pltpu.VMEM((2, tokens, 256), jnp.bfloat16),
+        pltpu.VMEM((2, tokens, 256), jnp.bfloat16),
+        pltpu.VMEM((2, 3, TILE, TILE), jnp.float32),
+        pltpu.VMEM((2, tokens, QROWS), jnp.float32),
+    ]
+
+
+def attention_forward(tables, info, query, key, value):
+    tokens, width = query.shape
+    pairs = width // 128
+    own = pl.BlockSpec((tokens, 128), lambda pair: (0, pair))
+    fixed, moving = attention_scratch(tokens)
+    return pl.pallas_call(
+        attention_forward_kernel,
+        grid=(pairs,),
+        out_shape=(
+            jax.ShapeDtypeStruct((tokens, width), jnp.bfloat16),
+            jax.ShapeDtypeStruct((width, tokens), jnp.float32),
+            jax.ShapeDtypeStruct((pairs, 2, tokens), jnp.float32),
+        ),
+        in_specs=[
+            pl.BlockSpec(memory_space=pltpu.SMEM),
+            pl.BlockSpec((tokens, 8), lambda pair: (0, 0)),
+            own,
+            own,
+            own,
+        ],
+        out_specs=(
+            own,
+            pl.BlockSpec((128, tokens), lambda pair: (pair, 0)),
+            pl.BlockSpec((1, 2, tokens), lambda pair: (pair, 0, 0)),
+        ),
+        scratch_shapes=fixed
+        + moving
+        + [
+            pltpu.VMEM((2, tokens, QROWS), jnp.bfloat16),
+        ],
+        compiler_params=pltpu.CompilerParams(
+            dimension_semantics=("arbitrary",), vmem_limit_bytes=48 * 2**20
+        ),
+        name="attention_forward",
+    )(tables, info, query, key, value)
+
+
+def attention_backward(tables, info, query, key, value, grad_context, exact, lse):
+    tokens, width = query.shape
+    pairs = width // 128
+    own = pl.BlockSpec((tokens, 128), lambda pair: (0, pair))
+    fixed, moving = attention_scratch(tokens)
+    low = jax.ShapeDtypeStruct((tokens, width), jnp.bfloat16)
+    return pl.pallas_call(
+        attention_backward_kernel,
+        grid=(pairs,),
+        out_shape=(low, low, low, jax.ShapeDtypeStruct((2 * pairs, 8, 256), jnp.float32)),
+        in_specs=[
+            pl.BlockSpec(memory_space=pltpu.SMEM),
+            pl.BlockSpec((tokens, 8), lambda pair: (0, 0)),
+            own,
+            own,
+            own,
+            own,
+            pl.BlockSpec((128, tokens), lambda pair: (pair, 0)),
+            pl.BlockSpec((1, 2, tokens), lambda pair: (pair, 0, 0)),
+        ],
+        out_specs=(own, own, own, pl.BlockSpec((2, 8, 256), lambda pair: (pair, 0, 0))),
+        scratch_shapes=fixed
+        + [pltpu.VMEM((tokens, 256), jnp.bfloat16)]
+        + moving
+        + [
+            pltpu.VMEM((2, tokens, QROWS), jnp.float32),
+            pltpu.VMEM((2, tokens, QROWS), jnp.bfloat16),
+            pltpu.VMEM((2, tokens, QROWS), jnp.bfloat16),
+            pltpu.VMEM((2, 256, tokens), jnp.bfloat16),
+            pltpu.VMEM((2, 3, TILE, TILE), jnp.float32),
+            pltpu.VMEM((2, 256, 256), jnp.float32),
+            pltpu.VMEM((tokens, 128), jnp.float32),
+            pltpu.VMEM((tokens, 128), jnp.float32),
+        ],
+        compiler_params=pltpu.CompilerParams(
+            dimension_semantics=("arbitrary",), vmem_limit_bytes=48 * 2**20
+        ),
+        name="attention_backward",
+    )(tables, info, query, key, value, grad_context, exact, lse)
+
+
+def bucket_grads(diagonals):
+    lane = jnp.arange(256, dtype=jnp.int32)
+    wide_buckets = [
+        bucket_of(lane - 127),
+        bucket_of(lane - 31),
+        bucket_of(lane - 127 - TILE),
+        bucket_of(lane - 127),
+        bucket_of(lane - 127 + TILE),
+        jnp.full((256,), NBUCKET // 2 - 1, jnp.int32),
+        jnp.full((256,), NBUCKET - 1, jnp.int32),
+    ]
+    table_of = (1, 2, 0, 0, 0, 0, 0)
+    slots = jnp.stack([bucket + NBUCKET * table for bucket, table in zip(wide_buckets, table_of)])
+    chosen = (slots[..., None] == jnp.arange(3 * NBUCKET, dtype=jnp.int32)).astype(jnp.float32)
+    sums = jnp.einsum("hrc,rcb->bh", diagonals[:, :7], chosen, precision=highest)
+    return sums.reshape(3, NBUCKET, -1)
 
 
 def on_device(
@@ -693,44 +1130,14 @@
         pooled, roi_proj, preferred_element_type=jnp.float32
     )
     attn_in, attn_hat, attn_inv = rms_forward(stream, attn_norm)
-    tokens = stream.shape[0]
-    local_heads = query_proj.shape[1] // HDIM
-    query_heads = (
-        jnp.dot(attn_in, query_proj, preferred_element_type=jnp.float32)
-        .astype(jnp.bfloat16)
-        .reshape(tokens, local_heads, HDIM)
-    )
-    key_heads = (
-        jnp.dot(attn_in, key_proj, preferred_element_type=jnp.float32)
-        .astype(jnp.bfloat16)
-        .reshape(tokens, local_heads, HDIM)
-    )
-    value_heads = (
-        jnp.dot(attn_in, value_proj, preferred_element_type=jnp.float32)
-        .astype(jnp.bfloat16)
-        .reshape(tokens, local_heads, HDIM)
-    )
-    segment = doc_ids[0]
-    padding = pad_mask[0]
-    scale = HDIM ** (-0.5)
-    log_sums = []
-    contexts = []
-    for start in range(0, tokens, QBLK):
-        buckets, allowed = block_terms(start, segment, padding, left_edge, top_edge)
-        masked = block_scores(
-            query_heads[start : start + QBLK], key_heads, bias_tables, buckets, allowed
-        )
-        top_score = jnp.max(masked, axis=-1, keepdims=True)
-        weights = jnp.exp(masked - top_score)
-        totals = jnp.sum(weights, axis=-1, keepdims=True)
-        log_sums.append(top_score + jnp.log(totals))
-        probs = (weights / totals).astype(jnp.bfloat16)
-        contexts.append(
-            jnp.einsum(
-                "hqk,khd->qhd", probs, value_heads, preferred_element_type=jnp.float32
-            ).astype(jnp.bfloat16)
-        )
-    context = jnp.concatenate(contexts, axis=0).reshape(tokens, -1)
+    query = jnp.dot(attn_in, query_proj, preferred_element_type=jnp.float32).astype(jnp.bfloat16)
+    key = jnp.dot(attn_in, key_proj, preferred_element_type=jnp.float32).astype(jnp.bfloat16)
+    value = jnp.dot(attn_in, value_proj, preferred_element_type=jnp.float32).astype(jnp.bfloat16)
+    blank = jnp.zeros_like(left_edge)
+    info = jnp.stack(
+        [left_edge, top_edge, doc_ids[0], pad_mask[0], blank, blank, blank, blank], axis=1
+    )
+    context, exact, lse = attention_forward(bias_tables, info, query, key, value)
     attn_out = lax.psum(jnp.dot(context, output_proj, preferred_element_type=jnp.float32), "tensor")
     middle = stream + attn_out
     ffn_in, ffn_hat, ffn_inv = rms_forward(middle, ffn_norm)
@@ -739,7 +1146,7 @@
     hidden = activated.astype(jnp.bfloat16)
     ffn_out = lax.psum(jnp.dot(hidden, down_proj, preferred_element_type=jnp.float32), "tensor")
     layer_out = (middle + ffn_out).astype(jnp.bfloat16)
-    grad_down = jnp.dot(hidden.T, cotangent, preferred_element_type=jnp.float32)
+    grad_down = jnp.dot(cotangent.T, hidden, preferred_element_type=jnp.float32)
     grad_hidden = jnp.dot(cotangent, down_proj.T, preferred_element_type=jnp.float32)
     grad_pre = gelu_pullback(grad_hidden)[0].astype(jnp.bfloat16)
     grad_up = jnp.dot(ffn_in.T, grad_pre, preferred_element_type=jnp.float32)
@@ -749,58 +1156,13 @@
     grad_mid_norm, grad_ffn_norm = rms_backward(grad_ffn_in, ffn_hat, ffn_inv, ffn_norm)
     grad_middle = cotangent.astype(jnp.float32) + grad_mid_norm
     grad_mid_low = grad_middle.astype(jnp.bfloat16)
-    grad_output = jnp.dot(context.T, grad_mid_low, preferred_element_type=jnp.float32)
-    grad_context = (
-        jnp.dot(grad_mid_low, output_proj.T, preferred_element_type=jnp.float32)
-        .astype(jnp.bfloat16)
-        .reshape(tokens, local_heads, HDIM)
-    )
-    grad_value = jnp.zeros((tokens, local_heads, HDIM), jnp.float32)
-    grad_key = jnp.zeros((tokens, local_heads, HDIM), jnp.float32)
-    grad_tables = jnp.zeros((3, NBUCKET, local_heads), jnp.float32)
-    grad_queries = []
-    for index, start in enumerate(range(0, tokens, QBLK)):
-        buckets, allowed = block_terms(start, segment, padding, left_edge, top_edge)
-        masked = block_scores(
-            query_heads[start : start + QBLK], key_heads, bias_tables, buckets, allowed
-        )
-        probs_full = jnp.exp(masked - log_sums[index])
-        probs = probs_full.astype(jnp.bfloat16)
-        grad_ctx_block = grad_context[start : start + QBLK]
-        grad_value = grad_value + jnp.einsum(
-            "hqk,qhd->khd", probs, grad_ctx_block, preferred_element_type=jnp.float32
-        )
-        grad_probs = jnp.einsum(
-            "qhd,khd->hqk", grad_ctx_block, value_heads, preferred_element_type=jnp.float32
-        )
-        delta = jnp.sum(grad_probs * probs_full, axis=-1, keepdims=True)
-        grad_full = probs_full * (grad_probs - delta)
-        grad_scores = grad_full.astype(jnp.bfloat16)
-        grad_lower = (grad_full - grad_scores.astype(jnp.float32)).astype(jnp.bfloat16)
-        table_terms = jnp.stack(
-            [bucket_sums(grad_scores, grad_lower, bucket_ids) for bucket_ids in buckets]
-        )
-        grad_tables = grad_tables + table_terms
-        grad_queries.append(
-            jnp.einsum("hqk,khd->qhd", grad_scores, key_heads, preferred_element_type=jnp.float32)
-            * scale
-        )
-        grad_key = (
-            grad_key
-            + jnp.einsum(
-                "hqk,qhd->khd",
-                grad_scores,
-                query_heads[start : start + QBLK],
-                preferred_element_type=jnp.float32,
-            )
-            * scale
-        )
-    grad_query_low = jnp.concatenate(grad_queries, axis=0).reshape(tokens, -1).astype(jnp.bfloat16)
-    grad_key_low = grad_key.reshape(tokens, -1).astype(jnp.bfloat16)
-    grad_value_low = grad_value.reshape(tokens, -1).astype(jnp.bfloat16)
-    grad_query_proj = jnp.dot(attn_in.T, grad_query_low, preferred_element_type=jnp.float32)
-    grad_key_proj = jnp.dot(attn_in.T, grad_key_low, preferred_element_type=jnp.float32)
-    grad_value_proj = jnp.dot(attn_in.T, grad_value_low, preferred_element_type=jnp.float32)
+    grad_context = jnp.dot(
+        grad_mid_low, output_proj.T, preferred_element_type=jnp.float32
+    ).astype(jnp.bfloat16)
+    grad_query_low, grad_key_low, grad_value_low, diagonals = attention_backward(
+        bias_tables, info, query, key, value, grad_context, exact, lse
+    )
+    grad_tables = bucket_grads(diagonals)
     attn_terms = jnp.dot(grad_query_low, query_proj.T, preferred_element_type=jnp.float32)
     attn_terms = attn_terms + jnp.dot(grad_key_low, key_proj.T, preferred_element_type=jnp.float32)
     attn_terms = attn_terms + jnp.dot(
@@ -810,45 +1172,66 @@
     grad_stream_norm, grad_attn_norm = rms_backward(grad_attn_in, attn_hat, attn_inv, attn_norm)
     grad_stream = grad_middle + grad_stream_norm
     grad_low = grad_stream.astype(jnp.bfloat16)
-    grad_roi = jnp.dot(pooled.T, grad_low, preferred_element_type=jnp.float32)
+    grad_roi = jnp.dot(grad_low.T, pooled, preferred_element_type=jnp.float32)
     grad_pooled = jnp.dot(grad_low, roi_proj.T, preferred_element_type=jnp.float32)
     grad_box = grad_pooled / box_area[:, None]
     map_pair = jnp.dot(box_mask.T, split_two(grad_box), preferred_element_type=jnp.float32)
     grad_map = map_pair[:, :128] + map_pair[:, 128:]
-    stem_totals = stem_backward(
-        grad_map, page_image, records, conv_weights, group_gain, group_shift, devices
-    )
-    table_totals = lax.psum(grad_tables, "dp")
-    weight_parts = (
-        lax.psum_scatter(grad_roi, "dp", scatter_dimension=1, tiled=True),
-        lax.psum_scatter(grad_attn_norm, "dp", scatter_dimension=0, tiled=True),
-        lax.psum_scatter(grad_query_proj, "dp", scatter_dimension=0, tiled=True),
-        lax.psum_scatter(grad_key_proj, "dp", scatter_dimension=0, tiled=True),
-        lax.psum_scatter(grad_value_proj, "dp", scatter_dimension=0, tiled=True),
-        lax.psum_scatter(grad_output, "dp", scatter_dimension=1, tiled=True),
-        lax.psum_scatter(grad_ffn_norm, "dp", scatter_dimension=0, tiled=True),
-        lax.psum_scatter(grad_up, "dp", scatter_dimension=0, tiled=True),
-        lax.psum_scatter(grad_down, "dp", scatter_dimension=1, tiled=True),
-    )
-    block_parts = weight_parts[:6]
-    ffn_parts = weight_parts[6:]
+    grad_attn = jnp.concatenate(
+        [
+            jnp.dot(
+                attn_in.T,
+                jnp.concatenate([grad_query_low, grad_key_low, grad_value_low], axis=1),
+                preferred_element_type=jnp.float32,
+            ),
+            jnp.dot(grad_mid_low.T, context, preferred_element_type=jnp.float32),
+        ],
+        axis=1,
+    )
+    rows_count = lax.axis_size("dp")
+    width = grad_attn_norm.shape[0]
+    own_rows = width // rows_count
+    heads = grad_tables.shape[2]
+    small = jnp.concatenate([grad_attn_norm, grad_ffn_norm, grad_tables.reshape(-1)])
+    small = jnp.pad(small, (0, -small.shape[0] % 1024)).reshape(-1, 128)
+    split = grad_roi.reshape(rows_count, 2, own_rows // 2, grad_roi.shape[1])
+    grad_first, grad_convs, grad_gains, grad_offsets, own_roi, small = stem_backward(
+        grad_map,
+        page_image,
+        records,
+        conv_weights,
+        group_gain,
+        group_shift,
+        split,
+        small,
+        devices,
+    )
+    small = small.reshape(-1)
+    start = lax.axis_index("dp") * own_rows
+    own_attn_norm = lax.dynamic_slice(small, (start,), (own_rows,))
+    own_ffn_norm = lax.dynamic_slice(small, (width + start,), (own_rows,))
+    own_tables = small[2 * width : 2 * width + grad_tables.size].reshape(3, NBUCKET, heads)
+    own_up = lax.psum_scatter(grad_up, "dp", scatter_dimension=0, tiled=True)
+    own_down = lax.psum_scatter(grad_down, "dp", scatter_dimension=0, tiled=True).T
+    own_attn = lax.psum_scatter(grad_attn, "dp", scatter_dimension=0, tiled=True)
+    part = query_proj.shape[1]
     return (
         layer_out,
         grad_stream,
-        stem_totals[0],
-        stem_totals[1],
-        stem_totals[2],
-        stem_totals[3],
-        block_parts[0],
-        block_parts[1],
-        block_parts[2],
-        block_parts[3],
-        block_parts[4],
-        block_parts[5],
-        table_totals,
-        ffn_parts[0],
-        ffn_parts[1],
-        ffn_parts[2],
+        grad_first,
+        grad_convs,
+        grad_gains,
+        grad_offsets,
+        own_roi.reshape(own_rows, -1).T,
+        own_attn_norm,
+        own_attn[:, :part],
+        own_attn[:, part : 2 * part],
+        own_attn[:, 2 * part : 3 * part],
+        own_attn[:, 3 * part :].T,
+        own_tables,
+        own_ffn_norm,
+        own_up,
+        own_down,
     )
 
 

time: 1560 us -> 746 us (0.48)
  matrix products: 438 us -> 66.1 us
  waiting for transfers between devices: 605 us -> 387 us
  local copies, waits for them, and re-layouts: 198 us -> 49.6 us
  blocking collectives: 77.1 us -> 0 us
  Pallas kernels: 116 us -> 185 us
  other arithmetic: 96.3 us -> 35.6 us
    reduce_scatter x7 -> x2, waiting for transfers between devices: 573 us -> 197 us  [the longest x1 142 us: on_device(): own_up = lax.psum_scatter(grad_up, 'dp', scatter_dimension=0, tiled=True)]
    dot_general x36 -> x5, matrix products: 379 us -> 12.3 us  [the longest x1 6.05 us: on_device(): grad_down = jnp.dot(cotangent.T, hidden, preferred_element_type=jnp.float32)]
    unnamed x11 -> x8, waiting for transfers between devices: 0.18 us -> 141 us
    dot_general x6 -> x0, local copies, waits for them, and re-layouts: 94 us -> none  [the longest x2 31.4 us: block_scores(): jnp.einsum('qkb,bh->hqk', bucket_table(buckets[0]), bias_tables[0], prefe...]
    unnamed x1 -> x0, blocking collectives: 77.1 us -> none
    pallas_call x0 -> x2, Pallas kernels: none -> 53.1 us  [the longest x1 29.8 us: attention_backward(): pl.pallas_call(attention_backward_kernel, grid=(pairs,), out_shape=(low,...]
    convert_element_type x4 -> x0, local copies, waits for them, and re-layouts: 48.2 us -> none  [the longest x2 24.2 us: on_device(): grad_scores = grad_full.astype(jnp.bfloat16)]
    convert_element_type x3 -> x0, other arithmetic: 23.8 us -> none  [the longest x2 22.1 us: on_device(): (grad_full - grad_scores.astype(jnp.float32)).astype(jnp.bfloat16)]
  transfers between devices with their start and end apart: 11 -> 7, of which waited for: 7 -> 6; matrix products, arithmetic and copies ran while one was open for 35% -> 9% of each run, Pallas kernels for 4% -> 11%
where the time goes in v2:
time: 746 us; the launch traced here: 740 us
  waiting for transfers between devices  387 us (52%)
  Pallas kernels  185 us (25%)
  matrix products  66.1 us (9%)
  local copies, waits for them, and re-layouts  49.6 us (7%)
  other arithmetic  35.6 us (5%)
  between operations  15.2 us (2%)
    reduce_scatter x1, waiting for transfers between devices, on_device(): own_up = lax.psum_scatter(grad_up, 'dp', scatter_dimension=0, tiled=True)  142 us
    unnamed x8, waiting for transfers between devices  141 us
    pallas_call x1, Pallas kernels, stem_backward(): pl.pallas_call(functools.partial(stem_backward_kernel, devices, places),...  78.1 us
    reduce_scatter x1, waiting for transfers between devices, on_device(): lax.psum_scatter(grad_attn, 'dp', scatter_dimension=0, tiled=True)  54.5 us
    pallas_call x1, Pallas kernels, stem_forward(): pl.pallas_call(functools.partial(stem_forward_kernel, devices, places), o...  54.2 us
    unnamed x131, local copies, waits for them, and re-layouts  45.7 us
    pallas_call x1, Pallas kernels, attention_backward(): pl.pallas_call(attention_backward_kernel, grid=(pairs,), out_shape=(low,...  29.8 us
    psum x1, waiting for transfers between devices, on_device(): lax.psum(jnp.dot(context, output_proj, preferred_element_type=jnp.float32...  24.1 us
  transfers between devices with their start and end apart: 7, of which 6 were waited for; matrix products, arithmetic and copies ran while one was open for 9% of the time, Pallas kernels for 11%

profile of v2, /device:TPU:0, one launch (start us, length us, event | category | flops | bytes accessed | tf_op | source)
XLA Modules:
  0.0 739.9 jit_solution(16195677024107395105)
XLA Ops:
  12.2 54.2 %stem_forward.1 = (f32[2048,128]{1,0:T(8,128)S(1)}, f32[5448,128]{1,0:T(8,128)S(1)}, f32[3400,128]{1,0:T(8,128)S(1)}, f32[9,128]{1,0:T(8,128)S(1)}) custom-call(bf16[3,2048]{1,0:T(4,128)(2,1)S(1)} %bitcast.67, bf16[3,128]{1,0:T(4,128)(2,1)S(1)} %copy-done.23, bf16[8,128,128]{2,1,0:T(8,128)(2,1)S(1)} %copy-done.15, f32[9,128]{1,0:T(8,128)S(1)} %copy-done.19, ...), custom_call_target="tpu_custom_call" | custom-call | tf_op jit(solution)/shard_map/stem_forward/pallas_call | solution.py:554
  66.9 5.8 multiply_convert_fusion
  76.2 2.6 copy.95
  78.8 15.9 %all-reduce.7.cloned.1.call-done = f32[1024,128]{1,0:T(8,128)} async-done(((f32[1024,128]{1,0:T(8,128)}), f32[1024,128]{1,0:T(8,128)}) %all-reduce.7.cloned.1.call-update) | async-done | bytes 524304 | tf_op jit(solution)/shard_map/psum | solution.py:1127
  102.4 23.3 %attention_forward.1 = (bf16[1024,384]{1,0:T(8,128)(2,1)S(1)}, f32[384,1024]{1,0:T(8,128)S(1)}, f32[3,2,1024]{2,1,0:T(2,128)S(1)}) custom-call(f32[3,32,6]{2,1,0:T(8,128)S(1)} %copy.97.tables_ref, s32[1024,8]{1,0:T(8,128)S(1)} %copy.98.info_ref, bf16[1024,384]{1,0:T(8,128)(2,1)S(1)} %convolution_convert_fusion.3.query_ref, ...), custom_call_target="tpu_custom_call" | custom-call | tf_op jit(solution)/shard_map/attention_forward/pallas_call | solution.py:991
  127.7 2.7 fusion.75
  130.9 24.1 %all-reduce.9.cloned.1.call-done = f32[1024,768]{0,1:T(8,128)} async-done(((f32[1024,768]{0,1:T(8,128)}), f32[1024,768]{0,1:T(8,128)}) %all-reduce.9.cloned.1.call-update) | async-done | bytes 3145744 | tf_op jit(solution)/shard_map/psum | solution.py:1141
  155.0 4.1 multiply_reduce_fusion.4
  159.2 2.8 fusion.72
  162.0 18.0 %add_convert_fusion = (bf16[1024,1536]{1,0:T(8,128)(2,1)S(1)}, f32[1024,1536]{1,0:T(8,128)}) fusion(f32[1024,1536]{1,0:T(8,128)S(1)} %fusion.72, bf16[1024,768]{1,0:T(8,128)(2,1)S(1)} %copy-done.42, bf16[1536,768]{1,0:T(8,128)(2,1)S(1)} %copy-done), kind=kOutput, calls=%fused_computation.3 | convolution fusion | flops 2529165312 | bytes 19660800 | tf_op jit(solution)/shard_map/dot_general | solution.py:1150
  181.8 4.2 fusion.77
  186.1 2.6 copy.101
  188.7 6.2 multiply_convert_fusion.1
  196.6 4.4 fusion.76
  201.0 9.6 %all-reduce.11.cloned.1.call-done = f32[1024,768]{0,1:T(8,128)} async-done(((f32[1024,768]{0,1:T(8,128)}), f32[1024,768]{0,1:T(8,128)}) %all-reduce.11.cloned.1.call-update) | async-done | bytes 3145744 | tf_op jit(solution)/shard_map/psum | solution.py:1153
  210.6 3.8 multiply_reduce_fusion
  220.3 29.8 %attention_backward.1 = (bf16[1024,384]{1,0:T(8,128)(2,1)S(1)}, bf16[1024,384]{1,0:T(8,128)(2,1)S(1)}, bf16[1024,384]{1,0:T(8,128)(2,1)S(1)}, f32[6,8,256]{2,1,0:T(8,128)S(1)}) custom-call(f32[3,32,6]{2,1,0:T(8,128)S(1)} %copy.97.tables_ref, s32[1024,8]{1,0:T(8,128)S(1)} %copy.98.info_ref, bf16[1024,384]{1,0:T(8,128)(2,1)S(1)} %copy-done.9, ...), custom_call_target="tpu_custom_call" | custom-call | tf_op jit(solution)/shard_map/attention_backward/pallas_call | solution.py:1029
  252.5 2.6 add_add_fusion
  256.3 3.0 fusion.24
  261.5 2.8 pad_maximum_fusion
  264.4 2.6 copy-done.38
  267.0 6.1 convolution_bitcast_fusion
  273.1 6.1 copy.126
  281.6 6.6 fusion.71
  290.1 2.9 multiply_reduce_fusion.1
  293.8 5.8 multiply_add_fusion
  299.6 2.7 copy.112
  302.3 2.4 copy.113
  311.0 78.1 %stem_backward.1 = (f32[3,128]{1,0:T(4,128)S(1)}, f32[8,128,128]{2,1,0:T(8,128)S(1)}, f32[9,128]{1,0:T(8,128)S(1)}, f32[9,128]{1,0:T(8,128)S(1)}, f32[2,24,128]{2,1,0:T(8,128)S(1)}, /*index=5*/f32[24,128]{1,0:T(8,128)S(1)}) custom-call(f32[2048,128]{1,0:T(8,128)S(1)} %slice_add_fusion.grad_ref, bf16[3,2048]{1,0:T(4,128)(2,1)S(1)} %bitcast.68, ...), custom_call_target="tpu_custom_call" | custom-call | tf_op jit(solution)/shard_map/stem_backward/pallas_call | solution.py:591
  390.6 54.5 %reduce-scatter.6.cloned.1.call-done = f32[48,1536]{1,0:T(8,128)} async-done(((f32[768,1536]{1,0:T(8,128)}), f32[48,1536]{1,0:T(8,128)}) %reduce-scatter.6.cloned.1.call-update) | async-done | bytes 294928 | tf_op jit(solution)/shard_map/reduce_scatter | solution.py:1216
  446.8 140.8 %reduce-scatter.10.cloned.1.call-done = f32[48,1536]{1,0:T(8,128)} async-done(((f32[768,1536]{1,0:T(8,128)}), f32[48,1536]{1,0:T(8,128)}) %reduce-scatter.10.cloned.1.call-update) | async-done | bytes 294928
  587.5 142.1 %reduce-scatter.8.cloned.1.call-done = f32[48,1536]{1,0:T(8,128)} async-done(((f32[768,1536]{1,0:T(8,128)}), f32[48,1536]{1,0:T(8,128)}) %reduce-scatter.8.cloned.1.call-update) | async-done | bytes 294928 | tf_op jit(solution)/shard_map/reduce_scatter | solution.py:1214
  (183 shorter events, 51.7 us)
Async XLA Ops:
  7.2 154.8 %copy-start = (bf16[1536,768]{1,0:T(8,128)(2,1)S(1)}, bf16[1536,768]{1,0:T(8,128)(2,1)}, u32[]{:S(2)}) copy-start(bf16[1536,768]{1,0:T(8,128)(2,1)} %param.39) | copy-start | bytes 7077892
  7.2 87.4 %all-reduce.7.cloned.1.call-start = ((), (), s32[]{:S(2)}) async-start(), calls=%async_computation.3 | async-start | bytes 1048576 | tf_op jit(solution)/shard_map/psum | solution.py:1127
  66.4 6.3 copy-start.10
  66.4 6.3 copy-start.12
  72.7 3.1 copy-start.54
  72.8 3.2 copy-start.55
  72.8 3.2 copy-start.56
  74.7 19.9 %copy-start.45 = (bf16[128,768]{1,0:T(8,128)(2,1)S(1)}, bf16[128,768]{1,0:T(8,128)(2,1)}, u32[]{:S(2)}) copy-start(bf16[128,768]{1,0:T(8,128)(2,1)} %param.30) | copy-start | bytes 589828
  75.6 79.4 %all-reduce.9.cloned.1.call-start = ((), (), s32[]{:S(2)}) async-start(), calls=%async_computation.4 | async-start | bytes 6291456 | tf_op jit(solution)/shard_map/psum | solution.py:1141
  78.8 18.2 %copy-start.52 = (f32[768]{0:T(1024)S(1)}, f32[768]{0:T(1024)}, u32[]{:S(2)}) copy-start(f32[768]{0:T(1024)} %param.31) | copy-start | bytes 9220
  97.0 4.0 copy-start.24
  102.3 23.4 %copy-start.8 = (bf16[1024,384]{1,0:T(8,128)(2,1)}, bf16[1024,384]{1,0:T(8,128)(2,1)S(1)}, u32[]{:S(2)}) copy-start(bf16[1024,384]{1,0:T(8,128)(2,1)S(1)} %convolution_convert_fusion.3.query_ref) | copy-start | bytes 2359300
  102.3 25.4 %copy-start.39 = (bf16[384,768]{1,0:T(8,128)(2,1)S(1)}, bf16[384,768]{1,0:T(8,128)(2,1)}, u32[]{:S(2)}) copy-start(bf16[384,768]{1,0:T(8,128)(2,1)} %param.35) | copy-start | bytes 1769476
  130.5 28.7 %copy-start.53 = (f32[768]{0:T(1024)S(1)}, f32[768]{0:T(1024)}, u32[]{:S(2)}) copy-start(f32[768]{0:T(1024)} %param.37) | copy-start | bytes 9220
  130.5 80.1 %all-reduce.11.cloned.1.call-start = ((), (), s32[]{:S(2)}) async-start(), calls=%async_computation.5 | async-start | bytes 6291456 | tf_op jit(solution)/shard_map/psum | solution.py:1153
  155.0 4.2 copy-start.57
  159.1 20.9 %copy-start.26 = (f32[1024,768]{0,1:T(8,128)}, f32[1024,768]{0,1:T(8,128)S(1)}, u32[]{:S(2)}) copy-start(f32[1024,768]{0,1:T(8,128)S(1)} %get-tuple-element.125) | copy-start | bytes 9437188
  159.2 2.8 copy-start.42
  162.0 18.0 %copy-start.34 = (f32[1024,1536]{1,0:T(8,128)}, f32[1024,1536]{1,0:T(8,128)S(1)}, u32[]{:S(2)}) copy-start(f32[1024,1536]{1,0:T(8,128)S(1)} %fusion.72) | copy-start | bytes 18874372
  186.0 102.9 %all-reduce.13.cloned.1.call-start = ((), (), s32[]{:S(2)}) async-start(), calls=%async_computation.9 | async-start | bytes 12582912 | tf_op jit(solution)/shard_map/psum | solution.py:1147
  210.6 3.8 copy-start.27
  210.6 4.7 copy-start.33
  218.6 31.5 %copy-start.47 = (bf16[768,384]{1,0:T(8,128)(2,1)S(1)}, bf16[768,384]{1,0:T(8,128)(2,1)}, u32[]{:S(2)}) copy-start(bf16[768,384]{1,0:T(8,128)(2,1)} %param.32) | copy-start | bytes 1769476
  255.2 4.1 copy-start.18
  255.2 189.9 %reduce-scatter.6.cloned.1.call-start = ((), (), s32[]{:S(2)}) async-start(), calls=%async_computation.6 | async-start | bytes 5013504 | tf_op jit(solution)/shard_map/reduce_scatter | solution.py:1216
  256.3 3.0 copy-start.44
  264.3 323.2 %reduce-scatter.10.cloned.1.call-start = ((), (), s32[]{:S(2)}) async-start(), calls=%async_computation.8 | async-start | bytes 5013504
  279.2 450.4 %reduce-scatter.8.cloned.1.call-start = ((), (), s32[]{:S(2)}) async-start(), calls=%async_computation.7 | async-start | bytes 5013504 | tf_op jit(solution)/shard_map/reduce_scatter | solution.py:1214
  290.1 2.9 copy-start.29
  290.1 3.8 copy-start.31
  299.6 2.7 copy-start.32
  309.3 423.5 %copy-start.1 = (bf16[1536,768]{1,0:T(8,128)(2,1)S(1)}, bf16[1536,768]{1,0:T(8,128)(2,1)}, u32[]{:S(2)}) copy-start(bf16[1536,768]{1,0:T(8,128)(2,1)} %param.39) | copy-start | bytes 7077892
  (34 other events, 57.3 us)
Sparse Core Ops, SparseCore 0:
  75.7 18.8 all-reduce.6
  130.6 24.3 all-reduce.8
  186.1 24.3 all-reduce.10
  255.3 33.2 all-reduce.12
  293.6 151.4 reduce-scatter.5
  451.5 136.0 reduce-scatter.9
  593.3 136.2 reduce-scatter.7

commit v3 on v2

--- a/solution.py
+++ b/solution.py
@@ -573,6 +573,9 @@
         compiler_params=pltpu.CompilerParams(
             collective_id=0, has_side_effects=True, vmem_limit_bytes=40 * 2**20
         ),
+        cost_estimate=pl.CostEstimate(
+            flops=54 * 10**9, bytes_accessed=2 * 10**7, transcendentals=0
+        ),
         name="stem_forward",
     )(image, conv_first, conv_weights, group_gain, group_shift)
 
@@ -629,27 +632,13 @@
         compiler_params=pltpu.CompilerParams(
             collective_id=1, has_side_effects=True, vmem_limit_bytes=40 * 2**20
         ),
+        cost_estimate=pl.CostEstimate(
+            flops=65 * 10**9, bytes_accessed=2 * 10**7, transcendentals=0
+        ),
         name="stem_backward",
     )(
         grad_map, image, norms, inputs, scales, conv_weights, group_gain, group_shift, split, small
     )
-
-
-def rms_forward(values, gains):
-    inverse = lax.rsqrt(jnp.mean(values * values, axis=-1, keepdims=True) + norm_eps)
-    normal = values * inverse
-    return ((normal * gains).astype(jnp.bfloat16), normal, inverse)
-
-
-def rms_backward(grads, normal, inverse, gains):
-    scaled = grads * gains
-    grad_gain = jnp.sum(grads * normal, axis=0)
-    back = inverse * (scaled - normal * jnp.mean(scaled * normal, axis=-1, keepdims=True))
-    return (back, grad_gain)
-
-
-def exact_gelu(values):
-    return jax.nn.gelu(values, approximate=False)
 
 
 TILE = 128
@@ -983,8 +972,8 @@
     ]
 
 
-def attention_forward(tables, info, query, key, value):
-    tokens, width = query.shape
+def attention_forward(tables, info, heads):
+    tokens, width = heads.shape[0], heads.shape[1] // 3
     pairs = width // 128
     own = pl.BlockSpec((tokens, 128), lambda pair: (0, pair))
     fixed, moving = attention_scratch(tokens)
@@ -1000,8 +989,8 @@
             pl.BlockSpec(memory_space=pltpu.SMEM),
             pl.BlockSpec((tokens, 8), lambda pair: (0, 0)),
             own,
-            own,
-            own,
+            pl.BlockSpec((tokens, 128), lambda pair: (0, pairs + pair)),
+            pl.BlockSpec((tokens, 128), lambda pair: (0, 2 * pairs + pair)),
         ],
         out_specs=(
             own,
@@ -1016,12 +1005,15 @@
         compiler_params=pltpu.CompilerParams(
             dimension_semantics=("arbitrary",), vmem_limit_bytes=48 * 2**20
         ),
+        cost_estimate=pl.CostEstimate(
+            flops=23 * 10**9, bytes_accessed=2 * 10**7, transcendentals=0
+        ),
         name="attention_forward",
-    )(tables, info, query, key, value)
-
-
-def attention_backward(tables, info, query, key, value, grad_context, exact, lse):
-    tokens, width = query.shape
+    )(tables, info, heads, heads, heads)
+
+
+def attention_backward(tables, info, heads, grad_context, exact, lse):
+    tokens, width = grad_context.shape
     pairs = width // 128
     own = pl.BlockSpec((tokens, 128), lambda pair: (0, pair))
     fixed, moving = attention_scratch(tokens)
@@ -1034,8 +1026,8 @@
             pl.BlockSpec(memory_space=pltpu.SMEM),
             pl.BlockSpec((tokens, 8), lambda pair: (0, 0)),
             own,
-            own,
-            own,
+            pl.BlockSpec((tokens, 128), lambda pair: (0, pairs + pair)),
+            pl.BlockSpec((tokens, 128), lambda pair: (0, 2 * pairs + pair)),
             own,
             pl.BlockSpec((128, tokens), lambda pair: (pair, 0)),
             pl.BlockSpec((1, 2, tokens), lambda pair: (pair, 0, 0)),
@@ -1057,8 +1049,11 @@
         compiler_params=pltpu.CompilerParams(
             dimension_semantics=("arbitrary",), vmem_limit_bytes=48 * 2**20
         ),
+        cost_estimate=pl.CostEstimate(
+            flops=30 * 10**9, bytes_accessed=2 * 10**7, transcendentals=0
+        ),
         name="attention_backward",
-    )(tables, info, query, key, value, grad_context, exact, lse)
+    )(tables, info, heads, heads, heads, grad_context, exact, lse)
 
 
 def bucket_grads(diagonals):
@@ -1077,6 +1072,544 @@
     chosen = (slots[..., None] == jnp.arange(3 * NBUCKET, dtype=jnp.int32)).astype(jnp.float32)
     sums = jnp.einsum("hrc,rcb->bh", diagonals[:, :7], chosen, precision=highest)
     return sums.reshape(3, NBUCKET, -1)
+
+
+ROWS = 256
+
+
+def greet_partner():
+    pl.semaphore_signal(
+        pltpu.get_barrier_semaphore(),
+        inc=1,
+        device_id=(lax.axis_index("dp"), 1 - lax.axis_index("tensor")),
+        device_id_type=MESH,
+    )
+
+
+def partner_copy(source, target, send_sem, recv_sem):
+    return pltpu.make_async_remote_copy(
+        src_ref=source,
+        dst_ref=target,
+        send_sem=send_sem,
+        recv_sem=recv_sem,
+        device_id=(lax.axis_index("dp"), 1 - lax.axis_index("tensor")),
+        device_id_type=MESH,
+    )
+
+
+def dot_rows(left, right):
+    return lax.dot_general(
+        left, right, (((0,), (0,)), ((), ())), preferred_element_type=jnp.float32
+    )
+
+
+def inverse_rms(values):
+    return lax.rsqrt(jnp.mean(values * values, axis=1, keepdims=True) + norm_eps)
+
+
+def box_kernel(
+    feature_ref,
+    info_ref,
+    embedded_ref,
+    roi_ref,
+    norm_ref,
+    query_proj_ref,
+    key_proj_ref,
+    value_proj_ref,
+    pooled_ref,
+    stream_ref,
+    input_ref,
+    heads_ref,
+    features,
+    mask,
+    part,
+    received,
+    projections,
+    send_sem,
+    recv_sem,
+):
+    greet_partner()
+    tokens = info_ref.shape[0]
+    pixels = feature_ref.shape[0]
+    tile_rows = pixels // 128
+    first_row = lax.axis_index("tensor") * tile_rows
+    features[...] = split_two(feature_ref[...])
+    lane = lax.broadcasted_iota(jnp.int32, (ROWS, 128), 1)
+    copies = []
+    for block in range(tokens // ROWS):
+        at = slice(block * ROWS, (block + 1) * ROWS)
+        column = (lane >= info_ref[at, 0:1]) & (lane < info_ref[at, 4:5])
+        column = jnp.where(column, 1.0, 0.0)
+        top = jnp.broadcast_to(info_ref[at, 1:2], (ROWS, 128)) - first_row
+        bottom = jnp.broadcast_to(info_ref[at, 5:6], (ROWS, 128)) - first_row
+        for row in range(tile_rows):
+            inside = jnp.where((top <= row) & (bottom > row), column, 0.0)
+            mask[block % 2, :, row * 128 : (row + 1) * 128] = inside.astype(jnp.bfloat16)
+        sums = dot_plain(mask[block % 2], features[...])
+        part[at, :] = sums[:, :128] + sums[:, 128:]
+        if block == 0:
+            pl.semaphore_wait(pltpu.get_barrier_semaphore(), 1)
+        copy = partner_copy(
+            part.at[pl.ds(block * ROWS, ROWS)],
+            received.at[pl.ds(block * ROWS, ROWS)],
+            send_sem.at[block],
+            recv_sem.at[block],
+        )
+        copy.start()
+        copies.append(copy)
+    width = query_proj_ref.shape[1]
+    for index, ref in enumerate((query_proj_ref, key_proj_ref, value_proj_ref)):
+        projections[:, index * width : (index + 1) * width] = ref[...]
+    for block in range(tokens // ROWS):
+        at = slice(block * ROWS, (block + 1) * ROWS)
+        copies[block].wait_recv()
+        area = (info_ref[at, 5:6] - info_ref[at, 1:2]) * (info_ref[at, 4:5] - info_ref[at, 0:1])
+        pooled = ((part[at, :] + received[at, :]) / area.astype(jnp.float32)).astype(jnp.bfloat16)
+        pooled_ref[at, :] = pooled
+        stream = embedded_ref[at, :].astype(jnp.float32) + dot_plain(pooled, roi_ref[...])
+        stream_ref[at, :] = stream
+        attn_in = (stream * inverse_rms(stream) * norm_ref[...]).astype(jnp.bfloat16)
+        input_ref[at, :] = attn_in
+        heads_ref[at, :] = dot_plain(attn_in, projections[...]).astype(jnp.bfloat16)
+    for copy in copies:
+        copy.wait_send()
+
+
+def box_forward(
+    feature_map, info, embeddings, roi_proj, attn_norm, query_proj, key_proj, value_proj
+):
+    tokens, width = embeddings.shape
+    local = query_proj.shape[1]
+    blocks = tokens // ROWS
+    whole = pl.BlockSpec(memory_space=pltpu.VMEM)
+    return pl.pallas_call(
+        box_kernel,
+        out_shape=(
+            jax.ShapeDtypeStruct((tokens, 128), jnp.bfloat16),
+            jax.ShapeDtypeStruct((tokens, width), jnp.float32),
+            jax.ShapeDtypeStruct((tokens, width), jnp.bfloat16),
+            jax.ShapeDtypeStruct((tokens, 3 * local), jnp.bfloat16),
+        ),
+        in_specs=[whole] * 8,
+        out_specs=(whole,) * 4,
+        scratch_shapes=[
+            pltpu.VMEM((feature_map.shape[0], 256), jnp.bfloat16),
+            pltpu.VMEM((2, ROWS, feature_map.shape[0]), jnp.bfloat16),
+            pltpu.VMEM((tokens, 128), jnp.float32),
+            pltpu.VMEM((tokens, 128), jnp.float32),
+            pltpu.VMEM((width, 3 * local), jnp.bfloat16),
+            pltpu.SemaphoreType.DMA((blocks,)),
+            pltpu.SemaphoreType.DMA((blocks,)),
+        ],
+        compiler_params=pltpu.CompilerParams(
+            collective_id=2, has_side_effects=True, vmem_limit_bytes=48 * 2**20
+        ),
+        cost_estimate=pl.CostEstimate(
+            flops=12 * 10**9, bytes_accessed=2 * 10**7, transcendentals=0
+        ),
+        name="box_forward",
+    )(
+        feature_map,
+        info,
+        embeddings,
+        roi_proj,
+        attn_norm.reshape(1, -1),
+        query_proj,
+        key_proj,
+        value_proj,
+    )
+
+
+def middle_kernel(
+    context_ref,
+    stream_hbm,
+    cotangent_hbm,
+    output_ref,
+    norm_ref,
+    up_hbm,
+    down_hbm,
+    layer_hbm,
+    grad_middle_hbm,
+    grad_context_hbm,
+    grad_up_hbm,
+    grad_down_hbm,
+    grad_output_ref,
+    grad_norm_ref,
+    middle,
+    cotangent,
+    up,
+    down,
+    part,
+    other,
+    part_out,
+    other_out,
+    other_grad,
+    ffn_in,
+    hidden,
+    grad_pre,
+    staged,
+    grad_low,
+    layer_low,
+    grad_context,
+    load_sem,
+    store_sem,
+    grad_sem,
+    send_sem,
+    recv_sem,
+):
+    greet_partner()
+    tokens, width = stream_hbm.shape
+    units = up_hbm.shape[1]
+    blocks = tokens // ROWS
+    loads = [
+        pltpu.make_async_copy(source, target, load_sem.at[index])
+        for index, (source, target) in enumerate(
+            [(cotangent_hbm, cotangent), (down_hbm, down), (stream_hbm, middle), (up_hbm, up)]
+        )
+    ]
+    for load in loads:
+        load.start()
+    attn_copies = []
+    for block in range(blocks):
+        at = slice(block * ROWS, (block + 1) * ROWS)
+        part[at, :] = dot_plain(context_ref[at, :], output_ref[...])
+        if block == 0:
+            pl.semaphore_wait(pltpu.get_barrier_semaphore(), 1)
+        copy = partner_copy(
+            part.at[pl.ds(block * ROWS, ROWS)],
+            other.at[pl.ds(block * ROWS, ROWS)],
+            send_sem.at[0, block],
+            recv_sem.at[0, block],
+        )
+        copy.start()
+        attn_copies.append(copy)
+    for load in loads:
+        load.wait()
+    out_copies = []
+    grad_copies = []
+    for block in range(blocks):
+        at = slice(block * ROWS, (block + 1) * ROWS)
+        grad_hidden = dot_last(cotangent[at, :], down[...])
+        attn_copies[block].wait()
+        values = middle[at, :] + (part[at, :] + other[at, :])
+        middle[at, :] = values
+        inner = (values * inverse_rms(values) * norm_ref[...]).astype(jnp.bfloat16)
+        ffn_in[at, :] = inner
+        pre_act = dot_plain(inner, up[...])
+        below = 0.5 * (1.0 + lax.erf(pre_act * (0.5**0.5)))
+        density = jnp.exp(-0.5 * (pre_act * pre_act)) * 0.3989422804014327
+        hidden[at, :] = (pre_act * below).astype(jnp.bfloat16)
+        grad_pre[at, :] = (grad_hidden * (below + pre_act * density)).astype(jnp.bfloat16)
+        part[at, :] = dot_last(grad_pre[at, :], up[...])
+        copy = partner_copy(
+            part.at[pl.ds(block * ROWS, ROWS)],
+            other_grad.at[pl.ds(block * ROWS, ROWS)],
+            send_sem.at[1, block],
+            recv_sem.at[1, block],
+        )
+        copy.start()
+        grad_copies.append(copy)
+        part_out[at, :] = dot_plain(hidden[at, :], down[...])
+        copy = partner_copy(
+            part_out.at[pl.ds(block * ROWS, ROWS)],
+            other_out.at[pl.ds(block * ROWS, ROWS)],
+            send_sem.at[2, block],
+            recv_sem.at[2, block],
+        )
+        copy.start()
+        out_copies.append(copy)
+    half = width // 2
+    stores = []
+    for index in range(4):
+        rows = slice((index % 2) * half, (index % 2 + 1) * half)
+        if index >= 2:
+            stores[index - 2].wait()
+        if index < 2:
+            staged[index % 2] = dot_rows(ffn_in[:, rows], grad_pre[...])
+            target = grad_up_hbm
+        else:
+            staged[index % 2] = dot_rows(cotangent[:, rows], hidden[...])
+            target = grad_down_hbm
+        store = pltpu.make_async_copy(
+            staged.at[index % 2], target.at[pl.ds((index % 2) * half, half)], grad_sem.at[index]
+        )
+        store.start()
+        stores.append(store)
+    norm_total = jnp.zeros((8, width), jnp.float32)
+    for block in range(blocks):
+        at = slice(block * ROWS, (block + 1) * ROWS)
+        values = middle[at, :]
+        inverse = inverse_rms(values)
+        hat = values * inverse
+        grad_copies[block].wait()
+        grad_inner = part[at, :] + other_grad[at, :]
+        norm_total = norm_total + jnp.sum((grad_inner * hat).reshape(ROWS // 8, 8, width), axis=0)
+        scaled = grad_inner * norm_ref[...]
+        back = inverse * (scaled - hat * jnp.mean(scaled * hat, axis=1, keepdims=True))
+        grad_values = cotangent[at, :].astype(jnp.float32) + back
+        out_copies[block].wait()
+        layer_low[at, :] = (values + (part_out[at, :] + other_out[at, :])).astype(jnp.bfloat16)
+        middle[at, :] = grad_values
+        low = grad_values.astype(jnp.bfloat16)
+        grad_low[at, :] = low
+        grad_context[at, :] = dot_last(low, output_ref[...]).astype(jnp.bfloat16)
+        for index, (source, target) in enumerate(
+            [
+                (layer_low, layer_hbm),
+                (middle, grad_middle_hbm),
+                (grad_context, grad_context_hbm),
+            ]
+        ):
+            rows = pl.ds(block * ROWS, ROWS)
+            store = pltpu.make_async_copy(
+                source.at[rows], target.at[rows], store_sem.at[index, block]
+            )
+            store.start()
+            stores.append(store)
+    grad_norm_ref[...] = jnp.sum(norm_total, axis=0, keepdims=True)
+    grad_output_ref[...] = dot_rows(grad_low[...], context_ref[...])
+    for store in stores[2:]:
+        store.wait()
+
+
+def middle_layer(context, stream, cotangent, output_proj, ffn_norm, up_proj, down_proj):
+    tokens, width = stream.shape
+    units = up_proj.shape[1]
+    local = context.shape[1]
+    blocks = tokens // ROWS
+    whole = pl.BlockSpec(memory_space=pltpu.VMEM)
+    far = pl.BlockSpec(memory_space=pl.ANY)
+    wide_sum = pltpu.VMEM((tokens, width), jnp.float32)
+    wide_low = pltpu.VMEM((tokens, width), jnp.bfloat16)
+    unit_low = pltpu.VMEM((tokens, units), jnp.bfloat16)
+    return pl.pallas_call(
+        middle_kernel,
+        out_shape=(
+            jax.ShapeDtypeStruct((tokens, width), jnp.bfloat16),
+            jax.ShapeDtypeStruct((tokens, width), jnp.float32),
+            jax.ShapeDtypeStruct((tokens, local), jnp.bfloat16),
+            jax.ShapeDtypeStruct((width, units), jnp.float32),
+            jax.ShapeDtypeStruct((width, units), jnp.float32),
+            jax.ShapeDtypeStruct((width, local), jnp.float32),
+            jax.ShapeDtypeStruct((1, width), jnp.float32),
+        ),
+        in_specs=[whole, far, far, whole, whole, far, far],
+        out_specs=(far, far, far, far, far, whole, whole),
+        scratch_shapes=[
+            wide_sum,
+            wide_low,
+            pltpu.VMEM((width, units), jnp.bfloat16),
+            pltpu.VMEM((units, width), jnp.bfloat16),
+            wide_sum,
+            wide_sum,
+            wide_sum,
+            wide_sum,
+            wide_sum,
+            wide_low,
+            unit_low,
+            unit_low,
+            pltpu.VMEM((2, width // 2, units), jnp.float32),
+            wide_low,
+            wide_low,
+            pltpu.VMEM((tokens, local), jnp.bfloat16),
+            pltpu.SemaphoreType.DMA((4,)),
+            pltpu.SemaphoreType.DMA((3, blocks)),
+            pltpu.SemaphoreType.DMA((4,)),
+            pltpu.SemaphoreType.DMA((3, blocks)),
+            pltpu.SemaphoreType.DMA((3, blocks)),
+        ],
+        compiler_params=pltpu.CompilerParams(
+            collective_id=3, has_side_effects=True, vmem_limit_bytes=60 * 2**20
+        ),
+        cost_estimate=pl.CostEstimate(
+            flops=32 * 10**9, bytes_accessed=2 * 10**7, transcendentals=0
+        ),
+        name="middle_layer",
+    )(context, stream, cotangent, output_proj, ffn_norm.reshape(1, -1), up_proj, down_proj)
+
+
+def end_kernel(
+    grad_query_ref,
+    grad_key_ref,
+    grad_value_ref,
+    query_proj_ref,
+    key_proj_ref,
+    value_proj_ref,
+    input_ref,
+    stream_hbm,
+    grad_middle_hbm,
+    norm_ref,
+    roi_ref,
+    pooled_ref,
+    info_ref,
+    boxes_ref,
+    grad_stream_hbm,
+    grad_heads_hbm,
+    grad_roi_ref,
+    grad_map_ref,
+    grad_norm_ref,
+    grad_heads,
+    projections,
+    stream,
+    grad_stream,
+    part,
+    other,
+    weight_grad,
+    grad_low,
+    grad_box,
+    load_sem,
+    store_sem,
+    grad_sem,
+    send_sem,
+    recv_sem,
+):
+    greet_partner()
+    tokens, width = stream_hbm.shape
+    local = grad_query_ref.shape[1]
+    blocks = tokens // ROWS
+    loads = [
+        pltpu.make_async_copy(stream_hbm, stream, load_sem.at[0]),
+        pltpu.make_async_copy(grad_middle_hbm, grad_stream, load_sem.at[1]),
+    ]
+    for load in loads:
+        load.start()
+    for index, (grad, proj) in enumerate(
+        (
+            (grad_query_ref, query_proj_ref),
+            (grad_key_ref, key_proj_ref),
+            (grad_value_ref, value_proj_ref),
+        )
+    ):
+        columns = slice(index * local, (index + 1) * local)
+        grad_heads[:, columns] = grad[...]
+        projections[:, columns] = proj[...]
+    copies = []
+    for block in range(blocks):
+        at = slice(block * ROWS, (block + 1) * ROWS)
+        part[at, :] = dot_last(grad_heads[at, :], projections[...])
+        if block == 0:
+            pl.semaphore_wait(pltpu.get_barrier_semaphore(), 1)
+        copy = partner_copy(
+            part.at[pl.ds(block * ROWS, ROWS)],
+            other.at[pl.ds(block * ROWS, ROWS)],
+            send_sem.at[block],
+            recv_sem.at[block],
+        )
+        copy.start()
+        copies.append(copy)
+    weight_grad[...] = dot_rows(input_ref[...], grad_heads[...])
+    weight_store = pltpu.make_async_copy(weight_grad, grad_heads_hbm, grad_sem)
+    weight_store.start()
+    for load in loads:
+        load.wait()
+    stores = []
+    norm_total = jnp.zeros((8, width), jnp.float32)
+    for block in range(blocks):
+        at = slice(block * ROWS, (block + 1) * ROWS)
+        values = stream[at, :]
+        inverse = inverse_rms(values)
+        hat = values * inverse
+        copies[block].wait()
+        grad_inner = part[at, :] + other[at, :]
+        norm_total = norm_total + jnp.sum((grad_inner * hat).reshape(ROWS // 8, 8, width), axis=0)
+        scaled = grad_inner * norm_ref[...]
+        back = inverse * (scaled - hat * jnp.mean(scaled * hat, axis=1, keepdims=True))
+        grad_values = grad_stream[at, :] + back
+        grad_stream[at, :] = grad_values
+        rows = pl.ds(block * ROWS, ROWS)
+        store = pltpu.make_async_copy(
+            grad_stream.at[rows], grad_stream_hbm.at[rows], store_sem.at[block]
+        )
+        store.start()
+        stores.append(store)
+        low = grad_values.astype(jnp.bfloat16)
+        grad_low[at, :] = low
+        area = (info_ref[at, 5:6] - info_ref[at, 1:2]) * (info_ref[at, 4:5] - info_ref[at, 0:1])
+        grad_box[at, :] = split_two(dot_last(low, roi_ref[...]) / area.astype(jnp.float32))
+    grad_norm_ref[...] = jnp.sum(norm_total, axis=0, keepdims=True)
+    tile_rows = grad_map_ref.shape[0] // 128
+    first_row = lax.axis_index("tensor") * tile_rows
+    column = lax.broadcasted_iota(jnp.int32, (128, tokens), 0)
+    inside = jnp.where(
+        (column >= boxes_ref[0:1, :]) & (column < boxes_ref[2:3, :]), 1.0, 0.0
+    ).astype(jnp.bfloat16)
+    top = boxes_ref[1:2, :] - first_row
+    bottom = boxes_ref[3:4, :] - first_row
+    for row in range(tile_rows):
+        chosen = jnp.where((top <= row) & (bottom > row), 1.0, 0.0).astype(jnp.bfloat16)
+        sums = dot_plain(inside * chosen, grad_box[...])
+        grad_map_ref[row * 128 : (row + 1) * 128, :] = sums[:, :128] + sums[:, 128:]
+    grad_roi_ref[...] = dot_rows(grad_low[...], pooled_ref[...])
+    weight_store.wait()
+    for store in stores:
+        store.wait()
+
+
+def end_layer(
+    grad_heads,
+    projections,
+    attn_in,
+    stream,
+    grad_middle,
+    attn_norm,
+    roi_proj,
+    pooled,
+    info,
+    boxes,
+    pixels,
+):
+    tokens, width = stream.shape
+    local = grad_heads[0].shape[1]
+    blocks = tokens // ROWS
+    whole = pl.BlockSpec(memory_space=pltpu.VMEM)
+    far = pl.BlockSpec(memory_space=pl.ANY)
+    wide_sum = pltpu.VMEM((tokens, width), jnp.float32)
+    return pl.pallas_call(
+        end_kernel,
+        out_shape=(
+            jax.ShapeDtypeStruct((tokens, width), jnp.float32),
+            jax.ShapeDtypeStruct((width, 3 * local), jnp.float32),
+            jax.ShapeDtypeStruct((width, 128), jnp.float32),
+            jax.ShapeDtypeStruct((pixels, 128), jnp.float32),
+            jax.ShapeDtypeStruct((1, width), jnp.float32),
+        ),
+        in_specs=[whole] * 7 + [far, far] + [whole] * 5,
+        out_specs=(far, far, whole, whole, whole),
+        scratch_shapes=[
+            pltpu.VMEM((tokens, 3 * local), jnp.bfloat16),
+            pltpu.VMEM((width, 3 * local), jnp.bfloat16),
+            wide_sum,
+            wide_sum,
+            wide_sum,
+            wide_sum,
+            pltpu.VMEM((width, 3 * local), jnp.float32),
+            pltpu.VMEM((tokens, width), jnp.bfloat16),
+            pltpu.VMEM((tokens, 256), jnp.bfloat16),
+            pltpu.SemaphoreType.DMA((2,)),
+            pltpu.SemaphoreType.DMA((blocks,)),
+            pltpu.SemaphoreType.DMA,
+            pltpu.SemaphoreType.DMA((blocks,)),
+            pltpu.SemaphoreType.DMA((blocks,)),
+        ],
+        compiler_params=pltpu.CompilerParams(
+            collective_id=4, has_side_effects=True, vmem_limit_bytes=56 * 2**20
+        ),
+        cost_estimate=pl.CostEstimate(
+            flops=15 * 10**9, bytes_accessed=2 * 10**7, transcendentals=0
+        ),
+        name="end_layer",
+    )(
+        *grad_heads,
+        *projections,
+        attn_in,
+        stream,
+        grad_middle,
+        attn_norm.reshape(1, -1),
+        roi_proj,
+        pooled,
+        info,
+        boxes,
+    )
 
 
 def on_device(
@@ -1105,94 +1638,42 @@
     feature_map, *records = stem_forward(
         page_image, conv_first, conv_weights, group_gain, group_shift, devices
     )
-    tile_rows = page_image.shape[1]
-    row_ids = lax.axis_index("tensor") * tile_rows + jnp.arange(tile_rows, dtype=jnp.int32)
-    col_ids = jnp.arange(page_image.shape[2], dtype=jnp.int32)
-    left_edge = token_boxes[0, 0]
-    top_edge = token_boxes[1, 0]
-    right_edge = token_boxes[2, 0]
-    bottom_edge = token_boxes[3, 0]
-    row_mask = (
-        (row_ids[None, :] >= top_edge[:, None]) & (row_ids[None, :] < bottom_edge[:, None])
-    ).astype(jnp.float32)
-    col_mask = (
-        (col_ids[None, :] >= left_edge[:, None]) & (col_ids[None, :] < right_edge[:, None])
-    ).astype(jnp.float32)
-    box_area = ((bottom_edge - top_edge) * (right_edge - left_edge)).astype(jnp.float32)
-    box_mask = (row_mask[:, :, None] * col_mask[:, None, :]).astype(jnp.bfloat16)
-    box_mask = box_mask.reshape(box_mask.shape[0], -1)
-    feature_pair = split_two(feature_map)
-    box_pair = jnp.dot(box_mask, feature_pair, preferred_element_type=jnp.float32)
-    partial_boxes = box_pair[:, :128] + box_pair[:, 128:]
-    box_sums = lax.psum(partial_boxes, "tensor")
-    pooled = (box_sums / box_area[:, None]).astype(jnp.bfloat16)
-    stream = embeddings.astype(jnp.float32) + jnp.dot(
-        pooled, roi_proj, preferred_element_type=jnp.float32
-    )
-    attn_in, attn_hat, attn_inv = rms_forward(stream, attn_norm)
-    query = jnp.dot(attn_in, query_proj, preferred_element_type=jnp.float32).astype(jnp.bfloat16)
-    key = jnp.dot(attn_in, key_proj, preferred_element_type=jnp.float32).astype(jnp.bfloat16)
-    value = jnp.dot(attn_in, value_proj, preferred_element_type=jnp.float32).astype(jnp.bfloat16)
+    left_edge, top_edge, right_edge, bottom_edge = token_boxes[:, 0]
     blank = jnp.zeros_like(left_edge)
     info = jnp.stack(
-        [left_edge, top_edge, doc_ids[0], pad_mask[0], blank, blank, blank, blank], axis=1
-    )
-    context, exact, lse = attention_forward(bias_tables, info, query, key, value)
-    attn_out = lax.psum(jnp.dot(context, output_proj, preferred_element_type=jnp.float32), "tensor")
-    middle = stream + attn_out
-    ffn_in, ffn_hat, ffn_inv = rms_forward(middle, ffn_norm)
-    pre_act = jnp.dot(ffn_in, up_proj, preferred_element_type=jnp.float32)
-    activated, gelu_pullback = jax.vjp(exact_gelu, pre_act)
-    hidden = activated.astype(jnp.bfloat16)
-    ffn_out = lax.psum(jnp.dot(hidden, down_proj, preferred_element_type=jnp.float32), "tensor")
-    layer_out = (middle + ffn_out).astype(jnp.bfloat16)
-    grad_down = jnp.dot(cotangent.T, hidden, preferred_element_type=jnp.float32)
-    grad_hidden = jnp.dot(cotangent, down_proj.T, preferred_element_type=jnp.float32)
-    grad_pre = gelu_pullback(grad_hidden)[0].astype(jnp.bfloat16)
-    grad_up = jnp.dot(ffn_in.T, grad_pre, preferred_element_type=jnp.float32)
-    grad_ffn_in = lax.psum(
-        jnp.dot(grad_pre, up_proj.T, preferred_element_type=jnp.float32), "tensor"
-    )
-    grad_mid_norm, grad_ffn_norm = rms_backward(grad_ffn_in, ffn_hat, ffn_inv, ffn_norm)
-    grad_middle = cotangent.astype(jnp.float32) + grad_mid_norm
-    grad_mid_low = grad_middle.astype(jnp.bfloat16)
-    grad_context = jnp.dot(
-        grad_mid_low, output_proj.T, preferred_element_type=jnp.float32
-    ).astype(jnp.bfloat16)
-    grad_query_low, grad_key_low, grad_value_low, diagonals = attention_backward(
-        bias_tables, info, query, key, value, grad_context, exact, lse
+        [left_edge, top_edge, doc_ids[0], pad_mask[0], right_edge, bottom_edge, blank, blank],
+        axis=1,
+    )
+    pooled, stream, attn_in, heads = box_forward(
+        feature_map, info, embeddings, roi_proj, attn_norm, query_proj, key_proj, value_proj
+    )
+    context, exact, lse = attention_forward(bias_tables, info, heads)
+    layer_out, grad_middle, grad_context, grad_up, grad_down, grad_output, grad_ffn_norm = (
+        middle_layer(context, stream, cotangent, output_proj, ffn_norm, up_proj, down_proj)
+    )
+    *grad_heads, diagonals = attention_backward(
+        bias_tables, info, heads, grad_context, exact, lse
     )
     grad_tables = bucket_grads(diagonals)
-    attn_terms = jnp.dot(grad_query_low, query_proj.T, preferred_element_type=jnp.float32)
-    attn_terms = attn_terms + jnp.dot(grad_key_low, key_proj.T, preferred_element_type=jnp.float32)
-    attn_terms = attn_terms + jnp.dot(
-        grad_value_low, value_proj.T, preferred_element_type=jnp.float32
-    )
-    grad_attn_in = lax.psum(attn_terms, "tensor")
-    grad_stream_norm, grad_attn_norm = rms_backward(grad_attn_in, attn_hat, attn_inv, attn_norm)
-    grad_stream = grad_middle + grad_stream_norm
-    grad_low = grad_stream.astype(jnp.bfloat16)
-    grad_roi = jnp.dot(grad_low.T, pooled, preferred_element_type=jnp.float32)
-    grad_pooled = jnp.dot(grad_low, roi_proj.T, preferred_element_type=jnp.float32)
-    grad_box = grad_pooled / box_area[:, None]
-    map_pair = jnp.dot(box_mask.T, split_two(grad_box), preferred_element_type=jnp.float32)
-    grad_map = map_pair[:, :128] + map_pair[:, 128:]
-    grad_attn = jnp.concatenate(
-        [
-            jnp.dot(
-                attn_in.T,
-                jnp.concatenate([grad_query_low, grad_key_low, grad_value_low], axis=1),
-                preferred_element_type=jnp.float32,
-            ),
-            jnp.dot(grad_mid_low.T, context, preferred_element_type=jnp.float32),
-        ],
-        axis=1,
-    )
+    grad_stream, grad_projections, grad_roi, grad_map, grad_attn_norm = end_layer(
+        grad_heads,
+        (query_proj, key_proj, value_proj),
+        attn_in,
+        stream,
+        grad_middle,
+        attn_norm,
+        roi_proj,
+        pooled,
+        info,
+        token_boxes[:, 0],
+        feature_map.shape[0],
+    )
+    grad_attn = jnp.concatenate([grad_projections, grad_output], axis=1)
     rows_count = lax.axis_size("dp")
-    width = grad_attn_norm.shape[0]
+    width = grad_attn_norm.shape[1]
     own_rows = width // rows_count
-    heads = grad_tables.shape[2]
-    small = jnp.concatenate([grad_attn_norm, grad_ffn_norm, grad_tables.reshape(-1)])
+    local_heads = grad_tables.shape[2]
+    small = jnp.concatenate([grad_attn_norm[0], grad_ffn_norm[0], grad_tables.reshape(-1)])
     small = jnp.pad(small, (0, -small.shape[0] % 1024)).reshape(-1, 128)
     split = grad_roi.reshape(rows_count, 2, own_rows // 2, grad_roi.shape[1])
     grad_first, grad_convs, grad_gains, grad_offsets, own_roi, small = stem_backward(
@@ -1210,7 +1691,7 @@
     start = lax.axis_index("dp") * own_rows
     own_attn_norm = lax.dynamic_slice(small, (start,), (own_rows,))
     own_ffn_norm = lax.dynamic_slice(small, (width + start,), (own_rows,))
-    own_tables = small[2 * width : 2 * width + grad_tables.size].reshape(3, NBUCKET, heads)
+    own_tables = small[2 * width : 2 * width + grad_tables.size].reshape(3, NBUCKET, local_heads)
     own_up = lax.psum_scatter(grad_up, "dp", scatter_dimension=0, tiled=True)
     own_down = lax.psum_scatter(grad_down, "dp", scatter_dimension=0, tiled=True).T
     own_attn = lax.psum_scatter(grad_attn, "dp", scatter_dimension=0, tiled=True)

time: 746 us -> 657 us (0.88)
  matrix products: 66.1 us -> 0.43 us
  Pallas kernels: 185 us -> 246 us
  waiting for transfers between devices: 387 us -> 349 us
  other arithmetic: 35.6 us -> 4.97 us
  local copies, waits for them, and re-layouts: 49.6 us -> 34.2 us
    reduce_scatter x0 -> x1, waiting for transfers between devices: none -> 141 us  [on_device(): lax.psum_scatter(grad_down, 'dp', scatter_dimension=0, tiled=True)]
    unnamed x8 -> x3, waiting for transfers between devices: 141 us -> 1.39 us
    dot_general x21 -> x0, matrix products: 65.6 us -> none  [the longest x1 18 us: on_device(): jnp.dot(cotangent, down_proj.T, preferred_element_type=jnp.float32)]
    pallas_call x0 -> x3, Pallas kernels: none -> 59.3 us  [the longest x1 32 us: middle_layer(): pl.pallas_call(middle_kernel, out_shape=(jax.ShapeDtypeStruct((tokens, wi...]
    psum x4 -> x0, waiting for transfers between devices: 49.6 us -> none  [the longest x1 24.1 us: on_device(): lax.psum(jnp.dot(context, output_proj, preferred_element_type=jnp.float32...]
    unnamed x131 -> x73, local copies, waits for them, and re-layouts: 45.7 us -> 27.9 us
    convert_element_type x7 -> x0, other arithmetic: 12.9 us -> none  [the longest x1 6.24 us: on_device(): hidden = activated.astype(jnp.bfloat16)]
    reduce_sum x3 -> x0, other arithmetic: 10.8 us -> none  [the longest x2 6.66 us: rms_backward(): grad_gain = jnp.sum(grads * normal, axis=0)]
  transfers between devices with their start and end apart: 7 -> 3, of which waited for: 6 -> 3; matrix products, arithmetic and copies ran while one was open for 9% -> 1% of each run, Pallas kernels for 11% -> 12%
where the time goes in v3:
time: 657 us; the launch traced here: 650 us
  waiting for transfers between devices  349 us (53%)
  Pallas kernels  246 us (37%)
  local copies, waits for them, and re-layouts  34.2 us (5%)
  between operations  14.4 us (2%)
    reduce_scatter x1, waiting for transfers between devices, on_device(): own_up = lax.psum_scatter(grad_up, 'dp', scatter_dimension=0, tiled=True)  142 us
    reduce_scatter x1, waiting for transfers between devices, on_device(): lax.psum_scatter(grad_down, 'dp', scatter_dimension=0, tiled=True)  141 us
    pallas_call x1, Pallas kernels, stem_backward(): pl.pallas_call(functools.partial(stem_backward_kernel, devices, places),...  78.6 us
    reduce_scatter x1, waiting for transfers between devices, on_device(): lax.psum_scatter(grad_attn, 'dp', scatter_dimension=0, tiled=True)  64.9 us
    pallas_call x1, Pallas kernels, stem_forward(): pl.pallas_call(functools.partial(stem_forward_kernel, devices, places), o...  54.5 us
    pallas_call x1, Pallas kernels, middle_layer(): pl.pallas_call(middle_kernel, out_shape=(jax.ShapeDtypeStruct((tokens, wi...  32 us
    pallas_call x1, Pallas kernels, attention_backward(): pl.pallas_call(attention_backward_kernel, grid=(pairs,), out_shape=(low,...  30 us
    unnamed x73, local copies, waits for them, and re-layouts  27.9 us
  transfers between devices with their start and end apart: 3, of which 3 were waited for; matrix products, arithmetic and copies ran while one was open for 1% of the time, Pallas kernels for 12%

profile of v3, /device:TPU:0, one launch (start us, length us, event | category | flops | bytes accessed | tf_op | source)
XLA Modules:
  0.0 649.7 jit_solution(14405532556866308636)
XLA Ops:
  7.2 0.7 slice_bitcast_fusion.1
  8.0 1.3 copy.69
  9.3 0.8 stack.21
  11.7 0.8 copy.52.tables_ref
  12.5 1.3 reshape.428.norm_ref
  13.8 0.9 copy-done.5
  16.8 54.5 %stem_forward.1 = (f32[2048,128]{1,0:T(8,128)S(1)}, f32[5448,128]{1,0:T(8,128)S(1)}, f32[3400,128]{1,0:T(8,128)S(1)}, f32[9,128]{1,0:T(8,128)S(1)}) custom-call(bf16[3,2048]{1,0:T(4,128)(2,1)S(1)} %bitcast.31, bf16[3,128]{1,0:T(4,128)(2,1)S(1)} %copy-done.12, bf16[8,128,128]{2,1,0:T(8,128)(2,1)S(1)} %copy-done.5, f32[9,128]{1,0:T(8,128)S(1)} %copy-done.8, ...), custom_call_target="tpu_custom_call" | custom-call | flops 54000001024 | bytes 20000000 | tf_op jit(solution)/shard_map/stem_forward/pallas_call | solution.py:554
  71.3 1.5 copy-done.23
  72.9 1.3 copy-done.25
  74.2 12.7 %box_forward.1 = (bf16[1024,128]{1,0:T(8,128)(2,1)S(1)}, f32[1024,768]{1,0:T(8,128)}, bf16[1024,768]{1,0:T(8,128)(2,1)S(1)}, bf16[1024,1152]{1,0:T(8,128)(2,1)}) custom-call(f32[2048,128]{1,0:T(8,128)S(1)} %get-tuple-element.49.feature_ref, s32[1024,8]{1,0:T(8,128)S(1)} %copy.53.info_ref, bf16[1024,768]{1,0:T(8,128)(2,1)} %embedded_ref.1, ...), custom_call_target="tpu_custom_call" | custom-call | flops 12000000000 | bytes 20000000 | tf_op jit(solution)/shard_map/box_forward/pallas_call | solution.py:1185
  86.9 1.1 copy-done.15
  88.1 1.8 copy-done.14
  89.8 24.0 %attention_forward.1 = (bf16[1024,384]{1,0:T(8,128)(2,1)S(1)}, f32[384,1024]{1,0:T(8,128)S(1)}, f32[3,2,1024]{2,1,0:T(2,128)S(1)}) custom-call(f32[3,32,6]{2,1,0:T(8,128)S(1)} %copy.52.tables_ref, s32[1024,8]{1,0:T(8,128)S(1)} %copy.53.info_ref, bf16[1024,1152]{1,0:T(8,128)(2,1)S(1)} %copy-done.14, bf16[1024,1152]{1,0:T(8,128)(2,1)S(1)} %copy-done.14, ...), custom_call_target="tpu_custom_call" | custom-call | flops 23000000512 | bytes 20000000 | tf_op jit(solution)/shard_map/attention_forward/pallas_call | solution.py:980
  113.9 0.9 copy-done.21
  114.7 32.0 %middle_layer.1 = (bf16[1024,768]{1,0:T(8,128)(2,1)}, f32[1024,768]{1,0:T(8,128)}, bf16[1024,384]{1,0:T(8,128)(2,1)}, f32[768,1536]{1,0:T(8,128)}, f32[768,1536]...) custom-call(bf16[1024,384]{1,0:T(8,128)(2,1)} %copy-done.21, f32[1024,768]{1,0:T(8,128)} %get-tuple-element.52.stream_hbm, ...), custom_call_target="tpu_custom_call" | custom-call | flops 32000000000 | bytes 20000000 | tf_op jit(solution)/shard_map/middle_layer/pallas_call | solution.py:1385
  146.8 1.1 copy-done.22
  147.9 30.0 %attention_backward.1 = (bf16[1024,384]{1,0:T(8,128)(2,1)S(1)}, bf16[1024,384]{1,0:T(8,128)(2,1)S(1)}, bf16[1024,384]{1,0:T(8,128)(2,1)S(1)}, f32[6,8,256]{2,1,0:T(8,128)S(1)}) custom-call(f32[3,32,6]{2,1,0:T(8,128)S(1)} %copy.52.tables_ref, s32[1024,8]{1,0:T(8,128)S(1)} %copy.53.info_ref, bf16[1024,1152]{1,0:T(8,128)(2,1)} %get-tuple-element.50.query_ref.key_ref.value_ref, ...), custom_call_target="tpu_custom_call" | custom-call | flops 30000001024 | bytes 20000000 | tf_op jit(solution)/shard_map/attention_backward/pallas_call | solution.py:1021
  177.9 0.9 copy-done.17
  178.8 0.9 copy-done.18
  179.7 0.9 copy-done.19
  180.6 14.5 %end_layer.1 = (f32[1024,768]{1,0:T(8,128)}, f32[768,1152]{1,0:T(8,128)}, f32[768,128]{1,0:T(8,128)}, f32[2048,128]{1,0:T(8,128)}, f32[1,768]{1,0:T(1,128)}) custom-call(bf16[1024,384]{1,0:T(8,128)(2,1)} %copy-done.17, bf16[1024,384]{1,0:T(8,128)(2,1)} %copy-done.18, bf16[1024,384]{1,0:T(8,128)(2,1)} %copy-done.19, bf16[768,384]{1,0:T(8,128)(2,1)} %query_proj_ref.3, ...), custom_call_target="tpu_custom_call" | custom-call | flops 15000000512 | bytes 20000000 | tf_op jit(solution)/shard_map/end_layer/pallas_call | solution.py:1567
  195.1 4.9 pad_maximum_fusion
  202.4 1.8 copy-done.24
  204.2 1.5 copy-done.26
  205.6 78.6 %stem_backward.1 = (f32[3,128]{1,0:T(4,128)S(1)}, f32[8,128,128]{2,1,0:T(8,128)S(1)}, f32[9,128]{1,0:T(8,128)S(1)}, f32[9,128]{1,0:T(8,128)S(1)}, f32[2,24,128]{2,1,0:T(8,128)S(1)}, /*index=5*/f32[24,128]{1,0:T(8,128)S(1)}) custom-call(f32[2048,128]{1,0:T(8,128)S(1)} %copy-done.16, bf16[3,2048]{1,0:T(4,128)(2,1)S(1)} %bitcast.32, ...), custom_call_target="tpu_custom_call" | custom-call | flops 65000001536 | bytes 20000000 | tf_op jit(solution)/shard_map/stem_backward/pallas_call | solution.py:594
  285.7 64.9 %reduce-scatter.4.cloned.1.call-done = f32[48,1536]{1,0:T(8,128)} async-done(((f32[768,1536]{1,0:T(8,128)}), f32[48,1536]{1,0:T(8,128)}) %reduce-scatter.4.cloned.1.call-update) | async-done | bytes 294928 | tf_op jit(solution)/shard_map/reduce_scatter | solution.py:1697
  350.6 1.7 slice_bitcast_fusion
  352.3 141.2 %reduce-scatter.8.cloned.1.call-done = f32[48,1536]{1,0:T(8,128)} async-done(((f32[768,1536]{1,0:T(8,128)}), f32[48,1536]{1,0:T(8,128)}) %reduce-scatter.8.cloned.1.call-update) | async-done | bytes 294928 | tf_op jit(solution)/shard_map/reduce_scatter | solution.py:1696
  493.5 141.8 %reduce-scatter.6.cloned.1.call-done = f32[48,1536]{1,0:T(8,128)} async-done(((f32[768,1536]{1,0:T(8,128)}), f32[48,1536]{1,0:T(8,128)}) %reduce-scatter.6.cloned.1.call-update) | async-done | bytes 294928 | tf_op jit(solution)/shard_map/reduce_scatter | solution.py:1695
  635.3 2.8 copy.77
  638.1 1.7 copy.78
  640.3 0.8 copy.80
  (79 shorter events, 9.9 us)
Async XLA Ops:
  7.2 343.4 %reduce-scatter.4.cloned.1.call-start = ((), (), s32[]{:S(2)}) async-start(), calls=%async_computation.3 | async-start | bytes 5013504 | tf_op jit(solution)/shard_map/reduce_scatter | solution.py:1697
  10.3 136.5 %copy-start = (s32[1024,8]{1,0:T(8,128)}, s32[1024,8]{1,0:T(8,128)S(1)}, u32[]{:S(2)}) copy-start(s32[1024,8]{1,0:T(8,128)S(1)} %copy.53.info_ref) | copy-start | bytes 98308
  11.7 62.5 %copy-start.1 = (f32[1,768]{1,0:T(1,128)}, f32[1,768]{1,0:T(1,128)S(1)}, u32[]{:S(2)}) copy-start(f32[1,768]{1,0:T(1,128)S(1)} %reshape.427.norm_ref) | copy-start | bytes 9220
  13.8 0.9 copy-start.5
  14.7 0.7 copy-start.8
  16.8 57.4 %copy-start.2 = (bf16[768,384]{1,0:T(8,128)(2,1)S(1)}, bf16[768,384]{1,0:T(8,128)(2,1)}, u32[]{:S(2)}) copy-start(bf16[768,384]{1,0:T(8,128)(2,1)} %query_proj_ref.3) | copy-start | bytes 1769476
  16.8 57.4 %copy-start.3 = (bf16[768,384]{1,0:T(8,128)(2,1)S(1)}, bf16[768,384]{1,0:T(8,128)(2,1)}, u32[]{:S(2)}) copy-start(bf16[768,384]{1,0:T(8,128)(2,1)} %key_proj_ref.3) | copy-start | bytes 1769476
  16.8 57.4 %copy-start.4 = (bf16[768,384]{1,0:T(8,128)(2,1)S(1)}, bf16[768,384]{1,0:T(8,128)(2,1)}, u32[]{:S(2)}) copy-start(bf16[768,384]{1,0:T(8,128)(2,1)} %value_proj_ref.3) | copy-start | bytes 1769476
  16.8 57.4 %copy-start.7 = (bf16[128,768]{1,0:T(8,128)(2,1)S(1)}, bf16[128,768]{1,0:T(8,128)(2,1)}, u32[]{:S(2)}) copy-start(bf16[128,768]{1,0:T(8,128)(2,1)} %roi_ref.3) | copy-start | bytes 589828
  71.3 1.5 copy-start.23
  72.9 1.3 copy-start.25
  86.9 1.1 copy-start.15
  88.1 25.8 %copy-start.20 = (bf16[1024,128]{1,0:T(8,128)(2,1)}, bf16[1024,128]{1,0:T(8,128)(2,1)S(1)}, u32[]{:S(2)}) copy-start(bf16[1024,128]{1,0:T(8,128)(2,1)S(1)} %get-tuple-element.62.pooled_ref) | copy-start | bytes 786436
  88.1 1.8 copy-start.14
  113.8 0.9 copy-start.21
  146.8 1.1 copy-start.22
  177.9 0.9 copy-start.17
  178.8 0.9 copy-start.18
  179.7 0.9 copy-start.19
  180.6 14.5 %copy-start.28 = (f32[768,384]{1,0:T(8,128)S(1)}, f32[768,384]{1,0:T(8,128)}, u32[]{:S(2)}) copy-start(f32[768,384]{1,0:T(8,128)} %get-tuple-element.79) | copy-start | bytes 3538948
  200.0 293.5 %reduce-scatter.8.cloned.1.call-start = ((), (), s32[]{:S(2)}) async-start(), calls=%async_computation.5 | async-start | bytes 5013504 | tf_op jit(solution)/shard_map/reduce_scatter | solution.py:1696
  200.8 1.5 copy-start.30
  200.8 1.5 copy-start.29
  200.8 1.6 copy-start.6
  200.8 1.6 copy-start.9
  200.8 1.6 copy-start.11
  200.8 1.6 copy-start.13
  200.8 1.6 copy-start.16
  200.8 434.5 %reduce-scatter.6.cloned.1.call-start = ((), (), s32[]{:S(2)}) async-start(), calls=%async_computation.4 | async-start | bytes 5013504 | tf_op jit(solution)/shard_map/reduce_scatter | solution.py:1695
  202.4 1.8 copy-start.24
  204.2 1.5 copy-start.26
  635.3 2.8 copy-start.27
  (2 other events, 1.4 us)
Sparse Core Ops, SparseCore 0:
  200.1 150.4 reduce-scatter.3
  357.2 136.2 reduce-scatter.7
  499.2 136.0 reduce-scatter.5
